TPU v7x, 512 devices: a whole 4x8x8 slice. The times are simulated.
512 devices in a mesh: grp: 16 (over y, core), row: 32 (over x, z).
Axes of the slice: x: 4, y: 8, z: 8, core: 2. Of those that a mesh axis runs over, the one named last changes fastest.
Arguments:
- embeddings: bfloat16 [262144, 1024], P(('grp', 'row')), may hold values from -24 to 24
- rotation: bfloat16 [1024, 1024], replicated, may hold values from -0.1875 to 0.1875
- pq_codes: int32 [262144, 64], P(('grp', 'row')), may hold values from 0 to 255, as said below
- codebook: bfloat16 [64, 16, 256], P('row'), may hold values from -6 to 6
Outputs:
- new_codebook: bfloat16 [64, 16, 256], replicated
- rerotated: bfloat16 [262144, 1024], P(('grp', 'row'))
Inputs may be any that keep to these rules, and one draw needn't show every extreme that they name: pq_codes[t, m] names one of the 256 centroids of subspace m.
All inputs are finite; a program needn't handle non-finite values.
Results may differ from a plain program's by a relative error of at most 0.025.
Values may be sent and summed in bfloat16 or wider, within the bound.
No kernel may reach another device: no remote copies, remote signals or barrier semaphores. Data moves between devices by JAX's collectives and lax.ppermute only.
A program may use at most 64 MiB of HBM per device.

v0:
```python
import jax
import jax.numpy as jnp
from jax import lax
from jax.sharding import PartitionSpec as P

ITERS = 4


epsilon = 1e-06


def one_hot(code_block, centroids):
    levels = lax.broadcasted_iota(jnp.int32, (1, 1, centroids), 2)
    return (code_block[:, :, None] == levels).astype(jnp.bfloat16)


def rebuild(pq_codes, full_book, rotated):
    tokens, subspaces = pq_codes.shape
    sub_width = full_book.shape[1]
    centroids = full_book.shape[2]
    stride = min(subspaces, 16)
    pieces = []
    sum_parts = []
    count_parts = []
    for first_sub in range(0, subspaces, stride):
        last_sub = first_sub + stride
        one_hots = one_hot(pq_codes[:, first_sub:last_sub], centroids)
        picked = jnp.einsum(
            "tmk,mdk->tmd",
            one_hots,
            full_book[first_sub:last_sub],
            preferred_element_type=jnp.float32,
        )
        pieces.append(picked.reshape(tokens, stride * sub_width).astype(jnp.bfloat16))
        sub_view = rotated[:, first_sub * sub_width : last_sub * sub_width].reshape(
            tokens, stride, sub_width
        )
        sum_parts.append(
            jnp.einsum("tmd,tmk->mdk", sub_view, one_hots, preferred_element_type=jnp.float32)
        )
        count_parts.append(jnp.sum(one_hots, axis=0, dtype=jnp.float32))
    rebuilt = jnp.concatenate(pieces, axis=1)
    return (rebuilt, (jnp.concatenate(sum_parts, axis=0), jnp.concatenate(count_parts, axis=0)))


def total_scale(gram_matrix):
    squares = jnp.sum(jnp.square(gram_matrix))
    return jnp.sqrt(lax.psum(squares, "grp")) + epsilon


def advance(polar_iter, gram_matrix, operand, norm_square):
    if norm_square is None:
        weights = gram_matrix.astype(jnp.bfloat16)
        return 1.5 * polar_iter - 0.5 * jnp.dot(
            weights, operand, preferred_element_type=jnp.float32
        )
    inverse = 1.0 / jnp.sqrt(norm_square)
    weights = (gram_matrix / norm_square).astype(jnp.bfloat16)
    return 1.5 * inverse * polar_iter - 0.5 * inverse * jnp.dot(
        weights, operand, preferred_element_type=jnp.float32
    )


def local(embeddings, rotation, pq_codes, codebook):
    full_book = lax.all_gather(codebook, "row", axis=0, tiled=True)
    rotated = jnp.dot(embeddings, rotation, preferred_element_type=jnp.float32).astype(jnp.bfloat16)
    rebuilt, local_tables = rebuild(pq_codes, full_book, rotated)
    own_sums, own_counts = (
        lax.psum_scatter(local_tables[0], "row", scatter_dimension=0, tiled=True),
        lax.psum_scatter(local_tables[1], "row", scatter_dimension=0, tiled=True),
    )
    cross_part = lax.dot_general(
        embeddings, rebuilt, (((0,), (0,)), ((), ())), preferred_element_type=jnp.float32
    )
    group_rows = lax.psum_scatter(
        cross_part.astype(jnp.bfloat16), "grp", scatter_dimension=0, tiled=True
    ).astype(jnp.float32)
    polar_iter = lax.psum(group_rows, "row")
    for turn_index in range(ITERS):
        packed = polar_iter.astype(jnp.bfloat16)
        gathered = lax.all_gather(packed, "grp", axis=0, tiled=True)
        gram_matrix = lax.dot_general(
            packed, gathered, (((1,), (1,)), ((), ())), preferred_element_type=jnp.float32
        )
        norm_square = total_scale(gram_matrix) if turn_index == 0 else None
        polar_iter = advance(polar_iter, gram_matrix, gathered, norm_square)
    rotation_rows = polar_iter.astype(jnp.bfloat16)
    rerotated = jnp.dot(
        embeddings,
        lax.all_gather(rotation_rows, "grp", axis=0, tiled=True),
        preferred_element_type=jnp.float32,
    )
    code_sums, counts = lax.psum((own_sums, own_counts), "grp")
    refreshed = jnp.where(
        counts[:, None, :] > 0,
        code_sums / jnp.maximum(counts, 1.0)[:, None, :],
        codebook.astype(jnp.float32),
    ).astype(jnp.bfloat16)
    new_codebook = lax.all_gather(refreshed, "row", axis=0, tiled=True)
    return (new_codebook, rerotated.astype(jnp.bfloat16))


def solution(mesh):
    placed = (P(("grp", "row"), None), P(), P(("grp", "row"), None), P("row", None, None))
    return jax.shard_map(
        local, mesh=mesh, in_specs=placed, out_specs=(P(), P(("grp", "row"), None)), check_vma=False
    )
```

profile of v0, /device:TPU:1, one launch (start us, length us, event | category | flops | bytes accessed | tf_op | source)
XLA Modules:
  0.0 753.7 jit_solution(12901459038142839629)
XLA Ops:
  8.1 1.0 fusion.44
  9.0 44.3 %all_gather.22 = bf16[64,16,256]{2,1,0:T(8,128)(2,1)S(1)} all-gather(bf16[2,16,256]{2,1,0:T(8,128)(2,1)} %param.7), channel_id=1, replica_groups=mesh['grp'=16,'row'=32] {'row'}, dimensions={0}, use_global_device_ids=true | all-gather | bytes 540672 | tf_op jit(solution)/shard_map/all_gather | solution.py:65
  53.4 2.0 fusion.24
  55.3 2.0 fusion.23
  57.3 2.0 fusion.22
  59.4 2.0 fusion.21
  61.4 2.6 convert_bitcast_fusion
  63.9 3.9 copy.28
  67.9 0.0 all-reduce.5.cloned.1.call-start
  67.9 2.9 convert_reduce_fusion
  70.9 2.9 convert_reduce_fusion.2
  73.8 0.6 pad_maximum_fusion.1
  74.5 62.5 %reduce-scatter.7.cloned.1.call-done = bf16[64,1024]{1,0:T(8,128)(2,1)} async-done(((bf16[1024,1024]{1,0:T(8,128)(2,1)}), bf16[64,1024]{1,0:T(8,128)(2,1)}) %reduce-scatter.7.cloned.1.call-update) | async-done | bytes 131088 | tf_op jit(solution)/shard_map/reduce_scatter | solution.py:75
  137.0 117.6 %all-reduce.6 = f32[64,1024]{1,0:T(8,128)S(1)} all-reduce(bf16[64,1024]{1,0:T(8,128)(2,1)} %reduce-scatter.7.cloned.1.call-done), channel_id=1, replica_groups=mesh['grp'=16,'row'=32] {'row'}, use_global_device_ids=true, to_apply=%region_9.0 | all-reduce | flops 65536 | bytes 393216 | tf_op jit(solution)/shard_map/psum | solution.py:78
  254.6 0.7 convert_element_type.137
  255.3 0.0 reduce-scatter.5.cloned.1.call-start
  255.4 1.3 convolution_convert_fusion.1
  256.6 0.1 fusion.43
  256.7 0.8 copy.25
  257.5 0.1 copy.24
  257.7 0.1 copy.23
  257.8 0.1 copy.22
  258.0 3.2 fusion.1
  261.2 2.7 fusion.4
  263.9 2.7 fusion.7
  266.6 2.7 fusion.10
  269.4 1.0 pad_maximum_fusion
  270.4 0.0 all-gather.8.cloned.1.call-start
  270.5 1.3 dynamic-slice
  272.5 0.7 constant_dynamic-slice_fusion
  273.2 47.4 %all-gather.6.cloned.1.call-done = bf16[1024,1024]{1,0:T(8,128)(2,1)} async-done(((bf16[64,1024]{1,0:T(8,128)(2,1)}), bf16[1024,1024]{1,0:T(8,128)(2,1)}) %all-gather.6.cloned.1.call-update) | async-done | bytes 2097168 | tf_op jit(solution)/shard_map/all_gather | solution.py:81
  320.5 3.0 multiply_reduce_fusion
  323.5 185.1 %reduce-scatter.5.cloned.1.call-done = f32[2,16,256]{2,1,0:T(8,128)} async-done(((f32[64,16,256]{2,1,0:T(8,128)}), f32[2,16,256]{2,1,0:T(8,128)}) %reduce-scatter.5.cloned.1.call-update) | async-done | bytes 32784 | tf_op jit(solution)/shard_map/reduce_scatter | solution.py:69
  508.6 49.2 %all-reduce.1 = (f32[2,16,256]{2,1,0:T(8,128)S(1)}, f32[2,256]{1,0:T(2,128)S(1)}, f32[]{:T(128)}) all-reduce(f32[2,16,256]{2,1,0:T(8,128)} %reduce-scatter.5.cloned.1.call-done, f32[2,256]{1,0:T(2,128)S(1)} %constant_dynamic-slice_fusion, f32[]{:T(128)} %get-tuple-element.19), channel_id=1, replica_groups=mesh['grp'=16,'row'=32] {'grp'}, use_global_device_ids=true, to_apply=%region_7.0 | all-reduce | flops 8705 | bytes 69640 | tf_op jit(solution)/shard_map/psum | solution.py:93
  558.5 2.7 fusion.45
  561.3 0.0 all-gather.10.cloned.1.call-start
  561.3 42.6 %all-gather.8.cloned.1.call-done = bf16[1024,1024]{1,0:T(8,128)(2,1)} async-done(((bf16[64,1024]{1,0:T(8,128)(2,1)}), bf16[1024,1024]{1,0:T(8,128)(2,1)}) %all-gather.8.cloned.1.call-update) | async-done | bytes 2097168 | tf_op jit(solution)/shard_map/all_gather | solution.py:81
  604.0 4.1 fusion.46
  608.0 0.0 all-gather.12.cloned.1.call-start
  608.1 40.9 %all-gather.10.cloned.1.call-done = bf16[1024,1024]{1,0:T(8,128)(2,1)} async-done(((bf16[64,1024]{1,0:T(8,128)(2,1)}), bf16[1024,1024]{1,0:T(8,128)(2,1)}) %all-gather.10.cloned.1.call-update) | async-done | bytes 2097168 | tf_op jit(solution)/shard_map/all_gather | solution.py:81
  649.0 4.0 fusion.47
  653.1 40.9 %all-gather.12.cloned.1.call-done = bf16[1024,1024]{1,0:T(8,128)(2,1)} async-done(((bf16[64,1024]{1,0:T(8,128)(2,1)}), bf16[1024,1024]{1,0:T(8,128)(2,1)}) %all-gather.12.cloned.1.call-update) | async-done | bytes 2097168 | tf_op jit(solution)/shard_map/all_gather | solution.py:81
  694.0 4.1 fusion.29
  698.2 40.4 %all_gather.21 = bf16[64,16,256]{2,1,0:T(8,128)(2,1)S(1)} all-gather(bf16[2,16,256]{2,1,0:T(8,128)(2,1)S(1)} %select_convert_fusion), channel_id=1, replica_groups=mesh['grp'=16,'row'=32] {'row'}, dimensions={0}, use_global_device_ids=true | all-gather | bytes 540672 | tf_op jit(solution)/shard_map/all_gather | solution.py:99
  738.6 0.5 all-gather.14.cloned.1.call-done
  739.1 4.1 fusion.20
  743.2 2.3 copy.27
  745.5 0.8 copy.34
  (23 shorter events, 0.3 us)
Async XLA Ops:
  8.0 247.4 %copy-start = (bf16[1024,1024]{1,0:T(8,128)(2,1)S(1)}, bf16[1024,1024]{1,0:T(8,128)(2,1)}, u32[]{:S(2)}) copy-start(bf16[1024,1024]{1,0:T(8,128)(2,1)} %param.5) | copy-start | bytes 6291460
  8.0 129.0 %reduce-scatter.7.cloned.1.call-start = ((), (), s32[]{:S(2)}) async-start(), calls=%async_computation.8 | async-start | bytes 2228224 | tf_op jit(solution)/shard_map/reduce_scatter | solution.py:75
  59.4 2.0 copy-start.3
  67.9 204.5 %all-reduce.5.cloned.1.call-start = ((), (), s32[]{:S(2)}) async-start(), calls=%async_computation.9 | async-start | bytes 131072
  74.4 246.1 %all-gather.6.cloned.1.call-start = ((), (), s32[]{:S(2)}) async-start(), calls=%async_computation.3 | async-start | bytes 2228224 | tf_op jit(solution)/shard_map/all_gather | solution.py:81
  255.3 253.3 %reduce-scatter.5.cloned.1.call-start = ((), (), s32[]{:S(2)}) async-start(), calls=%async_computation.2 | async-start | bytes 1081344 | tf_op jit(solution)/shard_map/reduce_scatter | solution.py:69
  269.4 51.2 %copy-start.1 = (bf16[64,1024]{1,0:T(8,128)(2,1)S(1)}, bf16[64,1024]{1,0:T(8,128)(2,1)}, u32[]{:S(2)}) copy-start(bf16[64,1024]{1,0:T(8,128)(2,1)} %convert_element_type.137) | copy-start | bytes 393220
  270.4 333.5 %all-gather.8.cloned.1.call-start = ((), (), s32[]{:S(2)}) async-start(), calls=%async_computation.4 | async-start | bytes 2228224 | tf_op jit(solution)/shard_map/all_gather | solution.py:81
  561.3 87.7 %all-gather.10.cloned.1.call-start = ((), (), s32[]{:S(2)}) async-start(), calls=%async_computation.5 | async-start | bytes 2228224 | tf_op jit(solution)/shard_map/all_gather | solution.py:81
  608.0 86.0 %all-gather.12.cloned.1.call-start = ((), (), s32[]{:S(2)}) async-start(), calls=%async_computation.6 | async-start | bytes 2228224 | tf_op jit(solution)/shard_map/all_gather | solution.py:81
  653.1 86.0 %all-gather.14.cloned.1.call-start = ((), (), s32[]{:S(2)}) async-start(), calls=%async_computation.7 | async-start | bytes 2228224 | tf_op jit(solution)/shard_map/all_gather | solution.py:90
  694.0 4.1 copy-start.2
Sparse Core Ops, SparseCore 0:
  68.0 68.9 reduce-scatter.6
  255.4 65.0 all-gather.5
  561.4 42.4 all-gather.7
  608.1 40.7 all-gather.9
  653.2 40.7 all-gather.11
  698.2 40.7 all-gather.13
Sparse Core Ops, SparseCore 1:
  74.5 155.0 all-reduce.4
  270.5 238.0 reduce-scatter.4
where the time goes:
time: 763 us; the launch traced here: 754 us
  waiting for transfers between devices  420 us (55%)
  blocking collectives  252 us (33%)
  matrix products  45.2 us (6%)
  between operations  17.1 us (2%)
  local copies, waits for them, and re-layouts  11.3 us (1%)
  other arithmetic  8.19 us (1%)
    reduce_scatter x1, waiting for transfers between devices, local(): lax.psum_scatter(local_tables[0], 'row', scatter_dimension=0, tiled=True)  185 us
    all_gather x4, waiting for transfers between devices, local(): gathered = lax.all_gather(packed, 'grp', axis=0, tiled=True)  172 us
    psum x1, blocking collectives, local(): polar_iter = lax.psum(group_rows, 'row')  118 us
    reduce_scatter x1, waiting for transfers between devices, local(): lax.psum_scatter(cross_part.astype(jnp.bfloat16), 'grp', scatter_dimensio...  62.5 us
    psum x1, blocking collectives, local(): code_sums, counts = lax.psum((own_sums, own_counts), 'grp')  49.2 us
    all_gather x1, blocking collectives, local(): full_book = lax.all_gather(codebook, 'row', axis=0, tiled=True)  44.3 us
    all_gather x1, blocking collectives, local(): new_codebook = lax.all_gather(refreshed, 'row', axis=0, tiled=True)  40.4 us
  transfers between devices with their start and end apart: 8, of which 7 were waited for; matrix products, arithmetic and copies ran while one was open for 4% of the time, Pallas kernels for 0%

commit v1 on v0

v1 whole, which is shorter than its diff:
```python
import jax
import jax.numpy as jnp
from jax import lax
from jax.sharding import Mesh, PartitionSpec as P

ITERS = 4
EPSILON = 1e-06
F32 = jnp.float32
BF16 = jnp.bfloat16

AXES = ("yh", "yl", "core", "x", "zh", "zl")
ROW = ("x", "zh", "zl")
BOX = ("x", "yl", "zl")
FAR = ("yh", "zh")
LEVEL = 256.0


def gather(value, axes, peers):
    return lax.all_to_all(
        jnp.broadcast_to(value[None], (peers,) + value.shape), axes, 0, 0, tiled=True
    )


def spread(parts, axes):
    return jnp.sum(lax.all_to_all(parts, axes, 0, 0, tiled=True).astype(F32), axis=0)


def one_hot(code_block, centroids):
    levels = lax.broadcasted_iota(jnp.int32, (1, 1, centroids), 2)
    return (code_block[:, :, None] == levels).astype(BF16)


def rebuild(pq_codes, full_book, rotated):
    tokens, subspaces = pq_codes.shape
    sub_width = full_book.shape[1]
    centroids = full_book.shape[2]
    stride = min(subspaces, 16)
    pieces = []
    sum_parts = []
    count_parts = []
    for first_sub in range(0, subspaces, stride):
        last_sub = first_sub + stride
        one_hots = one_hot(pq_codes[:, first_sub:last_sub], centroids)
        picked = jnp.einsum(
            "tmk,mdk->tmd",
            one_hots,
            full_book[first_sub:last_sub],
            preferred_element_type=F32,
        )
        pieces.append(picked.reshape(tokens, stride * sub_width).astype(BF16))
        sub_view = rotated[:, first_sub * sub_width : last_sub * sub_width].reshape(
            tokens, stride, sub_width
        )
        sum_parts.append(
            jnp.einsum("tmd,tmk->mdk", sub_view, one_hots, preferred_element_type=F32)
        )
        count_parts.append(jnp.sum(one_hots, axis=0, dtype=F32))
    rebuilt = jnp.concatenate(pieces, axis=1)
    return rebuilt, jnp.concatenate(sum_parts, axis=0), jnp.concatenate(count_parts, axis=0)


def digits(counts):
    high = jnp.floor(counts * (1.0 / LEVEL))
    return counts - LEVEL * high, high


def count_rows(counts):
    low, high = digits(counts)
    rows = jnp.concatenate([low, high], axis=1).reshape(-1, 4, 128)
    return jnp.pad(rows, ((0, 0), (0, 4), (0, 0))).reshape(-1, 128)


def counts_of(rows):
    both = rows.reshape(-1, 8, 128)[:, :4].reshape(-1, 512)
    return both[:, :256] + LEVEL * both[:, 256:]


def polar_of(cross):
    polar = cross.astype(F32)
    for turn in range(ITERS):
        packed = polar.astype(BF16)
        gram = lax.dot_general(packed, packed, (((1,), (1,)), ((), ())), preferred_element_type=F32)
        scale = 1.0
        if turn == 0:
            norm_square = jnp.sqrt(jnp.sum(jnp.square(gram))) + EPSILON
            scale = 1.0 / jnp.sqrt(norm_square)
            gram = gram / norm_square
        step = jnp.dot(gram.astype(BF16), packed, preferred_element_type=F32)
        polar = (1.5 * scale) * polar - (0.5 * scale) * step
    return polar.astype(BF16)


def local(embeddings, rotation, pq_codes, codebook):
    full_book = gather(codebook, ROW, 32).reshape(64, 16, 256)
    rotated = jnp.dot(embeddings, rotation, preferred_element_type=F32).astype(BF16)
    rebuilt, sums, counts = rebuild(pq_codes, full_book, rotated)
    cross = lax.dot_general(
        embeddings, rebuilt, (((0,), (0,)), ((), ())), preferred_element_type=F32
    ).astype(BF16)
    sums = sums.astype(BF16)
    payload = jnp.concatenate(
        [
            cross[:512],
            cross[512:],
            sums[:, :8].reshape(512, 256),
            sums[:, 8:].reshape(512, 256),
            count_rows(counts).astype(BF16),
        ],
        axis=1,
    )

    def repack(total):
        counted = count_rows(counts_of(total[:, 2560:]))
        return jnp.concatenate([total[:, :2560], counted], axis=1).astype(BF16)

    pair = repack(spread(payload.reshape(2, 256, 2688), "core"))
    boxed = spread(pair.reshape(16, 16, 2688), BOX)
    low, high = digits(counts_of(boxed[:, 2560:]))
    counted = jnp.repeat(jnp.concatenate([low, high], axis=1), 8, axis=0)
    far = jnp.concatenate([boxed[:, :2560], counted], axis=1).astype(BF16)
    total = spread(far.reshape(16, 24, 128), FAR)

    owner = lax.axis_index("core") * 256 + lax.axis_index(BOX) * 16 + lax.axis_index(FAR)
    old = lax.dynamic_slice_in_dim(full_book, owner // 8, 1, 0)[0]
    old = jnp.concatenate(
        [
            lax.dynamic_slice_in_dim(old, owner % 8, 1, 0),
            lax.dynamic_slice_in_dim(old, owner % 8 + 8, 1, 0),
        ],
        axis=0,
    ).astype(F32)
    own_sums = total[16:20].reshape(2, 256)
    own_counts = total[20:22].reshape(1, 256) + LEVEL * total[22:24].reshape(1, 256)
    fresh = jnp.where(own_counts > 0, own_sums / jnp.maximum(own_counts, 1.0), old)
    own = jnp.concatenate([total[:16], fresh.reshape(4, 128)], axis=0).astype(BF16)

    rows = gather(own, FAR, 16).reshape(16, 2560)
    rows = gather(rows, BOX, 16).reshape(256, 2560)
    rows = gather(rows, "core", 2).reshape(512, 2560)
    cross = jnp.concatenate([rows[:, :1024], rows[:, 1024:2048]], axis=0)
    new_codebook = jnp.concatenate(
        [rows[:, 2048:2304].reshape(64, 8, 256), rows[:, 2304:].reshape(64, 8, 256)], axis=1
    )
    rerotated = jnp.dot(embeddings, polar_of(cross), preferred_element_type=F32)
    return (new_codebook, rerotated.astype(BF16))


def solution(mesh):
    split = Mesh(mesh.devices.reshape(4, 2, 2, 4, 4, 2), AXES)
    placed = (P(AXES, None), P(), P(AXES, None), P(ROW, None, None))
    return jax.shard_map(
        local, mesh=split, in_specs=placed, out_specs=(P(), P(AXES, None)), check_vma=False
    )
```

time: 763 us -> 214 us (0.28); the launches traced: 754 us -> 213 us
  waiting for transfers between devices: 420 us -> 29.5 us
  blocking collectives: 252 us -> 49.9 us
  matrix products: 45.2 us -> 75.2 us
  starting transfers between devices: 0.33 us -> 30 us
  between operations: 17.1 us -> 1.98 us
    reduce_scatter x2 -> x0, waiting for transfers between devices: 248 us -> none  [the longest x1 185 us: local(): lax.psum_scatter(local_tables[0], 'row', scatter_dimension=0, tiled=True)]
    all_gather x5 -> x0, waiting for transfers between devices: 172 us -> none  [the longest x4 172 us: local(): gathered = lax.all_gather(packed, 'grp', axis=0, tiled=True)]
    psum x2 -> x0, blocking collectives: 167 us -> none  [the longest x1 118 us: local(): polar_iter = lax.psum(group_rows, 'row')]
    all_gather x2 -> x0, blocking collectives: 84.8 us -> none  [the longest x1 44.3 us: local(): full_book = lax.all_gather(codebook, 'row', axis=0, tiled=True)]
    all_to_all x0 -> x4, blocking collectives: none -> 49.9 us  [the longest x3 43.4 us: gather(): lax.all_to_all(jnp.broadcast_to(value[None], (peers,) + value.shape), axe...]
    dot_general x11, matrix products: 34.7 us -> 65.9 us  [the longest x4 45.8 us: polar_of(): step = jnp.dot(gram.astype(BF16), packed, preferred_element_type=F32)]
    all_to_all x0 -> x3, starting transfers between devices: none -> 30 us  [the longest x2 16.3 us: spread(): lax.all_to_all(parts, axes, 0, 0, tiled=True).astype(F32)]
    all_to_all x0 -> x3, waiting for transfers between devices: none -> 29.5 us  [the longest x2 29.5 us: spread(): lax.all_to_all(parts, axes, 0, 0, tiled=True).astype(F32)]
  transfers between devices with their start and end apart: 8 -> 3, of which waited for: 7 -> 2; matrix products, arithmetic and copies ran while one was open for 4% -> 14% of each run, Pallas kernels for 0% -> 0%
where the time goes in v1:
time: 214 us; the launch traced here: 213 us
  matrix products  75.2 us (35%)
  blocking collectives  49.9 us (23%)
  starting transfers between devices  30 us (14%)
  waiting for transfers between devices  29.5 us (14%)
  local copies, waits for them, and re-layouts  13.3 us (6%)
  other arithmetic  13.3 us (6%)
    dot_general x4, matrix products, polar_of(): step = jnp.dot(gram.astype(BF16), packed, preferred_element_type=F32)  45.8 us
    all_to_all x3, blocking collectives, gather(): lax.all_to_all(jnp.broadcast_to(value[None], (peers,) + value.shape), axe...  43.4 us
    all_to_all x2, waiting for transfers between devices, spread(): lax.all_to_all(parts, axes, 0, 0, tiled=True).astype(F32)  29.5 us
    all_to_all x2, starting transfers between devices, spread(): lax.all_to_all(parts, axes, 0, 0, tiled=True).astype(F32)  16.3 us
    all_to_all x1, starting transfers between devices, gather(): lax.all_to_all(jnp.broadcast_to(value[None], (peers,) + value.shape), axe...  13.7 us
    dot_general x4, matrix products, rebuild(): jnp.einsum('tmd,tmk->mdk', sub_view, one_hots, preferred_element_type=F32)  9.53 us
    reduce_sum x2, other arithmetic, rebuild(): count_parts.append(jnp.sum(one_hots, axis=0, dtype=F32))  9.45 us
    dot_general x4, matrix products, rebuild(): jnp.einsum('tmk,mdk->tmd', one_hots, full_book[first_sub:last_sub], prefe...  8.05 us
  transfers between devices with their start and end apart: 3, of which 2 were waited for; matrix products, arithmetic and copies ran while one was open for 14% of the time, Pallas kernels for 0%

profile of v1, /device:TPU:1, one launch (start us, length us, event | category | flops | bytes accessed | tf_op | source)
XLA Modules:
  0.0 213.1 jit_solution(4358668293005420886)
XLA Ops:
  0.6 1.7 broadcast_in_dim.24
  2.4 13.7 %all-to-all-start = ((bf16[32,2,16,256]{3,2,1,0:T(8,128)(2,1)}), bf16[32,2,16,256]{3,2,1,0:T(8,128)(2,1)S(1)}, u32[]{:S(2)}, u32[]{:S(2)}) async-start(bf16[32,2,16,256]{3,2,1,0:T(8,128)(2,1)} %broadcast_in_dim.24), calls=%async_computation | async-start | bytes 1048576 | tf_op jit(solution)/shard_map/all_to_all | solution.py:19
  16.1 1.5 fusion.77
  17.6 2.5 %convolution_convert_fusion.1 = bf16[512,1024]{1,0:T(8,128)(2,1)S(1)} fusion(bf16[512,1024]{1,0:T(8,128)(2,1)} %param.4, bf16[1024,1024]{1,0:T(8,128)(2,1)S(1)} %copy-done), kind=kOutput, calls=%fused_computation.49 | convolution fusion | flops 1074266112 | bytes 4194304 | tf_op jit(solution)/shard_map/dot_general | solution.py:95
  20.0 0.8 fusion.74
  20.8 1.8 copy.29
  22.6 0.8 copy.28
  23.4 0.8 copy.27
  24.3 0.8 copy.26
  25.1 4.7 %convert_reduce_fusion.2 = (f32[16,256]{1,0:T(8,128)S(1)}, f32[16,256]{1,0:T(8,128)S(1)}) fusion(s32[512,16]{0,1:T(8,128)} %get-tuple-element.31, s32[512,16]{0,1:T(8,128)} %get-tuple-element.30), kind=kLoop, calls=%fused_computation.2 | loop fusion | flops 16769024 | bytes 98304 | tf_op jit(solution)/shard_map/reduce_sum | solution.py:57
  29.9 2.5 %fusion.43 = bf16[16,16,256]{2,1,0:T(8,128)(2,1)S(1)} fusion(bf16[512,16,16]{0,2,1:T(8,128)(2,1)} %bitcast.120, s32[512,16]{0,1:T(8,128)} %get-tuple-element.32), kind=kOutput, calls=%fused_computation.59 | convolution fusion | flops 69271552 | bytes 425984 | tf_op jit(solution)/shard_map/tmd,tmk->mdk/dot_general | solution.py:55
  32.4 4.7 %convert_reduce_fusion = (f32[16,256]{1,0:T(8,128)S(1)}, f32[16,256]{1,0:T(8,128)S(1)}) fusion(s32[512,16]{0,1:T(8,128)} %get-tuple-element.32, s32[512,16]{0,1:T(8,128)} %get-tuple-element.33), kind=kLoop, calls=%fused_computation | loop fusion | flops 16769024 | bytes 98304 | tf_op jit(solution)/shard_map/reduce_sum | solution.py:57
  37.4 3.0 %fusion.42 = bf16[16,16,256]{2,1,0:T(8,128)(2,1)S(1)} fusion(bf16[512,16,16]{0,2,1:T(8,128)(2,1)S(1)} %bitcast.117, s32[512,16]{0,1:T(8,128)} %get-tuple-element.33), kind=kOutput, calls=%fused_computation.58 | convolution fusion | flops 69271552 | bytes 425984 | tf_op jit(solution)/shard_map/tmd,tmk->mdk/dot_general | solution.py:55
  40.4 2.0 fusion.41
  42.4 2.0 fusion.40
  44.6 2.0 fusion.39
  46.6 2.0 fusion.38
  48.7 2.0 fusion.37
  50.7 2.0 fusion.36
  52.7 1.3 convert_bitcast_fusion
  54.1 0.2 fusion.73
  54.3 0.1 constant_dynamic-update-slice_fusion.4
  54.5 6.5 %all_to_all.35 = bf16[2,256,2688]{2,1,0:T(8,128)(2,1)S(1)} all-to-all(bf16[2,256,2688]{2,1,0:T(8,128)(2,1)S(1)} %bitcast_dynamic-update-slice_fusion.2), channel_id=1, replica_groups=mesh['yh'=4,'yl'=2,'core'=2,'x'=4,'zh'=4,'zl'=2] {'core'}, dimensions={0} | all-to-all | bytes 5505024 | tf_op jit(solution)/shard_map/all_to_all | solution.py:25
  61.0 0.4 convert_reduce_fusion.4
  61.5 0.1 slice.234
  61.7 1.2 pad_maximum_fusion.1
  62.9 6.3 %all-to-all-start.2 = ((bf16[16,16,2688]{2,1,0:T(8,128)(2,1)}), bf16[16,16,2688]{2,1,0:T(8,128)(2,1)S(1)}, u32[]{:S(2)}, u32[]{:S(2)}) async-start(bf16[16,16,2688]{2,1,0:T(8,128)(2,1)} %pad_maximum_fusion.1), calls=%async_computation.2 | async-start | bytes 2752512 | tf_op jit(solution)/shard_map/all_to_all | solution.py:25
  69.3 18.8 %all-to-all-done.2 = bf16[16,16,2688]{2,1,0:T(8,128)(2,1)S(1)} async-done(((bf16[16,16,2688]{2,1,0:T(8,128)(2,1)}), bf16[16,16,2688]{2,1,0:T(8,128)(2,1)S(1)}, u32[]{:S(2)}, u32[]{:S(2)}) %all-to-all-start.2) | async-done | bytes 1376288 | tf_op jit(solution)/shard_map/all_to_all | solution.py:25
  88.1 0.2 convert_reduce_fusion.5
  88.4 0.7 copy.43
  89.1 10.0 %all-to-all-start.3 = ((bf16[16,24,128]{2,1,0:T(8,128)(2,1)}), bf16[16,24,128]{2,1,0:T(8,128)(2,1)S(1)}, u32[]{:S(2)}, u32[]{:S(2)}) async-start(bf16[16,24,128]{2,1,0:T(8,128)(2,1)} %bitcast.53), calls=%async_computation.3 | async-start | bytes 196608 | tf_op jit(solution)/shard_map/all_to_all | solution.py:25
  99.0 0.7 dynamic-slice_bitcast_fusion.1
  99.8 10.7 %all-to-all-done.3 = bf16[16,24,128]{2,1,0:T(8,128)(2,1)S(1)} async-done(((bf16[16,24,128]{2,1,0:T(8,128)(2,1)}), bf16[16,24,128]{2,1,0:T(8,128)(2,1)S(1)}, u32[]{:S(2)}, u32[]{:S(2)}) %all-to-all-start.3) | async-done | bytes 98336 | tf_op jit(solution)/shard_map/all_to_all | solution.py:25
  110.6 14.1 %all_to_all.36 = bf16[16,20,128]{2,1,0:T(8,128)(2,1)S(1)} all-to-all(bf16[16,20,128]{2,1,0:T(8,128)(2,1)S(1)} %broadcast_in_dim.47), channel_id=1, replica_groups=mesh['yh'=4,'yl'=2,'core'=2,'x'=4,'zh'=4,'zl'=2] {'yh','zh'}, dimensions={0} | all-to-all | bytes 163840 | tf_op jit(solution)/shard_map/all_to_all | solution.py:19
  124.8 0.1 broadcast_in_dim.49
  124.9 17.9 %all_to_all.37 = bf16[16,16,2560]{2,1,0:T(8,128)(2,1)S(1)} all-to-all(bf16[16,16,2560]{2,1,0:T(8,128)(2,1)S(1)} %broadcast_in_dim.49), channel_id=1, replica_groups=mesh['yh'=4,'yl'=2,'core'=2,'x'=4,'zh'=4,'zl'=2] {'x','yl','zl'}, dimensions={0} | all-to-all | bytes 2621440 | tf_op jit(solution)/shard_map/all_to_all | solution.py:19
  142.8 0.2 broadcast_in_dim.51
  143.0 11.4 %all_to_all.38 = bf16[2,256,2560]{2,1,0:T(8,128)(2,1)S(1)} all-to-all(bf16[2,256,2560]{2,1,0:T(8,128)(2,1)S(1)} %broadcast_in_dim.51), channel_id=1, replica_groups=mesh['yh'=4,'yl'=2,'core'=2,'x'=4,'zh'=4,'zl'=2] {'core'}, dimensions={0} | all-to-all | bytes 5242880 | tf_op jit(solution)/shard_map/all_to_all | solution.py:19
  154.3 0.8 slice_bitcast_fusion.1
  155.1 0.3 fusion.72
  155.4 4.9 %multiply_reduce_fusion = (f32[]{:T(128)}, f32[1024,1024]{1,0:T(8,128)}) fusion(bf16[512,1024]{1,0:T(8,128)(2,1)S(1)} %get-tuple-element.13, bf16[512,1024]{1,0:T(8,128)(2,1)S(1)} %get-tuple-element.12), kind=kOutput, calls=%fused_computation.26 | convolution fusion | flops 2153775104 | bytes 6291460 | tf_op jit(solution)/shard_map/dot_general | solution.py:82
  161.1 6.8 %fusion.21 = f32[1024,1024]{1,0:T(8,128)} fusion(f32[1024,1024]{1,0:T(8,128)} %get-tuple-element.41, f32[]{:T(128)S(6)} %add.78, bf16[512,1024]{1,0:T(8,128)(2,1)} %copy-done.2, bf16[512,1024]{1,0:T(8,128)(2,1)S(1)} %get-tuple-element.12), kind=kOutput, calls=%fused_computation.38 | convolution fusion | flops 2153775104 | bytes 10485764 | tf_op jit(solution)/shard_map/dot_general | solution.py:88
  167.9 14.2 %multiply_subtract_fusion.1 = f32[1024,1024]{1,0:T(8,128)} fusion(f32[1024,1024]{1,0:T(8,128)} %fusion.21, f32[]{:T(128)S(6)} %mul.126, f32[]{:T(128)S(6)} %mul.123, bf16[512,1024]{1,0:T(8,128)(2,1)} %copy-done.2, bf16[512,1024]{1,0:T(8,128)(2,1)S(1)} %get-tuple-element.12), kind=kOutput, calls=%fused_computation.23 | convolution fusion | flops 4323278848 | bytes 10485768 | tf_op jit(solution)/shard_map/dot_general | solution.py:88
  182.1 12.7 %multiply_subtract_fusion = f32[1024,1024]{1,0:T(8,128)} fusion(f32[1024,1024]{1,0:T(8,128)} %multiply_subtract_fusion.1), kind=kOutput, calls=%fused_computation.22 | convolution fusion | flops 4301258752 | bytes 8388608 | tf_op jit(solution)/shard_map/dot_general | solution.py:88
  194.8 12.1 %subtract_convert_fusion = bf16[1024,1024]{1,0:T(8,128)(2,1)} fusion(f32[1024,1024]{1,0:T(8,128)} %multiply_subtract_fusion), kind=kOutput, calls=%fused_computation.21 | convolution fusion | flops 4302307328 | bytes 6291456 | tf_op jit(solution)/shard_map/dot_general | solution.py:88
  206.9 3.1 %fusion.35 = bf16[512,1024]{0,1:T(8,128)(2,1)S(1)} fusion(bf16[1024,1024]{1,0:T(8,128)(2,1)} %subtract_convert_fusion, bf16[512,1024]{1,0:T(8,128)(2,1)} %param.4), kind=kOutput, calls=%fused_computation.51 | convolution fusion | flops 1074266112 | bytes 4194304 | tf_op jit(solution)/shard_map/dot_general | solution.py:144
  210.1 1.3 copy.35
  211.4 1.8 pad_maximum_fusion.7
  (70 shorter events, 0.8 us)
Async XLA Ops:
  0.6 16.9 %copy-start = (bf16[1024,1024]{1,0:T(8,128)(2,1)S(1)}, bf16[1024,1024]{1,0:T(8,128)(2,1)}, u32[]{:S(2)}) copy-start(bf16[1024,1024]{1,0:T(8,128)(2,1)} %param.5) | copy-start | bytes 6291460
  2.4 42.2 %all-to-all-start = ((bf16[32,2,16,256]{3,2,1,0:T(8,128)(2,1)}), bf16[32,2,16,256]{3,2,1,0:T(8,128)(2,1)S(1)}, u32[]{:S(2)}, u32[]{:S(2)}) async-start(bf16[32,2,16,256]{3,2,1,0:T(8,128)(2,1)} %broadcast_in_dim.24), calls=%async_computation | async-start | bytes 1048576 | tf_op jit(solution)/shard_map/all_to_all | solution.py:19
  23.4 13.9 %copy-start.3 = (bf16[512,256]{0,1:T(8,128)(2,1)S(1)}, bf16[512,256]{0,1:T(8,128)(2,1)}, u32[]{:S(2)}) copy-start(bf16[512,256]{0,1:T(8,128)(2,1)} %copy.28) | copy-start | bytes 786436
  29.9 10.5 %copy-start.4 = (bf16[512,256]{0,1:T(8,128)(2,1)S(1)}, bf16[512,256]{0,1:T(8,128)(2,1)}, u32[]{:S(2)}) copy-start(bf16[512,256]{0,1:T(8,128)(2,1)} %copy.27) | copy-start | bytes 786436
  29.9 10.5 %copy-start.8 = (s32[512,16]{0,1:T(8,128)S(1)}, s32[512,16]{0,1:T(8,128)}, u32[]{:S(2)}) copy-start(s32[512,16]{0,1:T(8,128)} %get-tuple-element.31) | copy-start | bytes 98308
  37.3 5.1 %copy-start.5 = (bf16[512,256]{0,1:T(8,128)(2,1)S(1)}, bf16[512,256]{0,1:T(8,128)(2,1)}, u32[]{:S(2)}) copy-start(bf16[512,256]{0,1:T(8,128)(2,1)} %copy.26) | copy-start | bytes 786436
  37.3 5.1 %copy-start.6 = (s32[512,16]{0,1:T(8,128)S(1)}, s32[512,16]{0,1:T(8,128)}, u32[]{:S(2)}) copy-start(s32[512,16]{0,1:T(8,128)} %get-tuple-element.30) | copy-start | bytes 98308
  42.4 2.2 %copy-start.11 = (s32[512,16]{0,1:T(8,128)S(1)}, s32[512,16]{0,1:T(8,128)}, u32[]{:S(2)}) copy-start(s32[512,16]{0,1:T(8,128)} %get-tuple-element.32) | copy-start | bytes 98308
  44.5 2.1 copy-start.10
  44.5 4.1 %copy-start.1 = (bf16[32,2,16,256]{3,2,1,0:T(8,128)(2,1)}, bf16[32,2,16,256]{3,2,1,0:T(8,128)(2,1)S(1)}, u32[]{:S(2)}) copy-start(bf16[32,2,16,256]{3,2,1,0:T(8,128)(2,1)S(1)} %all-to-all-done) | copy-start | bytes 1572868
  46.6 2.0 copy-start.9
  48.7 2.0 copy-start.7
  50.7 2.0 copy-start.12
  62.9 25.2 %all-to-all-start.2 = ((bf16[16,16,2688]{2,1,0:T(8,128)(2,1)}), bf16[16,16,2688]{2,1,0:T(8,128)(2,1)S(1)}, u32[]{:S(2)}, u32[]{:S(2)}) async-start(bf16[16,16,2688]{2,1,0:T(8,128)(2,1)} %pad_maximum_fusion.1), calls=%async_computation.2 | async-start | bytes 2752512 | tf_op jit(solution)/shard_map/all_to_all | solution.py:25
  89.1 21.4 %all-to-all-start.3 = ((bf16[16,24,128]{2,1,0:T(8,128)(2,1)}), bf16[16,24,128]{2,1,0:T(8,128)(2,1)S(1)}, u32[]{:S(2)}, u32[]{:S(2)}) async-start(bf16[16,24,128]{2,1,0:T(8,128)(2,1)} %bitcast.53), calls=%async_computation.3 | async-start | bytes 196608 | tf_op jit(solution)/shard_map/all_to_all | solution.py:25
  155.4 5.0 %copy-start.2 = (bf16[512,1024]{1,0:T(8,128)(2,1)}, bf16[512,1024]{1,0:T(8,128)(2,1)S(1)}, u32[]{:S(2)}) copy-start(bf16[512,1024]{1,0:T(8,128)(2,1)S(1)} %get-tuple-element.13) | copy-start | bytes 3145732

commit v2 on v1

v2 whole, which is shorter than its diff:
```python
import functools

import jax
import jax.numpy as jnp
from jax import lax
from jax.experimental import pallas as pl
from jax.experimental.pallas import tpu as pltpu
from jax.sharding import Mesh, PartitionSpec as P

ITERS = 4
EPSILON = 1e-06
F32 = jnp.float32
BF16 = jnp.bfloat16

AXES = ("yh", "yl", "core", "x", "zh", "zl")
ROW = ("x", "zh", "zl")
BOX = ("x", "yl", "zl")
FAR = ("yh", "zh")

D = 1024
SUBS = 64
HALF = SUBS // 2
DS = 16
K = 256
TOK = 512
LOW = 64.0
WIDE = 2 * D + 2 * K + 128
BACK = 2 * D + 2 * K

NN = (((1,), (0,)), ((), ()))
NT = (((1,), (1,)), ((), ()))
PARAMS = pltpu.CompilerParams(vmem_limit_bytes=56 * 1024 * 1024)


def dot(a, b, dims=NN):
    return lax.dot_general(a, b, dims, preferred_element_type=F32)


def whole():
    return pl.BlockSpec(memory_space=pltpu.VMEM)


def gather(value, axes, peers):
    return lax.all_to_all(
        jnp.broadcast_to(value[None], (peers,) + value.shape), axes, 0, 0, tiled=True
    )


def spread(parts, axes):
    return jnp.sum(lax.all_to_all(parts, axes, 0, 0, tiled=True).astype(F32), axis=0)


def picks(codes_ref, sub):
    row = codes_ref[pl.ds(sub, 1), :]
    levels = lax.broadcasted_iota(jnp.int32, (K, TOK), 0)
    return jnp.where(levels == row, 1.0, 0.0).astype(BF16)


def tables_kernel(emb_ref, rot_ref, codes_ref, out_ref, turned_ref):
    def turn(tile, carry):
        rows = pl.ds(pl.multiple_of(tile * 128, 128), 128)
        rotated = dot(emb_ref[rows, :], rot_ref[...])
        turned_ref[:, rows] = rotated.T.astype(BF16)
        return carry

    lax.fori_loop(0, TOK // 128, turn, 0)
    ones = jnp.ones((DS, TOK), BF16)
    line = lax.broadcasted_iota(jnp.int32, (DS, 128), 0)

    def one(sub):
        at = pl.ds(pl.multiple_of(sub * DS, DS), DS)
        left = jnp.concatenate([turned_ref[at, :], ones], axis=0)
        both = dot(left, picks(codes_ref, sub), NT)
        counts = both[DS:]
        high = jnp.floor(counts * (1.0 / LOW))
        return both[:DS], counts - LOW * high, high

    def step(pair, carry):
        at = pl.ds(pl.multiple_of(pair * DS, DS), DS)
        digits = jnp.zeros((DS, 128), F32)
        for half in range(2):
            sums, low, high = one(pair + HALF * half)
            out_ref[at, K * half : K * half + K] = sums.astype(BF16)
            for place, part in enumerate((low[:, :128], low[:, 128:], high[:, :128], high[:, 128:])):
                digits = jnp.where(line == 4 * half + place, part, digits)
        out_ref[at, 2 * K :] = digits.astype(BF16)
        return carry

    lax.fori_loop(0, HALF, step, 0, unroll=4)


def tables(embeddings, rotation, codes):
    return pl.pallas_call(
        tables_kernel,
        out_shape=jax.ShapeDtypeStruct((TOK, 2 * K + 128), BF16),
        in_specs=[whole()] * 3,
        out_specs=whole(),
        scratch_shapes=[pltpu.VMEM((D, TOK), BF16)],
        compiler_params=PARAMS,
        cost_estimate=pl.CostEstimate(flops=8 * 10**9, bytes_accessed=4 * 10**6, transcendentals=0),
        name="tables",
    )(embeddings, rotation, codes)


def cross_kernel(emb_ref, codes_ref, book_ref, table_ref, out_ref, rebuilt_ref):
    def step(sub, carry):
        at = pl.ds(pl.multiple_of(sub * DS, DS), DS)
        rebuilt_ref[at, :] = dot(book_ref[at, :], picks(codes_ref, sub)).astype(BF16)
        return carry

    lax.fori_loop(0, SUBS, step, 0, unroll=8)
    out_ref[:, 2 * D :] = table_ref[...]
    for side in range(2):

        def tile(i, carry):
            here = pl.multiple_of(i * 128, 128)
            part = dot(rebuilt_ref[pl.ds(side * TOK + here, 128), :], emb_ref[...])
            out_ref[pl.ds(here, 128), side * D : side * D + D] = part.astype(BF16)
            return carry

        lax.fori_loop(0, TOK // 128, tile, 0)


def crosses(embeddings, codes, book, table):
    return pl.pallas_call(
        cross_kernel,
        out_shape=jax.ShapeDtypeStruct((TOK, WIDE), BF16),
        in_specs=[whole()] * 4,
        out_specs=whole(),
        scratch_shapes=[pltpu.VMEM((D, TOK), BF16)],
        compiler_params=PARAMS,
        cost_estimate=pl.CostEstimate(flops=8 * 10**9, bytes_accessed=6 * 10**6, transcendentals=0),
        name="crosses",
    )(embeddings, codes, book, table)


TILE = 256


def polar_kernel(rows_ref, emb_ref, out_ref, book_ref, a_ref, b_ref, gram_ref, full_ref, polar_ref):
    book_ref[:TOK, :] = rows_ref[:, 2 * D : 2 * D + K]
    book_ref[TOK:, :] = rows_ref[:, 2 * D + K : 2 * D + 2 * K]
    a_ref[:TOK, :] = rows_ref[:, :D]
    a_ref[TOK:, :] = rows_ref[:, D : 2 * D]

    def tiles(body, init):
        def run(i, carry):
            return body(pl.ds(pl.multiple_of(i * TILE, TILE), TILE), carry)

        return lax.fori_loop(0, D // TILE, run, init)

    def first_gram(at, total):
        part = dot(a_ref[at, :], a_ref[...], NT)
        full_ref[at, :] = part
        return total + jnp.sum((part * part).reshape(TILE // 8, 8, D), axis=0)

    squares = tiles(first_gram, jnp.zeros((8, D), F32))
    norm_square = jnp.sqrt(jnp.sum(squares, keepdims=True)) + EPSILON
    scale = lax.rsqrt(norm_square)

    def first_step(at, carry):
        weights = (full_ref[at, :] / norm_square).astype(BF16)
        part = (1.5 * scale) * a_ref[at, :].astype(F32) - (0.5 * scale) * dot(weights, a_ref[...])
        polar_ref[at, :] = part
        b_ref[at, :] = part.astype(BF16)
        return carry

    tiles(first_step, 0)
    now, later = b_ref, a_ref
    for turn in range(1, ITERS):

        def advance(at, carry, now=now, later=later, turn=turn):
            gram = dot(now[at, :], now[...], NT).astype(BF16)
            part = 1.5 * polar_ref[at, :] - 0.5 * dot(gram, now[...])
            if turn < ITERS - 1:
                polar_ref[at, :] = part
            later[at, :] = part.astype(BF16)
            return carry

        tiles(advance, 0)
        now, later = later, now

    def rotate(i, carry):
        at = pl.ds(pl.multiple_of(i * TILE, TILE), TILE)
        out_ref[at, :] = dot(emb_ref[at, :], now[...], NT).astype(BF16)
        return carry

    lax.fori_loop(0, TOK // TILE, rotate, 0)


def finish(rows, embeddings):
    return pl.pallas_call(
        polar_kernel,
        out_shape=(
            jax.ShapeDtypeStruct((TOK, D), BF16),
            jax.ShapeDtypeStruct((SUBS * DS, K), BF16),
        ),
        in_specs=[whole()] * 2,
        out_specs=(whole(),) * 2,
        scratch_shapes=[
            pltpu.VMEM((D, D), BF16),
            pltpu.VMEM((D, D), BF16),
            pltpu.VMEM((8, 128), BF16),
            pltpu.VMEM((D, D), F32),
            pltpu.VMEM((D, D), F32),
        ],
        compiler_params=PARAMS,
        cost_estimate=pl.CostEstimate(flops=20 * 10**9, bytes_accessed=8 * 10**6, transcendentals=0),
        name="polar",
    )(rows, embeddings)


def local(embeddings, rotation, pq_codes, codebook):
    codes = pq_codes.T
    full_book = gather(codebook, ROW, 32).reshape(SUBS * DS, K)
    table = tables(embeddings, rotation, codes)
    payload = crosses(embeddings, codes, full_book, table)

    pair = spread(payload.reshape(2, 256, WIDE), "core").astype(BF16)
    boxed = spread(pair.reshape(16, 16, WIDE), BOX)
    counted = boxed[:8, BACK:].reshape(2, 2, 256)
    counted = counted[:, 0] + LOW * counted[:, 1]
    high = jnp.floor(counted * (1.0 / 256.0))
    digits = jnp.concatenate([counted - 256.0 * high, high], axis=0).reshape(1, 8, 128)
    far = jnp.concatenate(
        [
            boxed[:, :BACK].reshape(16, 20, 128),
            jnp.broadcast_to(digits, (16, 8, 128)),
            jnp.zeros((16, 4, 128), F32),
        ],
        axis=1,
    ).astype(BF16)
    total = spread(far, FAR)

    owner = lax.axis_index("core") * 256 + lax.axis_index(BOX) * 16 + lax.axis_index(FAR)
    old = jnp.concatenate(
        [lax.dynamic_slice_in_dim(full_book, owner + TOK * half, 1, 0) for half in range(2)], axis=0
    ).astype(F32)
    own_sums = total[16:20].reshape(2, K)
    own_counts = total[20:24].reshape(2, K) + 256.0 * total[24:28].reshape(2, K)
    fresh = jnp.where(own_counts > 0, own_sums / jnp.maximum(own_counts, 1.0), old)
    own = jnp.concatenate([total[:16], fresh.reshape(4, 128)], axis=0).astype(BF16)

    rows = gather(own, FAR, 16).reshape(16, BACK)
    rows = gather(rows, BOX, 16).reshape(256, BACK)
    rows = gather(rows, "core", 2).reshape(512, BACK)
    rerotated, new_codebook = finish(rows, embeddings)
    return (new_codebook.reshape(SUBS, DS, K), rerotated)


def solution(mesh):
    split = Mesh(mesh.devices.reshape(4, 2, 2, 4, 4, 2), AXES)
    placed = (P(AXES, None), P(), P(AXES, None), P(ROW, None, None))
    return jax.shard_map(
        local, mesh=split, in_specs=placed, out_specs=(P(), P(AXES, None)), check_vma=False
    )
```

time: 214 us -> 169 us (0.79)
  matrix products: 75.2 us -> 0 us
  Pallas kernels: 0 us -> 46 us
  other arithmetic: 13.3 us -> 2.93 us
  local copies, waits for them, and re-layouts: 13.3 us -> 3.6 us
  blocking collectives: 49.9 us -> 55.1 us
  waiting for transfers between devices: 29.5 us -> 33.1 us
  starting transfers between devices: 30 us -> 27.1 us
    dot_general x16 -> x0, matrix products: 75.2 us -> none  [the longest x4 45.8 us: polar_of(): step = jnp.dot(gram.astype(BF16), packed, preferred_element_type=F32)]
    pallas_call x0 -> x3, Pallas kernels: none -> 46 us  [the longest x1 26.4 us: finish(): pl.pallas_call(polar_kernel, out_shape=(jax.ShapeDtypeStruct((TOK, D), BF...]
    reduce_sum x2 -> x0, other arithmetic: 9.45 us -> none  [rebuild(): count_parts.append(jnp.sum(one_hots, axis=0, dtype=F32))]
    slice x13 -> x2, local copies, waits for them, and re-layouts: 7.27 us -> 0.01 us  [the longest x1 0.01 us: local(): boxed[:, :BACK].reshape(16, 20, 128)]
    all_to_all x1, blocking collectives: 6.53 us -> 10.3 us  [spread(): lax.all_to_all(parts, axes, 0, 0, tiled=True).astype(F32)]
    all_to_all x1, waiting for transfers between devices: 0.01 us -> 3.6 us  [gather(): lax.all_to_all(jnp.broadcast_to(value[None], (peers,) + value.shape), axe...]
    all_to_all x2, starting transfers between devices: 16.3 us -> 13.4 us  [spread(): lax.all_to_all(parts, axes, 0, 0, tiled=True).astype(F32)]
    concatenate x5 -> x1, other arithmetic: 3.06 us -> 0.75 us  [local(): jnp.concatenate([boxed[:, :BACK].reshape(16, 20, 128), jnp.broadcast_to(d...]
  transfers between devices with their start and end apart: 3 -> 3, of which waited for: 2 -> 3; matrix products, arithmetic and copies ran while one was open for 14% -> 0% of each run, Pallas kernels for 0% -> 6%
where the time goes in v2:
time: 169 us
  blocking collectives  55.1 us (33%)
  Pallas kernels  46 us (27%)
  waiting for transfers between devices  33.1 us (20%)
  starting transfers between devices  27.1 us (16%)
  local copies, waits for them, and re-layouts  3.6 us (2%)
  other arithmetic  2.93 us (2%)
    all_to_all x3, blocking collectives, gather(): lax.all_to_all(jnp.broadcast_to(value[None], (peers,) + value.shape), axe...  44.8 us
    all_to_all x2, waiting for transfers between devices, spread(): lax.all_to_all(parts, axes, 0, 0, tiled=True).astype(F32)  29.5 us
    pallas_call x1, Pallas kernels, finish(): pl.pallas_call(polar_kernel, out_shape=(jax.ShapeDtypeStruct((TOK, D), BF...  26.4 us
    all_to_all x1, starting transfers between devices, gather(): lax.all_to_all(jnp.broadcast_to(value[None], (peers,) + value.shape), axe...  13.7 us
    all_to_all x2, starting transfers between devices, spread(): lax.all_to_all(parts, axes, 0, 0, tiled=True).astype(F32)  13.4 us
    pallas_call x1, Pallas kernels, tables(): pl.pallas_call(tables_kernel, out_shape=jax.ShapeDtypeStruct((TOK, 2 * K...  10.7 us
    all_to_all x1, blocking collectives, spread(): lax.all_to_all(parts, axes, 0, 0, tiled=True).astype(F32)  10.3 us
    pallas_call x1, Pallas kernels, crosses(): pl.pallas_call(cross_kernel, out_shape=jax.ShapeDtypeStruct((TOK, WIDE),...  8.88 us
  transfers between devices with their start and end apart: 3, of which 3 were waited for; matrix products, arithmetic and copies ran while one was open for 0% of the time, Pallas kernels for 6%

profile of v2, /device:TPU:1, one launch (start us, length us, event | category | flops | bytes accessed | tf_op | source)
XLA Modules:
  0.0 168.6 jit_solution(11786031647547584093)
XLA Ops:
  0.6 1.6 broadcast_in_dim.36
  2.2 13.7 %all-to-all-start = ((bf16[32,2,16,256]{3,2,1,0:T(8,128)(2,1)}), bf16[32,2,16,256]{3,2,1,0:T(8,128)(2,1)S(1)}, u32[]{:S(2)}, u32[]{:S(2)}) async-start(bf16[32,2,16,256]{3,2,1,0:T(8,128)(2,1)} %broadcast_in_dim.36), calls=%async_computation | async-start | bytes 1048576 | tf_op jit(solution)/shard_map/all_to_all | solution.py:44
  15.9 10.7 %tables.1.table_ref = bf16[512,640]{1,0:T(8,128)(2,1)} custom-call(bf16[512,1024]{1,0:T(8,128)(2,1)} %emb_ref.5, bf16[1024,1024]{1,0:T(8,128)(2,1)} %rot_ref.1, s32[64,512]{1,0:T(8,128)} %bitcast.26), custom_call_target="tpu_custom_call" | custom-call | flops 8000000000 | bytes 4000000 | tf_op jit(solution)/shard_map/tables/pallas_call | solution.py:93
  26.6 3.6 %all-to-all-done = bf16[32,2,16,256]{3,2,1,0:T(8,128)(2,1)S(1)} async-done(((bf16[32,2,16,256]{3,2,1,0:T(8,128)(2,1)}), bf16[32,2,16,256]{3,2,1,0:T(8,128)(2,1)S(1)}, u32[]{:S(2)}, u32[]{:S(2)}) %all-to-all-start) | async-done | bytes 524320 | tf_op jit(solution)/shard_map/all_to_all | solution.py:44
  30.2 0.0 copy-start
  30.2 0.8 copy-done
  31.0 8.9 %crosses.1 = bf16[512,2688]{1,0:T(8,128)(2,1)} custom-call(bf16[512,1024]{1,0:T(8,128)(2,1)} %emb_ref.5, s32[64,512]{1,0:T(8,128)} %bitcast.27, bf16[1024,256]{1,0:T(8,128)(2,1)} %bitcast.22, bf16[512,640]{1,0:T(8,128)(2,1)} %tables.1.table_ref), custom_call_target="tpu_custom_call" | custom-call | flops 8000000000 | bytes 6000000 | tf_op jit(solution)/shard_map/crosses/pallas_call | solution.py:125
  39.9 10.3 %all_to_all.35 = bf16[2,256,2688]{2,1,0:T(8,128)(2,1)S(1)} all-to-all(bf16[2,256,2688]{2,1,0:T(8,128)(2,1)} %bitcast.20), channel_id=1, replica_groups=mesh['yh'=4,'yl'=2,'core'=2,'x'=4,'zh'=4,'zl'=2] {'core'}, dimensions={0} | all-to-all | bytes 5505024 | tf_op jit(solution)/shard_map/all_to_all | solution.py:50
  50.2 1.9 %reduce_sum.30 = bf16[256,2688]{1,0:T(8,128)(2,1)} reduce(bf16[2,256,2688]{2,1,0:T(8,128)(2,1)S(1)} %all_to_all.35, bf16[]{:T(256)} %constant.19.clone.1), dimensions={0}, to_apply=%region_0.0 | reduce | flops 688128 | bytes 4128770 | tf_op jit(solution)/shard_map/reduce_sum | solution.py:50
  52.2 5.5 %all-to-all-start.2 = ((bf16[16,16,2688]{2,1,0:T(8,128)(2,1)}), bf16[16,16,2688]{2,1,0:T(8,128)(2,1)S(1)}, u32[]{:S(2)}, u32[]{:S(2)}) async-start(bf16[16,16,2688]{2,1,0:T(8,128)(2,1)} %bitcast.18), calls=%async_computation.2 | async-start | bytes 2752512 | tf_op jit(solution)/shard_map/all_to_all | solution.py:50
  57.7 0.1 pad.6.clone
  57.7 18.8 %all-to-all-done.2 = bf16[16,16,2688]{2,1,0:T(8,128)(2,1)S(1)} async-done(((bf16[16,16,2688]{2,1,0:T(8,128)(2,1)}), bf16[16,16,2688]{2,1,0:T(8,128)(2,1)S(1)}, u32[]{:S(2)}, u32[]{:S(2)}) %all-to-all-start.2) | async-done | bytes 1376288 | tf_op jit(solution)/shard_map/all_to_all | solution.py:50
  76.5 0.2 convert_reduce_fusion
  76.8 0.1 reshape.59
  76.9 0.7 maximum_maximum_fusion
  77.6 7.9 %all-to-all-start.3 = ((bf16[16,32,128]{2,1,0:T(8,128)(2,1)}), bf16[16,32,128]{2,1,0:T(8,128)(2,1)S(1)}, u32[]{:S(2)}, u32[]{:S(2)}) async-start(bf16[16,32,128]{2,1,0:T(8,128)(2,1)} %maximum_maximum_fusion), calls=%async_computation.3 | async-start | bytes 262144 | tf_op jit(solution)/shard_map/all_to_all | solution.py:50
  85.6 0.7 constant_dynamic-slice_fusion.1
  86.3 10.7 %all-to-all-done.3 = bf16[16,32,128]{2,1,0:T(8,128)(2,1)S(1)} async-done(((bf16[16,32,128]{2,1,0:T(8,128)(2,1)}), bf16[16,32,128]{2,1,0:T(8,128)(2,1)S(1)}, u32[]{:S(2)}, u32[]{:S(2)}) %all-to-all-start.3) | async-done | bytes 131104 | tf_op jit(solution)/shard_map/all_to_all | solution.py:50
  97.2 14.3 %all_to_all.36 = bf16[16,20,128]{2,1,0:T(8,128)(2,1)S(1)} all-to-all(bf16[16,20,128]{2,1,0:T(8,128)(2,1)S(1)} %broadcast_in_dim.40), channel_id=1, replica_groups=mesh['yh'=4,'yl'=2,'core'=2,'x'=4,'zh'=4,'zl'=2] {'yh','zh'}, dimensions={0} | all-to-all | bytes 163840 | tf_op jit(solution)/shard_map/all_to_all | solution.py:44
  111.5 0.1 broadcast_in_dim.42
  111.6 18.9 %all_to_all.37 = bf16[16,16,2560]{2,1,0:T(8,128)(2,1)S(1)} all-to-all(bf16[16,16,2560]{2,1,0:T(8,128)(2,1)S(1)} %broadcast_in_dim.42), channel_id=1, replica_groups=mesh['yh'=4,'yl'=2,'core'=2,'x'=4,'zh'=4,'zl'=2] {'x','yl','zl'}, dimensions={0} | all-to-all | bytes 2621440 | tf_op jit(solution)/shard_map/all_to_all | solution.py:44
  130.5 0.2 broadcast_in_dim.44
  130.6 11.6 %all_to_all.38 = bf16[2,256,2560]{2,1,0:T(8,128)(2,1)} all-to-all(bf16[2,256,2560]{2,1,0:T(8,128)(2,1)S(1)} %broadcast_in_dim.44), channel_id=1, replica_groups=mesh['yh'=4,'yl'=2,'core'=2,'x'=4,'zh'=4,'zl'=2] {'core'}, dimensions={0} | all-to-all | bytes 5242880 | tf_op jit(solution)/shard_map/all_to_all | solution.py:44
  142.2 26.4 %polar.1 = (bf16[512,1024]{1,0:T(8,128)(2,1)}, bf16[1024,256]{1,0:T(8,128)(2,1)}) custom-call(bf16[512,2560]{1,0:T(8,128)(2,1)} %bitcast.21, bf16[512,1024]{1,0:T(8,128)(2,1)} %emb_ref.5), custom_call_target="tpu_custom_call" | custom-call | flops 20000000000 | bytes 8000000 | tf_op jit(solution)/shard_map/polar/pallas_call | solution.py:192
  (17 shorter events, 0.2 us)
Async XLA Ops:
  2.2 28.0 %all-to-all-start = ((bf16[32,2,16,256]{3,2,1,0:T(8,128)(2,1)}), bf16[32,2,16,256]{3,2,1,0:T(8,128)(2,1)S(1)}, u32[]{:S(2)}, u32[]{:S(2)}) async-start(bf16[32,2,16,256]{3,2,1,0:T(8,128)(2,1)} %broadcast_in_dim.36), calls=%async_computation | async-start | bytes 1048576 | tf_op jit(solution)/shard_map/all_to_all | solution.py:44
  30.2 0.8 copy-start
  52.2 24.4 %all-to-all-start.2 = ((bf16[16,16,2688]{2,1,0:T(8,128)(2,1)}), bf16[16,16,2688]{2,1,0:T(8,128)(2,1)S(1)}, u32[]{:S(2)}, u32[]{:S(2)}) async-start(bf16[16,16,2688]{2,1,0:T(8,128)(2,1)} %bitcast.18), calls=%async_computation.2 | async-start | bytes 2752512 | tf_op jit(solution)/shard_map/all_to_all | solution.py:50
  77.6 19.4 %all-to-all-start.3 = ((bf16[16,32,128]{2,1,0:T(8,128)(2,1)}), bf16[16,32,128]{2,1,0:T(8,128)(2,1)S(1)}, u32[]{:S(2)}, u32[]{:S(2)}) async-start(bf16[16,32,128]{2,1,0:T(8,128)(2,1)} %maximum_maximum_fusion), calls=%async_computation.3 | async-start | bytes 262144 | tf_op jit(solution)/shard_map/all_to_all | solution.py:50

commit v3 on v2

v3 whole, which is shorter than its diff:
```python
import jax
import jax.numpy as jnp
from jax import lax
from jax.experimental import pallas as pl
from jax.experimental.pallas import tpu as pltpu
from jax.sharding import Mesh, PartitionSpec as P

ITERS = 4
EPSILON = 1e-06
F32 = jnp.float32
BF16 = jnp.bfloat16

AXES = ("yh", "yl", "core", "x", "zh", "zl")
ROW = ("x", "zh", "zl")
NEAR = ("x", "zl")
FAR = ("yh", "yl", "zh")

D = 1024
SUBS = 64
HALF = SUBS // 2
QUARTER = SUBS // 4
DS = 16
K = 256
TOK = 512
MINE = TOK // 2
LOW = 64.0
BACK = 2 * D + 2 * K
WIDE = BACK + 128

NN = (((1,), (0,)), ((), ()))
NT = (((1,), (1,)), ((), ()))
PARAMS = pltpu.CompilerParams(vmem_limit_bytes=56 * 1024 * 1024)
VMEM = pl.BlockSpec(memory_space=pltpu.VMEM)
SMEM = pl.BlockSpec(memory_space=pltpu.SMEM)


def dot(a, b, dims=NN):
    return lax.dot_general(a, b, dims, preferred_element_type=F32)


def gather(value, axes, peers):
    return lax.all_to_all(
        jnp.broadcast_to(value[None], (peers,) + value.shape), axes, 0, 0, tiled=True
    )


def spread(parts, axes):
    return jnp.sum(lax.all_to_all(parts, axes, 0, 0, tiled=True).astype(F32), axis=0)


def swap(value):
    return lax.ppermute(value, "core", [(0, 1), (1, 0)])


def picks(codes_ref, sub):
    row = codes_ref[pl.ds(sub, 1), :]
    levels = lax.broadcasted_iota(jnp.int32, (K, TOK), 0)
    return jnp.where(levels == row, 1.0, 0.0).astype(BF16)


def tables_kernel(emb_ref, rot_ref, codes_ref, out_ref, turned_ref):
    turned_ref[...] = dot(emb_ref[...], rot_ref[...]).astype(BF16).T
    ones = jnp.ones((DS, TOK), BF16)
    line = lax.broadcasted_iota(jnp.int32, (DS, 128), 0)

    def one(sub):
        at = pl.ds(pl.multiple_of(sub * DS, DS), DS)
        left = jnp.concatenate([turned_ref[at, :], ones], axis=0)
        both = dot(left, picks(codes_ref, sub), NT)
        counts = both[DS:]
        high = jnp.floor(counts * (1.0 / LOW))
        return both[:DS], counts - LOW * high, high

    def step(q, carry):
        at = pl.ds(pl.multiple_of(q * DS, DS), DS)
        for side in range(2):
            digits = jnp.zeros((DS, 128), F32)
            for half in range(2):
                sums, low, high = one(2 * (q + QUARTER * half) + side)
                out_ref[side, at, K * half : K * half + K] = sums.astype(BF16)
                parts = (low[:, :128], low[:, 128:], high[:, :128], high[:, 128:])
                for place, part in enumerate(parts):
                    digits = jnp.where(line == 4 * half + place, part, digits)
            out_ref[side, at, 2 * K :] = digits.astype(BF16)
        return carry

    lax.fori_loop(0, QUARTER, step, 0, unroll=2)


def tables(embeddings, rotation, codes):
    return pl.pallas_call(
        tables_kernel,
        out_shape=jax.ShapeDtypeStruct((2, MINE, 2 * K + 128), BF16),
        in_specs=[VMEM] * 3,
        out_specs=VMEM,
        scratch_shapes=[pltpu.VMEM((D, TOK), BF16)],
        compiler_params=PARAMS,
        cost_estimate=pl.CostEstimate(flops=8 * 10**9, bytes_accessed=4 * 10**6, transcendentals=0),
        name="tables",
    )(embeddings, rotation, codes)


def cross_kernel(side_ref, emb_ref, codes_ref, book_ref, table_ref, out_ref, rebuilt_ref):
    side = side_ref[0]

    def step(q, carry):
        at = pl.ds(pl.multiple_of(q * DS, DS), DS)
        rebuilt_ref[at, :] = dot(book_ref[at, :], picks(codes_ref, 2 * q + side)).astype(BF16)
        return carry

    lax.fori_loop(0, HALF, step, 0, unroll=8)
    part = dot(rebuilt_ref[...], emb_ref[...])
    out_ref[:, :D] = part[:MINE].astype(BF16)
    out_ref[:, D : 2 * D] = part[MINE:].astype(BF16)
    out_ref[:, 2 * D :] = table_ref[side]


def crosses(side, embeddings, codes, book, table):
    return pl.pallas_call(
        cross_kernel,
        out_shape=jax.ShapeDtypeStruct((MINE, WIDE), BF16),
        in_specs=[SMEM] + [VMEM] * 4,
        out_specs=VMEM,
        scratch_shapes=[pltpu.VMEM((TOK, TOK), BF16)],
        compiler_params=PARAMS,
        cost_estimate=pl.CostEstimate(flops=4 * 10**9, bytes_accessed=4 * 10**6, transcendentals=0),
        name="crosses",
    )(side, embeddings, codes, book, table)


def gram_of(y_ref, gram_ref, squares=False):
    mid = D // 2
    top = dot(y_ref[:mid, :], y_ref[...], NT)
    low = dot(y_ref[mid:, :], y_ref[mid:, :], NT)
    gram_ref[:mid, :] = top.astype(BF16)
    gram_ref[mid:, :mid] = top[:, mid:].astype(BF16).T
    gram_ref[mid:, mid:] = low.astype(BF16)
    if squares:
        left, right = top[:, :mid], top[:, mid:]
        return jnp.sum(left * left + 2.0 * (right * right) + low * low, keepdims=True)
    return None


def polar_kernel(side_ref, mine_ref, other_ref, emb_ref, out_ref, book_ref, a_ref, b_ref, gram_ref, polar_ref):
    side = side_ref[0]
    for rows_ref, at in ((mine_ref, side), (other_ref, 1 - side)):
        for q in range(HALF):
            here = pl.ds((q % QUARTER) * DS, DS)
            left = (q // QUARTER) * D
            a_ref[pl.ds(pl.multiple_of((2 * q + at) * DS, DS), DS), :] = rows_ref[here, left : left + D]
            left = 2 * D + (q // QUARTER) * K
            book_ref[2 * q + at] = rows_ref[here, left : left + K]

    blocks = [pl.ds(i * (D // 2), D // 2) for i in range(2)]
    norm_square = jnp.sqrt(gram_of(a_ref, gram_ref, squares=True)) + EPSILON
    scale = lax.rsqrt(norm_square)
    for at in blocks:
        moved = dot(gram_ref[at, :], a_ref[...])
        part = (1.5 * scale) * a_ref[at, :].astype(F32) - (0.5 * scale / norm_square) * moved
        polar_ref[at, :] = part
        b_ref[at, :] = part.astype(BF16)
    now, later = b_ref, a_ref
    for turn in range(1, ITERS - 1):
        gram_of(now, gram_ref)
        for at in blocks:
            part = 1.5 * polar_ref[at, :] - 0.5 * dot(gram_ref[at, :], now[...])
            if turn < ITERS - 2:
                polar_ref[at, :] = part
            later[at, :] = part.astype(BF16)
        now, later = later, now
    gram_of(now, gram_ref)
    turned = dot(emb_ref[...], now[...], NT)
    out_ref[...] = (1.5 * turned - 0.5 * dot(turned.astype(BF16), gram_ref[...])).astype(BF16)


def finish(side, mine, other, embeddings):
    return pl.pallas_call(
        polar_kernel,
        out_shape=(
            jax.ShapeDtypeStruct((TOK, D), BF16),
            jax.ShapeDtypeStruct((SUBS, DS, K), BF16),
        ),
        in_specs=[SMEM] + [VMEM] * 3,
        out_specs=(VMEM,) * 2,
        scratch_shapes=[
            pltpu.VMEM((D, D), BF16),
            pltpu.VMEM((D, D), BF16),
            pltpu.VMEM((D, D), BF16),
            pltpu.VMEM((D, D), F32),
        ],
        compiler_params=PARAMS,
        cost_estimate=pl.CostEstimate(flops=20 * 10**9, bytes_accessed=8 * 10**6, transcendentals=0),
        name="polar",
    )(side, mine, other, embeddings)


def local(embeddings, rotation, pq_codes, codebook):
    codes = pq_codes.T
    core = lax.axis_index("core")
    mine, other = jnp.full((1,), core, jnp.int32), jnp.full((1,), 1 - core, jnp.int32)

    theirs = lax.dynamic_index_in_dim(codebook, 1 - core, 0, keepdims=False)
    other_book = gather(theirs, ROW, HALF).reshape(HALF * DS, K)
    table = tables(embeddings, rotation, codes)
    mine_book = swap(other_book)
    sent = crosses(other, embeddings, codes, other_book, table)
    got = swap(sent)
    kept = crosses(mine, embeddings, codes, mine_book, table)

    pair = (got.astype(F32) + kept.astype(F32)).astype(BF16)
    near = spread(pair.reshape(8, 32, WIDE), NEAR)
    counted = near[:, BACK:].reshape(2, 16, 128)[:, :8].reshape(2, 2, 2, K)
    counted = counted[:, :, 0] + LOW * counted[:, :, 1]
    high = jnp.floor(counted * (1.0 / 256.0))
    digits = jnp.concatenate([counted - 256.0 * high, high], axis=1).reshape(2, 1, 8, 128)
    far = jnp.concatenate(
        [
            near[:, :BACK].reshape(32, 20, 128),
            jnp.broadcast_to(digits, (2, 16, 8, 128)).reshape(32, 8, 128),
            jnp.zeros((32, 4, 128), F32),
        ],
        axis=1,
    ).astype(BF16)
    total = spread(far, FAR)

    owner = lax.axis_index(NEAR) * 32 + lax.axis_index(FAR)
    old = jnp.concatenate(
        [lax.dynamic_slice_in_dim(mine_book, owner + MINE * half, 1, 0) for half in range(2)], axis=0
    ).astype(F32)
    own_sums = total[16:20].reshape(2, K)
    own_counts = total[20:24].reshape(2, K) + 256.0 * total[24:28].reshape(2, K)
    fresh = jnp.where(own_counts > 0, own_sums / jnp.maximum(own_counts, 1.0), old)
    own = jnp.concatenate([total[:16], fresh.reshape(4, 128)], axis=0).astype(BF16)

    rows = gather(own, FAR, 32).reshape(32, BACK)
    rows = gather(rows, NEAR, 8).reshape(MINE, BACK)
    rerotated, new_codebook = finish(mine, rows, swap(rows), embeddings)
    return (new_codebook, rerotated)


def solution(mesh):
    split = Mesh(mesh.devices.reshape(4, 2, 2, 4, 4, 2), AXES)
    placed = (P(AXES, None), P(), P(AXES, None), P(ROW, None, None))
    return jax.shard_map(
        local, mesh=split, in_specs=placed, out_specs=(P(), P(AXES, None)), check_vma=False
    )
```

time: 169 us -> 160 us (0.947)
  blocking collectives: 55.1 us -> 36.9 us
  starting transfers between devices: 27.1 us -> 40.5 us
  Pallas kernels: 46 us -> 38.7 us
    ppermute x0 -> x3, starting transfers between devices: none -> 13.1 us  [swap(): return lax.ppermute(value, 'core', [(0, 1), (1, 0)])]
    all_to_all x1 -> x0, blocking collectives: 10.3 us -> none  [spread(): lax.all_to_all(parts, axes, 0, 0, tiled=True).astype(F32)]
    all_to_all x3 -> x2, blocking collectives: 44.8 us -> 36.9 us  [gather(): lax.all_to_all(jnp.broadcast_to(value[None], (peers,) + value.shape), axe...]
    pallas_call x1, Pallas kernels: 26.4 us -> 18.9 us  [finish(): pl.pallas_call(polar_kernel, out_shape=(jax.ShapeDtypeStruct((TOK, D), BF...]
    ppermute x0 -> x3, waiting for transfers between devices: none -> 4.17 us  [swap(): return lax.ppermute(value, 'core', [(0, 1), (1, 0)])]
    all_to_all x1, waiting for transfers between devices: 3.6 us -> 0.01 us  [gather(): lax.all_to_all(jnp.broadcast_to(value[None], (peers,) + value.shape), axe...]
    convert_element_type x1 -> x2, other arithmetic: 0.01 us -> 2.75 us  [the longest x1 2.74 us: local(): pair = (got.astype(F32) + kept.astype(F32)).astype(BF16)]
    unnamed x3 -> x11, local copies, waits for them, and re-layouts: 0.81 us -> 3.2 us
  transfers between devices with their start and end apart: 3 -> 6, of which waited for: 3 -> 4; matrix products, arithmetic and copies ran while one was open for 0% -> 1% of each run, Pallas kernels for 6% -> 9%
where the time goes in v3:
time: 160 us
  starting transfers between devices  40.5 us (25%)
  Pallas kernels  38.7 us (24%)
  blocking collectives  36.9 us (23%)
  waiting for transfers between devices  34 us (21%)
  local copies, waits for them, and re-layouts  5.04 us (3%)
  other arithmetic  3.85 us (2%)
    all_to_all x2, blocking collectives, gather(): lax.all_to_all(jnp.broadcast_to(value[None], (peers,) + value.shape), axe...  36.9 us
    all_to_all x2, waiting for transfers between devices, spread(): lax.all_to_all(parts, axes, 0, 0, tiled=True).astype(F32)  29.8 us
    pallas_call x1, Pallas kernels, finish(): pl.pallas_call(polar_kernel, out_shape=(jax.ShapeDtypeStruct((TOK, D), BF...  18.9 us
    all_to_all x1, starting transfers between devices, gather(): lax.all_to_all(jnp.broadcast_to(value[None], (peers,) + value.shape), axe...  13.7 us
    all_to_all x2, starting transfers between devices, spread(): lax.all_to_all(parts, axes, 0, 0, tiled=True).astype(F32)  13.7 us
    ppermute x3, starting transfers between devices, swap(): return lax.ppermute(value, 'core', [(0, 1), (1, 0)])  13.1 us
    pallas_call x1, Pallas kernels, tables(): pl.pallas_call(tables_kernel, out_shape=jax.ShapeDtypeStruct((2, MINE, 2...  9.92 us
    pallas_call x2, Pallas kernels, crosses(): pl.pallas_call(cross_kernel, out_shape=jax.ShapeDtypeStruct((MINE, WIDE),...  9.83 us
  transfers between devices with their start and end apart: 6, of which 4 were waited for; matrix products, arithmetic and copies ran while one was open for 1% of the time, Pallas kernels for 9%

profile of v3, /device:TPU:1, one launch (start us, length us, event | category | flops | bytes accessed | tf_op | source)
XLA Modules:
  0.0 159.8 jit_solution(3744379418907543373)
XLA Ops:
  0.6 0.0 copy-start
  0.7 0.7 copy-done
  1.4 0.7 broadcast_in_dim.40
  2.1 13.7 %all-to-all-start = ((bf16[32,16,256]{2,1,0:T(8,128)(2,1)}), bf16[32,16,256]{2,1,0:T(8,128)(2,1)S(1)}, u32[]{:S(2)}, u32[]{:S(2)}) async-start(bf16[32,16,256]{2,1,0:T(8,128)(2,1)} %broadcast_in_dim.40), calls=%async_computation | async-start | bytes 524288 | tf_op jit(solution)/shard_map/all_to_all | solution.py:42
  15.8 9.9 %tables.1.table_ref = bf16[2,256,640]{2,1,0:T(8,128)(2,1)} custom-call(bf16[512,1024]{1,0:T(8,128)(2,1)} %emb_ref.7, bf16[1024,1024]{1,0:T(8,128)(2,1)} %rot_ref.1, s32[64,512]{1,0:T(8,128)} %bitcast.29), custom_call_target="tpu_custom_call" | custom-call | flops 8000000000 | bytes 4000000 | tf_op jit(solution)/shard_map/tables/pallas_call | solution.py:91
  25.7 0.0 all-to-all-done
  25.7 0.0 copy-start.2
  25.7 0.7 copy-done.2
  26.4 4.9 %crosses.2 = bf16[256,2688]{1,0:T(8,128)(2,1)} custom-call(s32[1]{0:T(128)} %bitcast.1.side_ref, bf16[512,1024]{1,0:T(8,128)(2,1)} %emb_ref.7, s32[64,512]{1,0:T(8,128)} %bitcast.30, bf16[512,256]{1,0:T(8,128)(2,1)} %bitcast.26, bf16[2,256,640]{2,1,0:T(8,128)(2,1)} %tables.1.table_ref), custom_call_target="tpu_custom_call" | custom-call | flops 4000000000 | bytes 4000000 | tf_op jit(solution)/shard_map/crosses/pallas_call | solution.py:119
  31.3 5.4 %collective-permute-start = (bf16[256,2688]{1,0:T(8,128)(2,1)}, bf16[256,2688]{1,0:T(8,128)(2,1)S(1)}, u32[]{:S(2)}, u32[]{:S(2)}) collective-permute-start(bf16[256,2688]{1,0:T(8,128)(2,1)} %crosses.2), channel_id=1, source_target_pairs={{0,32},{32,0},{1,33},{33,1},{2,34},{34,2},{3,35},{35,3},{4,36},{36... | collective-permute-start | bytes 4128776 | tf_op jit(solution)/shard_map/ppermute | solution.py:52
  36.7 1.9 %collective-permute-start.1 = (bf16[512,256]{1,0:T(8,128)(2,1)}, bf16[512,256]{1,0:T(8,128)(2,1)S(1)}, u32[]{:S(2)}, u32[]{:S(2)}) collective-permute-start(bf16[512,256]{1,0:T(8,128)(2,1)} %bitcast.27), channel_id=1, source_target_pairs={{0,32},{32,0},{1,33},{33,1},{2,34},{34,2},{3,35},{35,3},{4,36},{36... | collective-permute-start | bytes 786440 | tf_op jit(solution)/shard_map/ppermute | solution.py:52
  38.7 1.7 %collective-permute-done.1.book_ref = bf16[512,256]{1,0:T(8,128)(2,1)S(1)} collective-permute-done((bf16[512,256]{1,0:T(8,128)(2,1)}, bf16[512,256]{1,0:T(8,128)(2,1)S(1)}, u32[]{:S(2)}, u32[]{:S(2)}) %collective-permute-start.1) | collective-permute-done | bytes 262176 | tf_op jit(solution)/shard_map/ppermute | solution.py:52
  40.4 0.0 copy-start.3
  40.4 0.7 copy-done.3
  41.1 4.9 %crosses.3 = bf16[256,2688]{1,0:T(8,128)(2,1)} custom-call(s32[1]{0:T(128)} %bitcast.side_ref, bf16[512,1024]{1,0:T(8,128)(2,1)} %emb_ref.7, s32[64,512]{1,0:T(8,128)} %bitcast.31, bf16[512,256]{1,0:T(8,128)(2,1)} %copy-done.3, bf16[2,256,640]{2,1,0:T(8,128)(2,1)} %tables.1.table_ref), custom_call_target="tpu_custom_call" | custom-call | flops 4000000000 | bytes 4000000 | tf_op jit(solution)/shard_map/crosses/pallas_call | solution.py:119
  46.0 0.0 collective-permute-done
  46.0 2.7 %add_convert_fusion = bf16[256,2688]{1,0:T(8,128)(2,1)} fusion(bf16[256,2688]{1,0:T(8,128)(2,1)} %crosses.3, bf16[256,2688]{1,0:T(8,128)(2,1)S(1)} %collective-permute-done), kind=kLoop, calls=%fused_computation.1 | loop fusion | flops 2752512 | bytes 4128768 | tf_op jit(solution)/shard_map/convert_element_type | solution.py:210
  48.7 3.6 %all-to-all-start.1 = ((bf16[8,32,2688]{2,1,0:T(8,128)(2,1)}), bf16[8,32,2688]{2,1,0:T(8,128)(2,1)S(1)}, u32[]{:S(2)}, u32[]{:S(2)}) async-start(bf16[8,32,2688]{2,1,0:T(8,128)(2,1)} %bitcast.5), calls=%async_computation.1 | async-start | bytes 2752512 | tf_op jit(solution)/shard_map/all_to_all | solution.py:48
  52.3 0.1 pad.6.clone
  52.4 19.0 %all-to-all-done.1 = bf16[8,32,2688]{2,1,0:T(8,128)(2,1)S(1)} async-done(((bf16[8,32,2688]{2,1,0:T(8,128)(2,1)}), bf16[8,32,2688]{2,1,0:T(8,128)(2,1)S(1)}, u32[]{:S(2)}, u32[]{:S(2)}) %all-to-all-start.1) | async-done | bytes 1376288 | tf_op jit(solution)/shard_map/all_to_all | solution.py:48
  71.4 0.2 convert_reduce_fusion
  71.7 0.1 reshape.57
  71.8 0.8 maximum_maximum_fusion
  72.6 10.1 %all-to-all-start.2 = ((bf16[32,32,128]{2,1,0:T(8,128)(2,1)}), bf16[32,32,128]{2,1,0:T(8,128)(2,1)S(1)}, u32[]{:S(2)}, u32[]{:S(2)}) async-start(bf16[32,32,128]{2,1,0:T(8,128)(2,1)} %maximum_maximum_fusion), calls=%async_computation.2 | async-start | bytes 524288 | tf_op jit(solution)/shard_map/all_to_all | solution.py:48
  82.8 0.7 constant_dynamic-slice_fusion.1
  83.5 10.9 %all-to-all-done.2 = bf16[32,32,128]{2,1,0:T(8,128)(2,1)S(1)} async-done(((bf16[32,32,128]{2,1,0:T(8,128)(2,1)}), bf16[32,32,128]{2,1,0:T(8,128)(2,1)S(1)}, u32[]{:S(2)}, u32[]{:S(2)}) %all-to-all-start.2) | async-done | bytes 262176 | tf_op jit(solution)/shard_map/all_to_all | solution.py:48
  94.5 17.7 %all_to_all.25 = bf16[32,20,128]{2,1,0:T(8,128)(2,1)S(1)} all-to-all(bf16[32,20,128]{2,1,0:T(8,128)(2,1)S(1)} %broadcast_in_dim.44), channel_id=1, replica_groups=mesh['yh'=4,'yl'=2,'core'=2,'x'=4,'zh'=4,'zl'=2] {'yh','yl','zh'}, dimensions={0} | all-to-all | bytes 327680 | tf_op jit(solution)/shard_map/all_to_all | solution.py:42
  112.3 0.1 broadcast_in_dim.46
  112.4 19.2 %all_to_all.26 = bf16[8,32,2560]{2,1,0:T(8,128)(2,1)S(1)} all-to-all(bf16[8,32,2560]{2,1,0:T(8,128)(2,1)S(1)} %broadcast_in_dim.46), channel_id=1, replica_groups=mesh['yh'=4,'yl'=2,'core'=2,'x'=4,'zh'=4,'zl'=2] {'x','zl'}, dimensions={0} | all-to-all | bytes 2621440 | tf_op jit(solution)/shard_map/all_to_all | solution.py:42
  131.6 0.0 copy-start.1
  131.6 5.8 %collective-permute-start.2 = (bf16[256,2560]{1,0:T(8,128)(2,1)S(1)}, bf16[256,2560]{1,0:T(8,128)(2,1)S(1)}, u32[]{:S(2)}, u32[]{:S(2)}) collective-permute-start(bf16[256,2560]{1,0:T(8,128)(2,1)S(1)} %bitcast.21), channel_id=1, source_target_pairs={{0,32},{32,0},{1,33},{33,1},{2,34},{34,2},{3,35},{35,3},{4,36},{36... | collective-permute-start | bytes 3932168 | tf_op jit(solution)/shard_map/ppermute | solution.py:52
  137.4 2.5 %collective-permute-done.2.other_ref = bf16[256,2560]{1,0:T(8,128)(2,1)S(1)} collective-permute-done((bf16[256,2560]{1,0:T(8,128)(2,1)S(1)}, bf16[256,2560]{1,0:T(8,128)(2,1)S(1)}, u32[]{:S(2)}, u32[]{:S(2)}) %collective-permute-start.2) | collective-permute-done | bytes 1310752 | tf_op jit(solution)/shard_map/ppermute | solution.py:52
  139.8 0.0 copy-done.1
  139.8 0.0 copy-start.4
  139.8 1.1 copy-done.4
  140.9 18.9 %polar.1 = (bf16[512,1024]{1,0:T(8,128)(2,1)}, bf16[64,16,256]{2,1,0:T(8,128)(2,1)}) custom-call(s32[1]{0:T(128)} %bitcast.side_ref, bf16[256,2560]{1,0:T(8,128)(2,1)} %bitcast.22, bf16[256,2560]{1,0:T(8,128)(2,1)} %copy-done.4, bf16[512,1024]{1,0:T(8,128)(2,1)} %emb_ref.7), custom_call_target="tpu_custom_call" | custom-call | flops 20000000000 | bytes 8000000 | tf_op jit(solution)/shard_map/polar/pallas_call | solution.py:177
  (19 shorter events, 0.2 us)
Async XLA Ops:
  0.6 0.7 copy-start
  2.1 23.7 %all-to-all-start = ((bf16[32,16,256]{2,1,0:T(8,128)(2,1)}), bf16[32,16,256]{2,1,0:T(8,128)(2,1)S(1)}, u32[]{:S(2)}, u32[]{:S(2)}) async-start(bf16[32,16,256]{2,1,0:T(8,128)(2,1)} %broadcast_in_dim.40), calls=%async_computation | async-start | bytes 524288 | tf_op jit(solution)/shard_map/all_to_all | solution.py:42
  25.7 0.7 copy-start.2
  31.3 14.7 %collective-permute-start = (bf16[256,2688]{1,0:T(8,128)(2,1)}, bf16[256,2688]{1,0:T(8,128)(2,1)S(1)}, u32[]{:S(2)}, u32[]{:S(2)}) collective-permute-start(bf16[256,2688]{1,0:T(8,128)(2,1)} %crosses.2), channel_id=1, source_target_pairs={{0,32},{32,0},{1,33},{33,1},{2,34},{34,2},{3,35},{35,3},{4,36},{36... | collective-permute-start | bytes 4128776 | tf_op jit(solution)/shard_map/ppermute | solution.py:52
  36.7 3.6 %collective-permute-start.1 = (bf16[512,256]{1,0:T(8,128)(2,1)}, bf16[512,256]{1,0:T(8,128)(2,1)S(1)}, u32[]{:S(2)}, u32[]{:S(2)}) collective-permute-start(bf16[512,256]{1,0:T(8,128)(2,1)} %bitcast.27), channel_id=1, source_target_pairs={{0,32},{32,0},{1,33},{33,1},{2,34},{34,2},{3,35},{35,3},{4,36},{36... | collective-permute-start | bytes 786440 | tf_op jit(solution)/shard_map/ppermute | solution.py:52
  40.4 0.7 copy-start.3
  48.7 22.6 %all-to-all-start.1 = ((bf16[8,32,2688]{2,1,0:T(8,128)(2,1)}), bf16[8,32,2688]{2,1,0:T(8,128)(2,1)S(1)}, u32[]{:S(2)}, u32[]{:S(2)}) async-start(bf16[8,32,2688]{2,1,0:T(8,128)(2,1)} %bitcast.5), calls=%async_computation.1 | async-start | bytes 2752512 | tf_op jit(solution)/shard_map/all_to_all | solution.py:48
  72.6 21.8 %all-to-all-start.2 = ((bf16[32,32,128]{2,1,0:T(8,128)(2,1)}), bf16[32,32,128]{2,1,0:T(8,128)(2,1)S(1)}, u32[]{:S(2)}, u32[]{:S(2)}) async-start(bf16[32,32,128]{2,1,0:T(8,128)(2,1)} %maximum_maximum_fusion), calls=%async_computation.2 | async-start | bytes 524288 | tf_op jit(solution)/shard_map/all_to_all | solution.py:48
  131.6 8.3 %copy-start.1 = (bf16[8,32,2560]{2,1,0:T(8,128)(2,1)}, bf16[8,32,2560]{2,1,0:T(8,128)(2,1)S(1)}, u32[]{:S(2)}) copy-start(bf16[8,32,2560]{2,1,0:T(8,128)(2,1)S(1)} %all_to_all.26) | copy-start | bytes 3932164
  131.6 8.2 %collective-permute-start.2 = (bf16[256,2560]{1,0:T(8,128)(2,1)S(1)}, bf16[256,2560]{1,0:T(8,128)(2,1)S(1)}, u32[]{:S(2)}, u32[]{:S(2)}) collective-permute-start(bf16[256,2560]{1,0:T(8,128)(2,1)S(1)} %bitcast.21), channel_id=1, source_target_pairs={{0,32},{32,0},{1,33},{33,1},{2,34},{34,2},{3,35},{35,3},{4,36},{36... | collective-permute-start | bytes 3932168 | tf_op jit(solution)/shard_map/ppermute | solution.py:52
  139.8 1.1 copy-start.4

commit v4 on v3

--- a/solution.py
+++ b/solution.py
@@ -12,8 +12,7 @@
 
 AXES = ("yh", "yl", "core", "x", "zh", "zl")
 ROW = ("x", "zh", "zl")
-NEAR = ("x", "zl")
-FAR = ("yh", "yl", "zh")
+BOX = ("x", "yl", "zl")
 
 D = 1024
 SUBS = 64
@@ -29,7 +28,7 @@
 
 NN = (((1,), (0,)), ((), ()))
 NT = (((1,), (1,)), ((), ()))
-PARAMS = pltpu.CompilerParams(vmem_limit_bytes=56 * 1024 * 1024)
+MIB = 1024 * 1024
 VMEM = pl.BlockSpec(memory_space=pltpu.VMEM)
 SMEM = pl.BlockSpec(memory_space=pltpu.SMEM)
 
@@ -46,6 +45,10 @@
 
 def spread(parts, axes):
     return jnp.sum(lax.all_to_all(parts, axes, 0, 0, tiled=True).astype(F32), axis=0)
+
+
+def total(value, axes, peers):
+    return jnp.sum(gather(value, axes, peers).astype(F32), axis=0)
 
 
 def swap(value):
@@ -94,7 +97,7 @@
         in_specs=[VMEM] * 3,
         out_specs=VMEM,
         scratch_shapes=[pltpu.VMEM((D, TOK), BF16)],
-        compiler_params=PARAMS,
+        compiler_params=pltpu.CompilerParams(vmem_limit_bytes=20 * MIB),
         cost_estimate=pl.CostEstimate(flops=8 * 10**9, bytes_accessed=4 * 10**6, transcendentals=0),
         name="tables",
     )(embeddings, rotation, codes)
@@ -122,7 +125,7 @@
         in_specs=[SMEM] + [VMEM] * 4,
         out_specs=VMEM,
         scratch_shapes=[pltpu.VMEM((TOK, TOK), BF16)],
-        compiler_params=PARAMS,
+        compiler_params=pltpu.CompilerParams(vmem_limit_bytes=16 * MIB),
         cost_estimate=pl.CostEstimate(flops=4 * 10**9, bytes_accessed=4 * 10**6, transcendentals=0),
         name="crosses",
     )(side, embeddings, codes, book, table)
@@ -188,7 +191,7 @@
             pltpu.VMEM((D, D), BF16),
             pltpu.VMEM((D, D), F32),
         ],
-        compiler_params=PARAMS,
+        compiler_params=pltpu.CompilerParams(vmem_limit_bytes=32 * MIB),
         cost_estimate=pl.CostEstimate(flops=20 * 10**9, bytes_accessed=8 * 10**6, transcendentals=0),
         name="polar",
     )(side, mine, other, embeddings)
@@ -204,36 +207,34 @@
     table = tables(embeddings, rotation, codes)
     mine_book = swap(other_book)
     sent = crosses(other, embeddings, codes, other_book, table)
+    sent, mine_book = lax.optimization_barrier((sent, mine_book))
     got = swap(sent)
     kept = crosses(mine, embeddings, codes, mine_book, table)
 
     pair = (got.astype(F32) + kept.astype(F32)).astype(BF16)
-    near = spread(pair.reshape(8, 32, WIDE), NEAR)
-    counted = near[:, BACK:].reshape(2, 16, 128)[:, :8].reshape(2, 2, 2, K)
-    counted = counted[:, :, 0] + LOW * counted[:, :, 1]
-    high = jnp.floor(counted * (1.0 / 256.0))
-    digits = jnp.concatenate([counted - 256.0 * high, high], axis=1).reshape(2, 1, 8, 128)
-    far = jnp.concatenate(
-        [
-            near[:, :BACK].reshape(32, 20, 128),
-            jnp.broadcast_to(digits, (2, 16, 8, 128)).reshape(32, 8, 128),
-            jnp.zeros((32, 4, 128), F32),
-        ],
-        axis=1,
-    ).astype(BF16)
-    total = spread(far, FAR)
-
-    owner = lax.axis_index(NEAR) * 32 + lax.axis_index(FAR)
-    old = jnp.concatenate(
-        [lax.dynamic_slice_in_dim(mine_book, owner + MINE * half, 1, 0) for half in range(2)], axis=0
-    ).astype(F32)
-    own_sums = total[16:20].reshape(2, K)
-    own_counts = total[20:24].reshape(2, K) + 256.0 * total[24:28].reshape(2, K)
-    fresh = jnp.where(own_counts > 0, own_sums / jnp.maximum(own_counts, 1.0), old)
-    own = jnp.concatenate([total[:16], fresh.reshape(4, 128)], axis=0).astype(BF16)
-
-    rows = gather(own, FAR, 32).reshape(32, BACK)
-    rows = gather(rows, NEAR, 8).reshape(MINE, BACK)
+    boxed = spread(pair.reshape(16, 16, WIDE), BOX)
+    counted = boxed[:8, BACK:].reshape(2, 2, K)
+    counted = counted[:, 0] + LOW * counted[:, 1]
+    rest = jnp.floor(counted * (1.0 / LOW))
+    high = jnp.floor(rest * (1.0 / LOW))
+    digits = jnp.concatenate([counted - LOW * rest, rest - LOW * high, high], axis=0)
+    digits = jnp.pad(digits.reshape(12, 128), ((0, 4), (0, 0)))
+    packed = jnp.concatenate([boxed[:, :BACK], digits], axis=1).astype(BF16)
+    packed = total(packed, "yh", 4).astype(BF16)
+    summed = total(packed, "zh", 4)
+
+    counted = summed[:12, BACK:].reshape(3, 2, K)
+    counted = counted[0] + LOW * counted[1] + (LOW * LOW) * counted[2]
+    box = lax.axis_index(BOX)
+    fresh = []
+    for half in range(2):
+        old = lax.dynamic_slice_in_dim(mine_book, box * DS + MINE * half, DS, 0).astype(F32)
+        sums = summed[:, 2 * D + K * half : 2 * D + K * half + K]
+        count = counted[half : half + 1]
+        fresh.append(jnp.where(count > 0, sums / jnp.maximum(count, 1.0), old))
+    own = jnp.concatenate([summed[:, : 2 * D]] + fresh, axis=1).astype(BF16)
+
+    rows = gather(own, BOX, 16).reshape(MINE, BACK)
     rerotated, new_codebook = finish(mine, rows, swap(rows), embeddings)
     return (new_codebook, rerotated)
 

time: 160 us -> 141 us (0.88)
  blocking collectives: 36.9 us -> 59.4 us
  waiting for transfers between devices: 34 us -> 11.8 us
  Pallas kernels: 38.7 us -> 28.7 us
  starting transfers between devices: 40.5 us -> 33.2 us
  other arithmetic: 3.85 us -> 0.7 us
    all_to_all x2 -> x0, waiting for transfers between devices: 29.8 us -> none  [spread(): lax.all_to_all(parts, axes, 0, 0, tiled=True).astype(F32)]
    all_to_all x0 -> x1, blocking collectives: none -> 23.2 us  [spread(): lax.all_to_all(parts, axes, 0, 0, tiled=True).astype(F32)]
    all_to_all x2 -> x0, starting transfers between devices: 13.7 us -> none  [spread(): lax.all_to_all(parts, axes, 0, 0, tiled=True).astype(F32)]
    all_to_all x1 -> x2, waiting for transfers between devices: 0.01 us -> 8.49 us  [gather(): lax.all_to_all(jnp.broadcast_to(value[None], (peers,) + value.shape), axe...]
    all_to_all x1 -> x2, starting transfers between devices: 13.7 us -> 19.2 us  [gather(): lax.all_to_all(jnp.broadcast_to(value[None], (peers,) + value.shape), axe...]
    pallas_call x2, Pallas kernels: 9.83 us -> 4.54 us  [crosses(): pl.pallas_call(cross_kernel, out_shape=jax.ShapeDtypeStruct((MINE, WIDE),...]
    pallas_call x1, Pallas kernels: 9.92 us -> 7.22 us  [tables(): pl.pallas_call(tables_kernel, out_shape=jax.ShapeDtypeStruct((2, MINE, 2...]
    convert_element_type x1, other arithmetic: 2.74 us -> 0.33 us  [local(): pair = (got.astype(F32) + kept.astype(F32)).astype(BF16)]
  transfers between devices with their start and end apart: 6 -> 5, of which waited for: 4 -> 3; matrix products, arithmetic and copies ran while one was open for 1% -> 0% of each run, Pallas kernels for 9% -> 8%
where the time goes in v4:
time: 141 us
  blocking collectives  59.4 us (42%)
  starting transfers between devices  33.2 us (24%)
  Pallas kernels  28.7 us (20%)
  waiting for transfers between devices  11.8 us (8%)
  local copies, waits for them, and re-layouts  6.1 us (4%)
    all_to_all x2, blocking collectives, gather(): lax.all_to_all(jnp.broadcast_to(value[None], (peers,) + value.shape), axe...  36.1 us
    all_to_all x1, blocking collectives, spread(): lax.all_to_all(parts, axes, 0, 0, tiled=True).astype(F32)  23.2 us
    all_to_all x2, starting transfers between devices, gather(): lax.all_to_all(jnp.broadcast_to(value[None], (peers,) + value.shape), axe...  19.2 us
    pallas_call x1, Pallas kernels, finish(): pl.pallas_call(polar_kernel, out_shape=(jax.ShapeDtypeStruct((TOK, D), BF...  16.9 us
    ppermute x3, starting transfers between devices, swap(): return lax.ppermute(value, 'core', [(0, 1), (1, 0)])  14 us
    all_to_all x2, waiting for transfers between devices, gather(): lax.all_to_all(jnp.broadcast_to(value[None], (peers,) + value.shape), axe...  8.49 us
    pallas_call x1, Pallas kernels, tables(): pl.pallas_call(tables_kernel, out_shape=jax.ShapeDtypeStruct((2, MINE, 2...  7.22 us
    pallas_call x2, Pallas kernels, crosses(): pl.pallas_call(cross_kernel, out_shape=jax.ShapeDtypeStruct((MINE, WIDE),...  4.54 us
  transfers between devices with their start and end apart: 5, of which 3 were waited for; matrix products, arithmetic and copies ran while one was open for 0% of the time, Pallas kernels for 8%

profile of v4, /device:TPU:1, one launch (start us, length us, event | category | flops | bytes accessed | tf_op | source)
XLA Modules:
  0.0 140.6 jit_solution(3567344861907965429)
XLA Ops:
  0.6 0.0 copy-start
  0.7 0.7 copy-done
  1.4 0.7 broadcast_in_dim.52
  2.1 13.7 %all-to-all-start = ((bf16[32,16,256]{2,1,0:T(8,128)(2,1)}), bf16[32,16,256]{2,1,0:T(8,128)(2,1)S(1)}, u32[]{:S(2)}, u32[]{:S(2)}) async-start(bf16[32,16,256]{2,1,0:T(8,128)(2,1)} %broadcast_in_dim.52), calls=%async_computation | async-start | bytes 524288 | tf_op jit(solution)/shard_map/all_to_all | solution.py:41
  15.8 0.0 copy-start.1
  15.8 1.6 %copy-done.1 = bf16[1024,1024]{1,0:T(8,128)(2,1)S(1)} copy-done((bf16[1024,1024]{1,0:T(8,128)(2,1)S(1)}, bf16[1024,1024]{1,0:T(8,128)(2,1)}, u32[]{:S(2)}) %copy-start.1) | copy-done | bytes 2097176
  17.4 0.0 copy-start.2
  17.4 1.2 copy-done.2
  18.6 0.0 copy-start.4
  18.6 0.9 copy-done.4
  19.5 0.0 copy-start.3
  19.5 0.0 copy-start.5
  19.5 7.2 %tables.1.table_ref = bf16[2,256,640]{2,1,0:T(8,128)(2,1)S(1)} custom-call(bf16[512,1024]{1,0:T(8,128)(2,1)S(1)} %copy-done.2, bf16[1024,1024]{1,0:T(8,128)(2,1)S(1)} %copy-done.1, s32[64,512]{1,0:T(8,128)S(1)} %bitcast.23), custom_call_target="tpu_custom_call" | custom-call | flops 8000000000 | bytes 4000000 | tf_op jit(solution)/shard_map/tables/pallas_call | solution.py:94
  26.8 0.0 all-to-all-done
  26.8 4.3 %collective-permute-start = (bf16[512,256]{1,0:T(8,128)(2,1)S(1)}, bf16[512,256]{1,0:T(8,128)(2,1)S(1)}, u32[]{:S(2)}, u32[]{:S(2)}) collective-permute-start(bf16[512,256]{1,0:T(8,128)(2,1)S(1)} %bitcast.21), channel_id=1, source_target_pairs={{0,32},{32,0},{1,33},{33,1},{2,34},{34,2},{3,35},{35,3},{4,36},{36... | collective-permute-start | bytes 786440 | tf_op jit(solution)/shard_map/ppermute | solution.py:55
  31.1 0.0 copy-done.3
  31.1 0.0 copy-done.5
  31.1 2.3 %crosses.2 = bf16[256,2688]{1,0:T(8,128)(2,1)S(1)} custom-call(s32[1]{0:T(128)} %bitcast.1.side_ref, bf16[512,1024]{1,0:T(8,128)(2,1)S(1)} %copy-done.3, s32[64,512]{1,0:T(8,128)S(1)} %bitcast.24, bf16[512,256]{1,0:T(8,128)(2,1)S(1)} %bitcast.22, bf16[2,256,640]{2,1,0:T(8,128)(2,1)S(1)} %tables.1.table_ref), custom_call_target="tpu_custom_call" | custom-call | flops 4000000000 | bytes 4000000 | tf_op jit(solution)/shard_map/crosses/pallas_call | solution.py:122
  33.4 0.0 collective-permute-done.book_ref
  33.4 1.9 %collective-permute-start.1 = (bf16[256,2688]{1,0:T(8,128)(2,1)S(1)}, bf16[256,2688]{1,0:T(8,128)(2,1)S(1)}, u32[]{:S(2)}, u32[]{:S(2)}) collective-permute-start(bf16[256,2688]{1,0:T(8,128)(2,1)S(1)} %crosses.2), channel_id=1, source_target_pairs={{0,32},{32,0},{1,33},{33,1},{2,34},{34,2},{3,35},{35,3},{4,36},{36... | collective-permute-start | bytes 4128776 | tf_op jit(solution)/shard_map/ppermute | solution.py:55
  35.4 2.3 %crosses.3 = bf16[256,2688]{1,0:T(8,128)(2,1)S(1)} custom-call(s32[1]{0:T(128)} %bitcast.side_ref, bf16[512,1024]{1,0:T(8,128)(2,1)S(1)} %copy-done.3, s32[64,512]{1,0:T(8,128)S(1)} %bitcast.25, bf16[512,256]{1,0:T(8,128)(2,1)S(1)} %collective-permute-done.book_ref, bf16[2,256,640]{2,1,0:T(8,128)(2,1)S(1)} %tables.1.table_ref), custom_call_target="tpu_custom_call" | custom-call | flops 4000000000 | bytes 4000000 | tf_op jit(solution)/shard_map/crosses/pallas_call | solution.py:122
  37.6 0.8 collective-permute-done.1
  38.5 0.3 add_convert_fusion
  38.8 23.2 %all_to_all.25 = bf16[16,16,2688]{2,1,0:T(8,128)(2,1)S(1)} all-to-all(bf16[16,16,2688]{2,1,0:T(8,128)(2,1)S(1)} %bitcast.26), channel_id=1, replica_groups=mesh['yh'=4,'yl'=2,'core'=2,'x'=4,'zh'=4,'zl'=2] {'x','yl','zl'}, dimensions={0} | all-to-all | bytes 2752512 | tf_op jit(solution)/shard_map/all_to_all | solution.py:47
  62.0 0.2 convert_reduce_fusion
  62.4 15.5 %all_to_all.26 = bf16[4,16,2688]{2,1,0:T(8,128)(2,1)S(1)} all-to-all(bf16[4,16,2688]{2,1,0:T(8,128)(2,1)S(1)} %broadcast_in_dim.53), channel_id=1, replica_groups=mesh['yh'=4,'yl'=2,'core'=2,'x'=4,'zh'=4,'zl'=2] {'yh'}, dimensions={0} | all-to-all | bytes 688128 | tf_op jit(solution)/shard_map/all_to_all | solution.py:41
  77.9 0.1 reduce_sum.31
  77.9 0.8 broadcast_in_dim.54
  78.7 5.5 %all-to-all-start.3 = ((bf16[4,16,2688]{2,1,0:T(8,128)(2,1)}), bf16[4,16,2688]{2,1,0:T(8,128)(2,1)S(1)}, u32[]{:S(2)}, u32[]{:S(2)}) async-start(bf16[4,16,2688]{2,1,0:T(8,128)(2,1)} %broadcast_in_dim.54), calls=%async_computation.3 | async-start | bytes 688128 | tf_op jit(solution)/shard_map/all_to_all | solution.py:41
  84.2 8.5 %all-to-all-done.3 = bf16[4,16,2688]{2,1,0:T(8,128)(2,1)S(1)} async-done(((bf16[4,16,2688]{2,1,0:T(8,128)(2,1)}), bf16[4,16,2688]{2,1,0:T(8,128)(2,1)S(1)}, u32[]{:S(2)}, u32[]{:S(2)}) %all-to-all-start.3) | async-done | bytes 344096 | tf_op jit(solution)/shard_map/all_to_all | solution.py:41
  92.8 0.1 broadcast_in_dim.59
  92.9 20.6 %all_to_all.27 = bf16[16,16,2560]{2,1,0:T(8,128)(2,1)S(1)} all-to-all(bf16[16,16,2560]{2,1,0:T(8,128)(2,1)S(1)} %broadcast_in_dim.59), channel_id=1, replica_groups=mesh['yh'=4,'yl'=2,'core'=2,'x'=4,'zh'=4,'zl'=2] {'x','yl','zl'}, dimensions={0} | all-to-all | bytes 2621440 | tf_op jit(solution)/shard_map/all_to_all | solution.py:41
  113.5 7.7 %collective-permute-start.2 = (bf16[256,2560]{1,0:T(8,128)(2,1)S(1)}, bf16[256,2560]{1,0:T(8,128)(2,1)S(1)}, u32[]{:S(2)}, u32[]{:S(2)}) collective-permute-start(bf16[256,2560]{1,0:T(8,128)(2,1)S(1)} %bitcast.19), channel_id=1, source_target_pairs={{0,32},{32,0},{1,33},{33,1},{2,34},{34,2},{3,35},{35,3},{4,36},{36... | collective-permute-start | bytes 3932168 | tf_op jit(solution)/shard_map/ppermute | solution.py:55
  121.3 2.5 %collective-permute-done.2.other_ref = bf16[256,2560]{1,0:T(8,128)(2,1)S(1)} collective-permute-done((bf16[256,2560]{1,0:T(8,128)(2,1)S(1)}, bf16[256,2560]{1,0:T(8,128)(2,1)S(1)}, u32[]{:S(2)}, u32[]{:S(2)}) %collective-permute-start.2) | collective-permute-done | bytes 1310752 | tf_op jit(solution)/shard_map/ppermute | solution.py:55
  123.7 16.9 %polar.1 = (bf16[512,1024]{1,0:T(8,128)(2,1)}, bf16[64,16,256]{2,1,0:T(8,128)(2,1)}) custom-call(s32[1]{0:T(128)} %bitcast.side_ref, bf16[256,2560]{1,0:T(8,128)(2,1)S(1)} %bitcast.20, bf16[256,2560]{1,0:T(8,128)(2,1)S(1)} %collective-permute-done.2.other_ref, bf16[512,1024]{1,0:T(8,128)(2,1)S(1)} %copy-done.3), custom_call_target="tpu_custom_call" | custom-call | flops 20000000000 | bytes 8000000 | tf_op jit(solution)/shard_map/polar/pallas_call | solution.py:180
  (18 shorter events, 0.2 us)
Async XLA Ops:
  0.6 0.7 copy-start
  2.1 24.7 %all-to-all-start = ((bf16[32,16,256]{2,1,0:T(8,128)(2,1)}), bf16[32,16,256]{2,1,0:T(8,128)(2,1)S(1)}, u32[]{:S(2)}, u32[]{:S(2)}) async-start(bf16[32,16,256]{2,1,0:T(8,128)(2,1)} %broadcast_in_dim.52), calls=%async_computation | async-start | bytes 524288 | tf_op jit(solution)/shard_map/all_to_all | solution.py:41
  15.8 1.6 %copy-start.1 = (bf16[1024,1024]{1,0:T(8,128)(2,1)S(1)}, bf16[1024,1024]{1,0:T(8,128)(2,1)}, u32[]{:S(2)}) copy-start(bf16[1024,1024]{1,0:T(8,128)(2,1)} %rot_ref.1) | copy-start | bytes 6291460
  17.4 1.2 copy-start.2
  18.6 0.9 copy-start.4
  19.5 11.6 %copy-start.3 = (bf16[512,1024]{1,0:T(8,128)(2,1)S(1)}, bf16[512,1024]{1,0:T(8,128)(2,1)}, u32[]{:S(2)}) copy-start(bf16[512,1024]{1,0:T(8,128)(2,1)} %emb_ref.7) | copy-start | bytes 3145732
  19.5 11.6 %copy-start.5 = (s32[512,64]{0,1:T(8,128)S(1)}, s32[512,64]{0,1:T(8,128)}, u32[]{:S(2)}) copy-start(s32[512,64]{0,1:T(8,128)} %param.6) | copy-start | bytes 393220
  26.8 6.7 %collective-permute-start = (bf16[512,256]{1,0:T(8,128)(2,1)S(1)}, bf16[512,256]{1,0:T(8,128)(2,1)S(1)}, u32[]{:S(2)}, u32[]{:S(2)}) collective-permute-start(bf16[512,256]{1,0:T(8,128)(2,1)S(1)} %bitcast.21), channel_id=1, source_target_pairs={{0,32},{32,0},{1,33},{33,1},{2,34},{34,2},{3,35},{35,3},{4,36},{36... | collective-permute-start | bytes 786440 | tf_op jit(solution)/shard_map/ppermute | solution.py:55
  33.4 5.0 %collective-permute-start.1 = (bf16[256,2688]{1,0:T(8,128)(2,1)S(1)}, bf16[256,2688]{1,0:T(8,128)(2,1)S(1)}, u32[]{:S(2)}, u32[]{:S(2)}) collective-permute-start(bf16[256,2688]{1,0:T(8,128)(2,1)S(1)} %crosses.2), channel_id=1, source_target_pairs={{0,32},{32,0},{1,33},{33,1},{2,34},{34,2},{3,35},{35,3},{4,36},{36... | collective-permute-start | bytes 4128776 | tf_op jit(solution)/shard_map/ppermute | solution.py:55
  78.7 14.0 %all-to-all-start.3 = ((bf16[4,16,2688]{2,1,0:T(8,128)(2,1)}), bf16[4,16,2688]{2,1,0:T(8,128)(2,1)S(1)}, u32[]{:S(2)}, u32[]{:S(2)}) async-start(bf16[4,16,2688]{2,1,0:T(8,128)(2,1)} %broadcast_in_dim.54), calls=%async_computation.3 | async-start | bytes 688128 | tf_op jit(solution)/shard_map/all_to_all | solution.py:41
  113.5 10.2 %collective-permute-start.2 = (bf16[256,2560]{1,0:T(8,128)(2,1)S(1)}, bf16[256,2560]{1,0:T(8,128)(2,1)S(1)}, u32[]{:S(2)}, u32[]{:S(2)}) collective-permute-start(bf16[256,2560]{1,0:T(8,128)(2,1)S(1)} %bitcast.19), channel_id=1, source_target_pairs={{0,32},{32,0},{1,33},{33,1},{2,34},{34,2},{3,35},{35,3},{4,36},{36... | collective-permute-start | bytes 3932168 | tf_op jit(solution)/shard_map/ppermute | solution.py:55

commit v5 on v4

--- a/solution.py
+++ b/solution.py
@@ -56,48 +56,66 @@
 
 
 def picks(codes_ref, sub):
-    row = codes_ref[pl.ds(sub, 1), :]
-    levels = lax.broadcasted_iota(jnp.int32, (K, TOK), 0)
-    return jnp.where(levels == row, 1.0, 0.0).astype(BF16)
-
-
-def tables_kernel(emb_ref, rot_ref, codes_ref, out_ref, turned_ref):
-    turned_ref[...] = dot(emb_ref[...], rot_ref[...]).astype(BF16).T
-    ones = jnp.ones((DS, TOK), BF16)
+    row = codes_ref[pl.ds(sub, 1), :].astype(jnp.int16)
+    levels = lax.broadcasted_iota(jnp.int32, (K, TOK), 0).astype(jnp.int16)
+    return jnp.where(levels == row, jnp.ones((), BF16), jnp.zeros((), BF16))
+
+
+def tables_kernel(emb_hbm, rot_hbm, codes_hbm, out_ref, emb_ref, rot_ref, codes_ref, sems):
+    copies = [
+        pltpu.make_async_copy(source, target, sems.at[i])
+        for i, (source, target) in enumerate(((emb_hbm, emb_ref), (rot_hbm, rot_ref), (codes_hbm, codes_ref)))
+    ]
+    for copy in copies:
+        copy.start()
+    lane = lax.broadcasted_iota(jnp.int32, (K, 128), 1) // DS
     line = lax.broadcasted_iota(jnp.int32, (DS, 128), 0)
-
-    def one(sub):
-        at = pl.ds(pl.multiple_of(sub * DS, DS), DS)
-        left = jnp.concatenate([turned_ref[at, :], ones], axis=0)
-        both = dot(left, picks(codes_ref, sub), NT)
-        counts = both[DS:]
-        high = jnp.floor(counts * (1.0 / LOW))
-        return both[:DS], counts - LOW * high, high
-
-    def step(q, carry):
-        at = pl.ds(pl.multiple_of(q * DS, DS), DS)
-        for side in range(2):
+    for copy in copies:
+        copy.wait()
+
+    rotated = dot(emb_ref[...], rot_ref[...]).astype(BF16)
+    ones = jnp.ones((TOK, 128), BF16)
+
+    def group(g):
+        right = jnp.concatenate([rotated[:, 128 * g : 128 * g + 128], ones], axis=1)
+        sums = jnp.zeros((K, 128), F32)
+        counts = jnp.zeros((K, 128), F32)
+        for place in range(8):
+            both = dot(picks(codes_ref, 8 * g + place), right)
+            sums = jnp.where(lane == place, both[:, :128], sums)
+            counts = jnp.where(lane == place, both[:, 128:], counts)
+        return sums.T, counts.T
+
+    for g in range(4):
+        made = [group(g), group(g + 4)]
+        for place in range(8):
+            here = slice(DS * place, DS * place + DS)
+            at = pl.ds((4 * g + place // 2) * DS, DS)
             digits = jnp.zeros((DS, 128), F32)
-            for half in range(2):
-                sums, low, high = one(2 * (q + QUARTER * half) + side)
-                out_ref[side, at, K * half : K * half + K] = sums.astype(BF16)
+            for half, (sums, counts) in enumerate(made):
+                out_ref[place % 2, at, K * half : K * half + K] = sums[here].astype(BF16)
+                count = counts[here]
+                high = jnp.floor(count * (1.0 / LOW))
+                low = count - LOW * high
                 parts = (low[:, :128], low[:, 128:], high[:, :128], high[:, 128:])
-                for place, part in enumerate(parts):
-                    digits = jnp.where(line == 4 * half + place, part, digits)
-            out_ref[side, at, 2 * K :] = digits.astype(BF16)
-        return carry
-
-    lax.fori_loop(0, QUARTER, step, 0, unroll=2)
+                for row, part in enumerate(parts):
+                    digits = jnp.where(line == 4 * half + row, part, digits)
+            out_ref[place % 2, at, 2 * K :] = digits.astype(BF16)
 
 
 def tables(embeddings, rotation, codes):
     return pl.pallas_call(
         tables_kernel,
         out_shape=jax.ShapeDtypeStruct((2, MINE, 2 * K + 128), BF16),
-        in_specs=[VMEM] * 3,
+        in_specs=[pl.BlockSpec(memory_space=pl.ANY)] * 3,
         out_specs=VMEM,
-        scratch_shapes=[pltpu.VMEM((D, TOK), BF16)],
-        compiler_params=pltpu.CompilerParams(vmem_limit_bytes=20 * MIB),
+        scratch_shapes=[
+            pltpu.VMEM((TOK, D), BF16),
+            pltpu.VMEM((D, D), BF16),
+            pltpu.VMEM((SUBS, TOK), jnp.int32),
+            pltpu.SemaphoreType.DMA((3,)),
+        ],
+        compiler_params=pltpu.CompilerParams(vmem_limit_bytes=60 * MIB),
         cost_estimate=pl.CostEstimate(flops=8 * 10**9, bytes_accessed=4 * 10**6, transcendentals=0),
         name="tables",
     )(embeddings, rotation, codes)
@@ -111,7 +129,7 @@
         rebuilt_ref[at, :] = dot(book_ref[at, :], picks(codes_ref, 2 * q + side)).astype(BF16)
         return carry
 
-    lax.fori_loop(0, HALF, step, 0, unroll=8)
+    lax.fori_loop(0, HALF, step, 0, unroll=32)
     part = dot(rebuilt_ref[...], emb_ref[...])
     out_ref[:, :D] = part[:MINE].astype(BF16)
     out_ref[:, D : 2 * D] = part[MINE:].astype(BF16)
@@ -132,16 +150,19 @@
 
 
 def gram_of(y_ref, gram_ref, squares=False):
-    mid = D // 2
-    top = dot(y_ref[:mid, :], y_ref[...], NT)
-    low = dot(y_ref[mid:, :], y_ref[mid:, :], NT)
-    gram_ref[:mid, :] = top.astype(BF16)
-    gram_ref[mid:, :mid] = top[:, mid:].astype(BF16).T
-    gram_ref[mid:, mid:] = low.astype(BF16)
-    if squares:
-        left, right = top[:, :mid], top[:, mid:]
-        return jnp.sum(left * left + 2.0 * (right * right) + low * low, keepdims=True)
-    return None
+    size = D // 4
+    total = 0.0
+    for i in range(4):
+        at = slice(i * size, (i + 1) * size)
+        part = dot(y_ref[at, :], y_ref[i * size :, :], NT)
+        gram_ref[at, i * size :] = part.astype(BF16)
+        if i < 3:
+            gram_ref[(i + 1) * size :, at] = part[:, size:].astype(BF16).T
+        if squares:
+            total = total + jnp.sum(part[:, :size] * part[:, :size], keepdims=True)
+            if i < 3:
+                total = total + 2.0 * jnp.sum(part[:, size:] * part[:, size:], keepdims=True)
+    return total
 
 
 def polar_kernel(side_ref, mine_ref, other_ref, emb_ref, out_ref, book_ref, a_ref, b_ref, gram_ref, polar_ref):

time: 141 us -> 139 us (0.986)
  local copies, waits for them, and re-layouts: 6.1 us -> 3.48 us
  waiting for transfers between devices: 11.8 us -> 13.3 us
    unnamed x12 -> x8, local copies, waits for them, and re-layouts: 4.43 us -> 1.81 us
    all_to_all x2, starting transfers between devices: 19.2 us -> 17.2 us  [gather(): lax.all_to_all(jnp.broadcast_to(value[None], (peers,) + value.shape), axe...]
  transfers between devices with their start and end apart: 5 -> 5, of which waited for: 3 -> 4; matrix products, arithmetic and copies ran while one was open for 0% -> 0% of each run, Pallas kernels for 8% -> 9%
where the time goes in v5:
time: 139 us; the launch traced here: 138 us
  blocking collectives  59 us (42%)
  starting transfers between devices  32.5 us (23%)
  Pallas kernels  28.2 us (20%)
  waiting for transfers between devices  13.3 us (10%)
  local copies, waits for them, and re-layouts  3.48 us (3%)
    all_to_all x2, blocking collectives, gather(): lax.all_to_all(jnp.broadcast_to(value[None], (peers,) + value.shape), axe...  36.1 us
    all_to_all x1, blocking collectives, spread(): lax.all_to_all(parts, axes, 0, 0, tiled=True).astype(F32)  22.9 us
    all_to_all x2, starting transfers between devices, gather(): lax.all_to_all(jnp.broadcast_to(value[None], (peers,) + value.shape), axe...  17.2 us
    pallas_call x1, Pallas kernels, finish(): pl.pallas_call(polar_kernel, out_shape=(jax.ShapeDtypeStruct((TOK, D), BF...  16 us
    ppermute x3, starting transfers between devices, swap(): return lax.ppermute(value, 'core', [(0, 1), (1, 0)])  15.3 us
    all_to_all x2, waiting for transfers between devices, gather(): lax.all_to_all(jnp.broadcast_to(value[None], (peers,) + value.shape), axe...  9.55 us
    pallas_call x1, Pallas kernels, tables(): pl.pallas_call(tables_kernel, out_shape=jax.ShapeDtypeStruct((2, MINE, 2...  8.59 us
    ppermute x3, waiting for transfers between devices, swap(): return lax.ppermute(value, 'core', [(0, 1), (1, 0)])  3.74 us
  transfers between devices with their start and end apart: 5, of which 4 were waited for; matrix products, arithmetic and copies ran while one was open for 0% of the time, Pallas kernels for 9%

profile of v5, /device:TPU:1, one launch (start us, length us, event | category | flops | bytes accessed | tf_op | source)
XLA Modules:
  0.0 138.0 jit_solution(12803030924773616949)
XLA Ops:
  0.6 0.0 copy-start
  0.7 0.7 copy-done
  1.4 0.7 broadcast_in_dim.52
  2.1 13.7 %all-to-all-start = ((bf16[32,16,256]{2,1,0:T(8,128)(2,1)}), bf16[32,16,256]{2,1,0:T(8,128)(2,1)S(1)}, u32[]{:S(2)}, u32[]{:S(2)}) async-start(bf16[32,16,256]{2,1,0:T(8,128)(2,1)} %broadcast_in_dim.52), calls=%async_computation | async-start | bytes 524288 | tf_op jit(solution)/shard_map/all_to_all | solution.py:41
  15.8 0.0 copy-start.1
  15.8 0.0 copy-start.2
  15.8 8.6 %tables.1.table_ref = bf16[2,256,640]{2,1,0:T(8,128)(2,1)} custom-call(bf16[512,1024]{1,0:T(8,128)(2,1)} %emb_ref.5, bf16[1024,1024]{1,0:T(8,128)(2,1)} %rot_hbm.1, s32[64,512]{1,0:T(8,128)} %bitcast.23), custom_call_target="tpu_custom_call" | custom-call | flops 8000000000 | bytes 4000000 | tf_op jit(solution)/shard_map/tables/pallas_call | solution.py:107
  24.4 1.1 all-to-all-done
  25.5 5.6 %collective-permute-start = (bf16[512,256]{1,0:T(8,128)(2,1)S(1)}, bf16[512,256]{1,0:T(8,128)(2,1)S(1)}, u32[]{:S(2)}, u32[]{:S(2)}) collective-permute-start(bf16[512,256]{1,0:T(8,128)(2,1)S(1)} %bitcast.21), channel_id=1, source_target_pairs={{0,32},{32,0},{1,33},{33,1},{2,34},{34,2},{3,35},{35,3},{4,36},{36... | collective-permute-start | bytes 786440 | tf_op jit(solution)/shard_map/ppermute | solution.py:55
  31.1 0.0 copy-done.1
  31.1 0.0 copy-done.2
  31.1 0.0 copy-start.3
  31.2 1.1 copy-done.3
  32.2 1.8 %crosses.2 = bf16[256,2688]{1,0:T(8,128)(2,1)S(1)} custom-call(s32[1]{0:T(128)} %bitcast.1.side_ref, bf16[512,1024]{1,0:T(8,128)(2,1)S(1)} %copy-done.1, s32[64,512]{1,0:T(8,128)S(1)} %bitcast.24, bf16[512,256]{1,0:T(8,128)(2,1)S(1)} %bitcast.22, bf16[2,256,640]{2,1,0:T(8,128)(2,1)S(1)} %copy-done.3), custom_call_target="tpu_custom_call" | custom-call | flops 4000000000 | bytes 4000000 | tf_op jit(solution)/shard_map/crosses/pallas_call | solution.py:140
  34.0 0.0 collective-permute-done.book_ref
  34.0 1.9 %collective-permute-start.1 = (bf16[256,2688]{1,0:T(8,128)(2,1)S(1)}, bf16[256,2688]{1,0:T(8,128)(2,1)S(1)}, u32[]{:S(2)}, u32[]{:S(2)}) collective-permute-start(bf16[256,2688]{1,0:T(8,128)(2,1)S(1)} %crosses.2), channel_id=1, source_target_pairs={{0,32},{32,0},{1,33},{33,1},{2,34},{34,2},{3,35},{35,3},{4,36},{36... | collective-permute-start | bytes 4128776 | tf_op jit(solution)/shard_map/ppermute | solution.py:55
  36.0 1.8 %crosses.3 = bf16[256,2688]{1,0:T(8,128)(2,1)S(1)} custom-call(s32[1]{0:T(128)} %bitcast.side_ref, bf16[512,1024]{1,0:T(8,128)(2,1)S(1)} %copy-done.1, s32[64,512]{1,0:T(8,128)S(1)} %bitcast.25, bf16[512,256]{1,0:T(8,128)(2,1)S(1)} %collective-permute-done.book_ref, bf16[2,256,640]{2,1,0:T(8,128)(2,1)S(1)} %copy-done.3), custom_call_target="tpu_custom_call" | custom-call | flops 4000000000 | bytes 4000000 | tf_op jit(solution)/shard_map/crosses/pallas_call | solution.py:140
  37.8 1.3 collective-permute-done.1
  39.1 0.3 add_convert_fusion
  39.4 22.9 %all_to_all.25 = bf16[16,16,2688]{2,1,0:T(8,128)(2,1)S(1)} all-to-all(bf16[16,16,2688]{2,1,0:T(8,128)(2,1)S(1)} %bitcast.26), channel_id=1, replica_groups=mesh['yh'=4,'yl'=2,'core'=2,'x'=4,'zh'=4,'zl'=2] {'x','yl','zl'}, dimensions={0} | all-to-all | bytes 2752512 | tf_op jit(solution)/shard_map/all_to_all | solution.py:47
  62.3 0.2 convert_reduce_fusion
  62.6 15.5 %all_to_all.26 = bf16[4,16,2688]{2,1,0:T(8,128)(2,1)S(1)} all-to-all(bf16[4,16,2688]{2,1,0:T(8,128)(2,1)S(1)} %broadcast_in_dim.53), channel_id=1, replica_groups=mesh['yh'=4,'yl'=2,'core'=2,'x'=4,'zh'=4,'zl'=2] {'yh'}, dimensions={0} | all-to-all | bytes 688128 | tf_op jit(solution)/shard_map/all_to_all | solution.py:41
  78.1 0.1 reduce_sum.31
  78.2 0.8 broadcast_in_dim.54
  78.9 3.5 %all-to-all-start.3 = ((bf16[4,16,2688]{2,1,0:T(8,128)(2,1)}), bf16[4,16,2688]{2,1,0:T(8,128)(2,1)S(1)}, u32[]{:S(2)}, u32[]{:S(2)}) async-start(bf16[4,16,2688]{2,1,0:T(8,128)(2,1)} %broadcast_in_dim.54), calls=%async_computation.3 | async-start | bytes 688128 | tf_op jit(solution)/shard_map/all_to_all | solution.py:41
  82.4 8.5 %all-to-all-done.3 = bf16[4,16,2688]{2,1,0:T(8,128)(2,1)S(1)} async-done(((bf16[4,16,2688]{2,1,0:T(8,128)(2,1)}), bf16[4,16,2688]{2,1,0:T(8,128)(2,1)S(1)}, u32[]{:S(2)}, u32[]{:S(2)}) %all-to-all-start.3) | async-done | bytes 344096 | tf_op jit(solution)/shard_map/all_to_all | solution.py:41
  91.1 0.1 broadcast_in_dim.59
  91.2 20.6 %all_to_all.27 = bf16[16,16,2560]{2,1,0:T(8,128)(2,1)S(1)} all-to-all(bf16[16,16,2560]{2,1,0:T(8,128)(2,1)S(1)} %broadcast_in_dim.59), channel_id=1, replica_groups=mesh['yh'=4,'yl'=2,'core'=2,'x'=4,'zh'=4,'zl'=2] {'x','yl','zl'}, dimensions={0} | all-to-all | bytes 2621440 | tf_op jit(solution)/shard_map/all_to_all | solution.py:41
  111.8 7.7 %collective-permute-start.2 = (bf16[256,2560]{1,0:T(8,128)(2,1)S(1)}, bf16[256,2560]{1,0:T(8,128)(2,1)S(1)}, u32[]{:S(2)}, u32[]{:S(2)}) collective-permute-start(bf16[256,2560]{1,0:T(8,128)(2,1)S(1)} %bitcast.19), channel_id=1, source_target_pairs={{0,32},{32,0},{1,33},{33,1},{2,34},{34,2},{3,35},{35,3},{4,36},{36... | collective-permute-start | bytes 3932168 | tf_op jit(solution)/shard_map/ppermute | solution.py:55
  119.6 2.5 %collective-permute-done.2.other_ref = bf16[256,2560]{1,0:T(8,128)(2,1)S(1)} collective-permute-done((bf16[256,2560]{1,0:T(8,128)(2,1)S(1)}, bf16[256,2560]{1,0:T(8,128)(2,1)S(1)}, u32[]{:S(2)}, u32[]{:S(2)}) %collective-permute-start.2) | collective-permute-done | bytes 1310752 | tf_op jit(solution)/shard_map/ppermute | solution.py:55
  122.0 16.0 %polar.1 = (bf16[512,1024]{1,0:T(8,128)(2,1)}, bf16[64,16,256]{2,1,0:T(8,128)(2,1)}) custom-call(s32[1]{0:T(128)} %bitcast.side_ref, bf16[256,2560]{1,0:T(8,128)(2,1)S(1)} %bitcast.20, bf16[256,2560]{1,0:T(8,128)(2,1)S(1)} %collective-permute-done.2.other_ref, bf16[512,1024]{1,0:T(8,128)(2,1)S(1)} %copy-done.1), custom_call_target="tpu_custom_call" | custom-call | flops 20000000000 | bytes 8000000 | tf_op jit(solution)/shard_map/polar/pallas_call | solution.py:201
  (18 shorter events, 0.2 us)
Async XLA Ops:
  0.6 0.7 copy-start
  2.1 23.4 %all-to-all-start = ((bf16[32,16,256]{2,1,0:T(8,128)(2,1)}), bf16[32,16,256]{2,1,0:T(8,128)(2,1)S(1)}, u32[]{:S(2)}, u32[]{:S(2)}) async-start(bf16[32,16,256]{2,1,0:T(8,128)(2,1)} %broadcast_in_dim.52), calls=%async_computation | async-start | bytes 524288 | tf_op jit(solution)/shard_map/all_to_all | solution.py:41
  15.8 15.3 %copy-start.1 = (bf16[512,1024]{1,0:T(8,128)(2,1)S(1)}, bf16[512,1024]{1,0:T(8,128)(2,1)}, u32[]{:S(2)}) copy-start(bf16[512,1024]{1,0:T(8,128)(2,1)} %emb_ref.5) | copy-start | bytes 3145732
  15.8 15.3 %copy-start.2 = (s32[512,64]{0,1:T(8,128)S(1)}, s32[512,64]{0,1:T(8,128)}, u32[]{:S(2)}) copy-start(s32[512,64]{0,1:T(8,128)} %param.6) | copy-start | bytes 393220
  25.5 8.6 %collective-permute-start = (bf16[512,256]{1,0:T(8,128)(2,1)S(1)}, bf16[512,256]{1,0:T(8,128)(2,1)S(1)}, u32[]{:S(2)}, u32[]{:S(2)}) collective-permute-start(bf16[512,256]{1,0:T(8,128)(2,1)S(1)} %bitcast.21), channel_id=1, source_target_pairs={{0,32},{32,0},{1,33},{33,1},{2,34},{34,2},{3,35},{35,3},{4,36},{36... | collective-permute-start | bytes 786440 | tf_op jit(solution)/shard_map/ppermute | solution.py:55
  31.1 1.1 copy-start.3
  34.0 5.0 %collective-permute-start.1 = (bf16[256,2688]{1,0:T(8,128)(2,1)S(1)}, bf16[256,2688]{1,0:T(8,128)(2,1)S(1)}, u32[]{:S(2)}, u32[]{:S(2)}) collective-permute-start(bf16[256,2688]{1,0:T(8,128)(2,1)S(1)} %crosses.2), channel_id=1, source_target_pairs={{0,32},{32,0},{1,33},{33,1},{2,34},{34,2},{3,35},{35,3},{4,36},{36... | collective-permute-start | bytes 4128776 | tf_op jit(solution)/shard_map/ppermute | solution.py:55
  78.9 12.0 %all-to-all-start.3 = ((bf16[4,16,2688]{2,1,0:T(8,128)(2,1)}), bf16[4,16,2688]{2,1,0:T(8,128)(2,1)S(1)}, u32[]{:S(2)}, u32[]{:S(2)}) async-start(bf16[4,16,2688]{2,1,0:T(8,128)(2,1)} %broadcast_in_dim.54), calls=%async_computation.3 | async-start | bytes 688128 | tf_op jit(solution)/shard_map/all_to_all | solution.py:41
  111.8 10.2 %collective-permute-start.2 = (bf16[256,2560]{1,0:T(8,128)(2,1)S(1)}, bf16[256,2560]{1,0:T(8,128)(2,1)S(1)}, u32[]{:S(2)}, u32[]{:S(2)}) collective-permute-start(bf16[256,2560]{1,0:T(8,128)(2,1)S(1)} %bitcast.19), channel_id=1, source_target_pairs={{0,32},{32,0},{1,33},{33,1},{2,34},{34,2},{3,35},{35,3},{4,36},{36... | collective-permute-start | bytes 3932168 | tf_op jit(solution)/shard_map/ppermute | solution.py:55

commit v6 on v5

--- a/solution.py
+++ b/solution.py
@@ -5,7 +5,6 @@
 from jax.experimental.pallas import tpu as pltpu
 from jax.sharding import Mesh, PartitionSpec as P
 
-ITERS = 4
 EPSILON = 1e-06
 F32 = jnp.float32
 BF16 = jnp.bfloat16
@@ -149,52 +148,72 @@
     )(side, embeddings, codes, book, table)
 
 
-def gram_of(y_ref, gram_ref, squares=False):
-    size = D // 4
-    total = 0.0
-    for i in range(4):
-        at = slice(i * size, (i + 1) * size)
-        part = dot(y_ref[at, :], y_ref[i * size :, :], NT)
-        gram_ref[at, i * size :] = part.astype(BF16)
-        if i < 3:
-            gram_ref[(i + 1) * size :, at] = part[:, size:].astype(BF16).T
-        if squares:
-            total = total + jnp.sum(part[:, :size] * part[:, :size], keepdims=True)
-            if i < 3:
-                total = total + 2.0 * jnp.sum(part[:, size:] * part[:, size:], keepdims=True)
-    return total
-
-
-def polar_kernel(side_ref, mine_ref, other_ref, emb_ref, out_ref, book_ref, a_ref, b_ref, gram_ref, polar_ref):
+PARTS = 4
+PART = D // PARTS
+
+
+def symmetric(product, store):
+    for i in range(PARTS):
+        at, right = slice(i * PART, (i + 1) * PART), slice(i * PART, D)
+        for target, value in store(at, right, product(at, right)):
+            target[at, right] = value
+            if i < PARTS - 1:
+                target[(i + 1) * PART :, at] = value[:, PART:].T
+
+
+def two_steps(g_ref, g2_ref, k_ref, w_ref):
+    def square(at, right, part):
+        k = 0.0625 * part - 0.5625 * g_ref[at, right].astype(F32)
+        return (g2_ref, part.astype(BF16)), (k_ref, k.astype(BF16))
+
+    symmetric(lambda at, right: dot(g_ref[at, :], g_ref[:, right]), square)
+
+    def rest(at, right, part):
+        w = part + 1.6875 * g2_ref[at, right].astype(F32) - 2.4375 * g_ref[at, right].astype(F32)
+        return ((w_ref, w.astype(BF16)),)
+
+    symmetric(lambda at, right: dot(g2_ref[at, :], k_ref[:, right]), rest)
+
+
+def polar_kernel(side_ref, mine_ref, other_ref, emb_ref, out_ref, book_ref, y_ref, z_ref, g_ref, g2_ref, k_ref, w_ref, full_ref):
     side = side_ref[0]
     for rows_ref, at in ((mine_ref, side), (other_ref, 1 - side)):
         for q in range(HALF):
             here = pl.ds((q % QUARTER) * DS, DS)
             left = (q // QUARTER) * D
-            a_ref[pl.ds(pl.multiple_of((2 * q + at) * DS, DS), DS), :] = rows_ref[here, left : left + D]
+            y_ref[pl.ds(pl.multiple_of((2 * q + at) * DS, DS), DS), :] = rows_ref[here, left : left + D]
             left = 2 * D + (q // QUARTER) * K
             book_ref[2 * q + at] = rows_ref[here, left : left + K]
 
-    blocks = [pl.ds(i * (D // 2), D // 2) for i in range(2)]
-    norm_square = jnp.sqrt(gram_of(a_ref, gram_ref, squares=True)) + EPSILON
+    squares = 0.0
+    for i in range(PARTS):
+        at, right = slice(i * PART, (i + 1) * PART), slice(i * PART, D)
+        part = dot(y_ref[at, :], y_ref[right, :], NT)
+        full_ref[at, right] = part
+        squares = squares + jnp.sum(part[:, :PART] * part[:, :PART], keepdims=True)
+        if i < PARTS - 1:
+            squares = squares + 2.0 * jnp.sum(part[:, PART:] * part[:, PART:], keepdims=True)
+    norm_square = jnp.sqrt(squares) + EPSILON
     scale = lax.rsqrt(norm_square)
-    for at in blocks:
-        moved = dot(gram_ref[at, :], a_ref[...])
-        part = (1.5 * scale) * a_ref[at, :].astype(F32) - (0.5 * scale / norm_square) * moved
-        polar_ref[at, :] = part
-        b_ref[at, :] = part.astype(BF16)
-    now, later = b_ref, a_ref
-    for turn in range(1, ITERS - 1):
-        gram_of(now, gram_ref)
-        for at in blocks:
-            part = 1.5 * polar_ref[at, :] - 0.5 * dot(gram_ref[at, :], now[...])
-            if turn < ITERS - 2:
-                polar_ref[at, :] = part
-            later[at, :] = part.astype(BF16)
-        now, later = later, now
-    gram_of(now, gram_ref)
-    turned = dot(emb_ref[...], now[...], NT)
-    out_ref[...] = (1.5 * turned - 0.5 * dot(turned.astype(BF16), gram_ref[...])).astype(BF16)
+    shrink = 1.0 / norm_square
+
+    symmetric(
+        lambda at, right: full_ref[at, right],
+        lambda at, right, part: ((g_ref, (part * shrink).astype(BF16)),),
+    )
+    two_steps(g_ref, g2_ref, k_ref, w_ref)
+    for i in range(2):
+        at = slice(i * (D // 2), (i + 1) * (D // 2))
+        part = 2.25 * y_ref[at, :].astype(F32) + dot(w_ref[at, :], y_ref[...])
+        z_ref[at, :] = (scale * part).astype(BF16)
+
+    symmetric(
+        lambda at, right: dot(z_ref[at, :], z_ref[right, :], NT),
+        lambda at, right, part: ((g_ref, part.astype(BF16)),),
+    )
+    turned = dot(emb_ref[...], z_ref[...], NT)
+    two_steps(g_ref, g2_ref, k_ref, w_ref)
+    out_ref[...] = (2.25 * turned + dot(turned.astype(BF16), w_ref[...])).astype(BF16)
 
 
 def finish(side, mine, other, embeddings):
@@ -207,6 +226,9 @@
         in_specs=[SMEM] + [VMEM] * 3,
         out_specs=(VMEM,) * 2,
         scratch_shapes=[
+            pltpu.VMEM((D, D), BF16),
+            pltpu.VMEM((D, D), BF16),
+            pltpu.VMEM((D, D), BF16),
             pltpu.VMEM((D, D), BF16),
             pltpu.VMEM((D, D), BF16),
             pltpu.VMEM((D, D), BF16),
@@ -243,6 +265,7 @@
     packed = jnp.concatenate([boxed[:, :BACK], digits], axis=1).astype(BF16)
     packed = total(packed, "yh", 4).astype(BF16)
     summed = total(packed, "zh", 4)
+    summed, mine_book = lax.optimization_barrier((summed, mine_book))
 
     counted = summed[:12, BACK:].reshape(3, 2, K)
     counted = counted[0] + LOW * counted[1] + (LOW * LOW) * counted[2]

time: 139 us -> 137 us (0.986)
  no operation moved by 1% of the time
where the time goes in v6:
time: 137 us
  blocking collectives  59 us (43%)
  starting transfers between devices  32.5 us (24%)
  Pallas kernels  27.1 us (20%)
  waiting for transfers between devices  13.3 us (10%)
  local copies, waits for them, and re-layouts  3.48 us (3%)
    all_to_all x2, blocking collectives, gather(): lax.all_to_all(jnp.broadcast_to(value[None], (peers,) + value.shape), axe...  36.1 us
    all_to_all x1, blocking collectives, spread(): lax.all_to_all(parts, axes, 0, 0, tiled=True).astype(F32)  22.9 us
    all_to_all x2, starting transfers between devices, gather(): lax.all_to_all(jnp.broadcast_to(value[None], (peers,) + value.shape), axe...  17.2 us
    ppermute x3, starting transfers between devices, swap(): return lax.ppermute(value, 'core', [(0, 1), (1, 0)])  15.3 us
    pallas_call x1, Pallas kernels, finish(): pl.pallas_call(polar_kernel, out_shape=(jax.ShapeDtypeStruct((TOK, D), BF...  14.9 us
    all_to_all x2, waiting for transfers between devices, gather(): lax.all_to_all(jnp.broadcast_to(value[None], (peers,) + value.shape), axe...  9.55 us
    pallas_call x1, Pallas kernels, tables(): pl.pallas_call(tables_kernel, out_shape=jax.ShapeDtypeStruct((2, MINE, 2...  8.59 us
    ppermute x3, waiting for transfers between devices, swap(): return lax.ppermute(value, 'core', [(0, 1), (1, 0)])  3.74 us
  transfers between devices with their start and end apart: 5, of which 4 were waited for; matrix products, arithmetic and copies ran while one was open for 0% of the time, Pallas kernels for 9%

profile of v6, /device:TPU:1, one launch (start us, length us, event | category | flops | bytes accessed | tf_op | source)
XLA Modules:
  0.0 136.9 jit_solution(4508214512979007177)
XLA Ops:
  0.6 0.0 copy-start
  0.7 0.7 copy-done
  1.4 0.7 broadcast_in_dim.52
  2.1 13.7 %all-to-all-start = ((bf16[32,16,256]{2,1,0:T(8,128)(2,1)}), bf16[32,16,256]{2,1,0:T(8,128)(2,1)S(1)}, u32[]{:S(2)}, u32[]{:S(2)}) async-start(bf16[32,16,256]{2,1,0:T(8,128)(2,1)} %broadcast_in_dim.52), calls=%async_computation | async-start | bytes 524288 | tf_op jit(solution)/shard_map/all_to_all | solution.py:40
  15.8 0.0 copy-start.1
  15.8 0.0 copy-start.2
  15.8 8.6 %tables.1.table_ref = bf16[2,256,640]{2,1,0:T(8,128)(2,1)} custom-call(bf16[512,1024]{1,0:T(8,128)(2,1)} %emb_ref.5, bf16[1024,1024]{1,0:T(8,128)(2,1)} %rot_hbm.1, s32[64,512]{1,0:T(8,128)} %bitcast.23), custom_call_target="tpu_custom_call" | custom-call | flops 8000000000 | bytes 4000000 | tf_op jit(solution)/shard_map/tables/pallas_call | solution.py:106
  24.4 1.1 all-to-all-done
  25.5 5.6 %collective-permute-start = (bf16[512,256]{1,0:T(8,128)(2,1)S(1)}, bf16[512,256]{1,0:T(8,128)(2,1)S(1)}, u32[]{:S(2)}, u32[]{:S(2)}) collective-permute-start(bf16[512,256]{1,0:T(8,128)(2,1)S(1)} %bitcast.21), channel_id=1, source_target_pairs={{0,32},{32,0},{1,33},{33,1},{2,34},{34,2},{3,35},{35,3},{4,36},{36... | collective-permute-start | bytes 786440 | tf_op jit(solution)/shard_map/ppermute | solution.py:54
  31.1 0.0 copy-done.1
  31.1 0.0 copy-done.2
  31.1 0.0 copy-start.3
  31.2 1.1 copy-done.3
  32.2 1.8 %crosses.2 = bf16[256,2688]{1,0:T(8,128)(2,1)S(1)} custom-call(s32[1]{0:T(128)} %bitcast.1.side_ref, bf16[512,1024]{1,0:T(8,128)(2,1)S(1)} %copy-done.1, s32[64,512]{1,0:T(8,128)S(1)} %bitcast.24, bf16[512,256]{1,0:T(8,128)(2,1)S(1)} %bitcast.22, bf16[2,256,640]{2,1,0:T(8,128)(2,1)S(1)} %copy-done.3), custom_call_target="tpu_custom_call" | custom-call | flops 4000000000 | bytes 4000000 | tf_op jit(solution)/shard_map/crosses/pallas_call | solution.py:139
  34.0 0.0 collective-permute-done.book_ref
  34.0 1.9 %collective-permute-start.1 = (bf16[256,2688]{1,0:T(8,128)(2,1)S(1)}, bf16[256,2688]{1,0:T(8,128)(2,1)S(1)}, u32[]{:S(2)}, u32[]{:S(2)}) collective-permute-start(bf16[256,2688]{1,0:T(8,128)(2,1)S(1)} %crosses.2), channel_id=1, source_target_pairs={{0,32},{32,0},{1,33},{33,1},{2,34},{34,2},{3,35},{35,3},{4,36},{36... | collective-permute-start | bytes 4128776 | tf_op jit(solution)/shard_map/ppermute | solution.py:54
  36.0 1.8 %crosses.3 = bf16[256,2688]{1,0:T(8,128)(2,1)S(1)} custom-call(s32[1]{0:T(128)} %bitcast.side_ref, bf16[512,1024]{1,0:T(8,128)(2,1)S(1)} %copy-done.1, s32[64,512]{1,0:T(8,128)S(1)} %bitcast.25, bf16[512,256]{1,0:T(8,128)(2,1)S(1)} %collective-permute-done.book_ref, bf16[2,256,640]{2,1,0:T(8,128)(2,1)S(1)} %copy-done.3), custom_call_target="tpu_custom_call" | custom-call | flops 4000000000 | bytes 4000000 | tf_op jit(solution)/shard_map/crosses/pallas_call | solution.py:139
  37.8 1.3 collective-permute-done.1
  39.1 0.3 add_convert_fusion
  39.4 22.9 %all_to_all.25 = bf16[16,16,2688]{2,1,0:T(8,128)(2,1)S(1)} all-to-all(bf16[16,16,2688]{2,1,0:T(8,128)(2,1)S(1)} %bitcast.26), channel_id=1, replica_groups=mesh['yh'=4,'yl'=2,'core'=2,'x'=4,'zh'=4,'zl'=2] {'x','yl','zl'}, dimensions={0} | all-to-all | bytes 2752512 | tf_op jit(solution)/shard_map/all_to_all | solution.py:46
  62.3 0.2 convert_reduce_fusion
  62.6 15.5 %all_to_all.26 = bf16[4,16,2688]{2,1,0:T(8,128)(2,1)S(1)} all-to-all(bf16[4,16,2688]{2,1,0:T(8,128)(2,1)S(1)} %broadcast_in_dim.53), channel_id=1, replica_groups=mesh['yh'=4,'yl'=2,'core'=2,'x'=4,'zh'=4,'zl'=2] {'yh'}, dimensions={0} | all-to-all | bytes 688128 | tf_op jit(solution)/shard_map/all_to_all | solution.py:40
  78.1 0.1 reduce_sum.31
  78.2 0.8 broadcast_in_dim.54
  78.9 3.5 %all-to-all-start.3 = ((bf16[4,16,2688]{2,1,0:T(8,128)(2,1)}), bf16[4,16,2688]{2,1,0:T(8,128)(2,1)S(1)}, u32[]{:S(2)}, u32[]{:S(2)}) async-start(bf16[4,16,2688]{2,1,0:T(8,128)(2,1)} %broadcast_in_dim.54), calls=%async_computation.3 | async-start | bytes 688128 | tf_op jit(solution)/shard_map/all_to_all | solution.py:40
  82.4 8.5 %all-to-all-done.3 = bf16[4,16,2688]{2,1,0:T(8,128)(2,1)S(1)} async-done(((bf16[4,16,2688]{2,1,0:T(8,128)(2,1)}), bf16[4,16,2688]{2,1,0:T(8,128)(2,1)S(1)}, u32[]{:S(2)}, u32[]{:S(2)}) %all-to-all-start.3) | async-done | bytes 344096 | tf_op jit(solution)/shard_map/all_to_all | solution.py:40
  91.1 0.1 broadcast_in_dim.59
  91.2 20.6 %all_to_all.27 = bf16[16,16,2560]{2,1,0:T(8,128)(2,1)S(1)} all-to-all(bf16[16,16,2560]{2,1,0:T(8,128)(2,1)S(1)} %broadcast_in_dim.59), channel_id=1, replica_groups=mesh['yh'=4,'yl'=2,'core'=2,'x'=4,'zh'=4,'zl'=2] {'x','yl','zl'}, dimensions={0} | all-to-all | bytes 2621440 | tf_op jit(solution)/shard_map/all_to_all | solution.py:40
  111.8 7.7 %collective-permute-start.2 = (bf16[256,2560]{1,0:T(8,128)(2,1)S(1)}, bf16[256,2560]{1,0:T(8,128)(2,1)S(1)}, u32[]{:S(2)}, u32[]{:S(2)}) collective-permute-start(bf16[256,2560]{1,0:T(8,128)(2,1)S(1)} %bitcast.19), channel_id=1, source_target_pairs={{0,32},{32,0},{1,33},{33,1},{2,34},{34,2},{3,35},{35,3},{4,36},{36... | collective-permute-start | bytes 3932168 | tf_op jit(solution)/shard_map/ppermute | solution.py:54
  119.6 2.5 %collective-permute-done.2.other_ref = bf16[256,2560]{1,0:T(8,128)(2,1)S(1)} collective-permute-done((bf16[256,2560]{1,0:T(8,128)(2,1)S(1)}, bf16[256,2560]{1,0:T(8,128)(2,1)S(1)}, u32[]{:S(2)}, u32[]{:S(2)}) %collective-permute-start.2) | collective-permute-done | bytes 1310752 | tf_op jit(solution)/shard_map/ppermute | solution.py:54
  122.0 14.9 %polar.1 = (bf16[512,1024]{1,0:T(8,128)(2,1)}, bf16[64,16,256]{2,1,0:T(8,128)(2,1)}) custom-call(s32[1]{0:T(128)} %bitcast.side_ref, bf16[256,2560]{1,0:T(8,128)(2,1)S(1)} %bitcast.20, bf16[256,2560]{1,0:T(8,128)(2,1)S(1)} %collective-permute-done.2.other_ref, bf16[512,1024]{1,0:T(8,128)(2,1)S(1)} %copy-done.1), custom_call_target="tpu_custom_call" | custom-call | flops 20000000000 | bytes 8000000 | tf_op jit(solution)/shard_map/polar/pallas_call | solution.py:220
  (18 shorter events, 0.2 us)
Async XLA Ops:
  0.6 0.7 copy-start
  2.1 23.4 %all-to-all-start = ((bf16[32,16,256]{2,1,0:T(8,128)(2,1)}), bf16[32,16,256]{2,1,0:T(8,128)(2,1)S(1)}, u32[]{:S(2)}, u32[]{:S(2)}) async-start(bf16[32,16,256]{2,1,0:T(8,128)(2,1)} %broadcast_in_dim.52), calls=%async_computation | async-start | bytes 524288 | tf_op jit(solution)/shard_map/all_to_all | solution.py:40
  15.8 15.3 %copy-start.1 = (bf16[512,1024]{1,0:T(8,128)(2,1)S(1)}, bf16[512,1024]{1,0:T(8,128)(2,1)}, u32[]{:S(2)}) copy-start(bf16[512,1024]{1,0:T(8,128)(2,1)} %emb_ref.5) | copy-start | bytes 3145732
  15.8 15.3 %copy-start.2 = (s32[512,64]{0,1:T(8,128)S(1)}, s32[512,64]{0,1:T(8,128)}, u32[]{:S(2)}) copy-start(s32[512,64]{0,1:T(8,128)} %param.6) | copy-start | bytes 393220
  25.5 8.6 %collective-permute-start = (bf16[512,256]{1,0:T(8,128)(2,1)S(1)}, bf16[512,256]{1,0:T(8,128)(2,1)S(1)}, u32[]{:S(2)}, u32[]{:S(2)}) collective-permute-start(bf16[512,256]{1,0:T(8,128)(2,1)S(1)} %bitcast.21), channel_id=1, source_target_pairs={{0,32},{32,0},{1,33},{33,1},{2,34},{34,2},{3,35},{35,3},{4,36},{36... | collective-permute-start | bytes 786440 | tf_op jit(solution)/shard_map/ppermute | solution.py:54
  31.1 1.1 copy-start.3
  34.0 5.0 %collective-permute-start.1 = (bf16[256,2688]{1,0:T(8,128)(2,1)S(1)}, bf16[256,2688]{1,0:T(8,128)(2,1)S(1)}, u32[]{:S(2)}, u32[]{:S(2)}) collective-permute-start(bf16[256,2688]{1,0:T(8,128)(2,1)S(1)} %crosses.2), channel_id=1, source_target_pairs={{0,32},{32,0},{1,33},{33,1},{2,34},{34,2},{3,35},{35,3},{4,36},{36... | collective-permute-start | bytes 4128776 | tf_op jit(solution)/shard_map/ppermute | solution.py:54
  78.9 12.0 %all-to-all-start.3 = ((bf16[4,16,2688]{2,1,0:T(8,128)(2,1)}), bf16[4,16,2688]{2,1,0:T(8,128)(2,1)S(1)}, u32[]{:S(2)}, u32[]{:S(2)}) async-start(bf16[4,16,2688]{2,1,0:T(8,128)(2,1)} %broadcast_in_dim.54), calls=%async_computation.3 | async-start | bytes 688128 | tf_op jit(solution)/shard_map/all_to_all | solution.py:40
  111.8 10.2 %collective-permute-start.2 = (bf16[256,2560]{1,0:T(8,128)(2,1)S(1)}, bf16[256,2560]{1,0:T(8,128)(2,1)S(1)}, u32[]{:S(2)}, u32[]{:S(2)}) collective-permute-start(bf16[256,2560]{1,0:T(8,128)(2,1)S(1)} %bitcast.19), channel_id=1, source_target_pairs={{0,32},{32,0},{1,33},{33,1},{2,34},{34,2},{3,35},{35,3},{4,36},{36... | collective-permute-start | bytes 3932168 | tf_op jit(solution)/shard_map/ppermute | solution.py:54

commit v7 on v6

--- a/solution.py
+++ b/solution.py
@@ -36,18 +36,32 @@
     return lax.dot_general(a, b, dims, preferred_element_type=F32)
 
 
-def gather(value, axes, peers):
-    return lax.all_to_all(
-        jnp.broadcast_to(value[None], (peers,) + value.shape), axes, 0, 0, tiled=True
-    )
+def far_groups(turn):
+    groups = []
+    for yl in range(2):
+        for core in range(2):
+            for x in range(4):
+                for other in range(4):
+                    for zl in range(2):
+                        along_y = core == turn
+                        places = [(i, other) if along_y else (other, i) for i in range(4)]
+                        groups.append(
+                            [((((yh * 2 + yl) * 2 + core) * 4 + x) * 4 + zh) * 2 + zl for yh, zh in places]
+                        )
+    return groups
+
+
+def gather(value, axes, peers, groups=None):
+    spreadout = jnp.broadcast_to(value[None], (peers,) + value.shape)
+    return lax.all_to_all(spreadout, axes, 0, 0, axis_index_groups=groups, tiled=True)
 
 
 def spread(parts, axes):
     return jnp.sum(lax.all_to_all(parts, axes, 0, 0, tiled=True).astype(F32), axis=0)
 
 
-def total(value, axes, peers):
-    return jnp.sum(gather(value, axes, peers).astype(F32), axis=0)
+def total(value, turn):
+    return jnp.sum(gather(value, AXES, 4, far_groups(turn)).astype(F32), axis=0)
 
 
 def swap(value):
@@ -114,7 +128,7 @@
             pltpu.VMEM((SUBS, TOK), jnp.int32),
             pltpu.SemaphoreType.DMA((3,)),
         ],
-        compiler_params=pltpu.CompilerParams(vmem_limit_bytes=60 * MIB),
+        compiler_params=pltpu.CompilerParams(vmem_limit_bytes=53 * MIB),
         cost_estimate=pl.CostEstimate(flops=8 * 10**9, bytes_accessed=4 * 10**6, transcendentals=0),
         name="tables",
     )(embeddings, rotation, codes)
@@ -263,13 +277,13 @@
     digits = jnp.concatenate([counted - LOW * rest, rest - LOW * high, high], axis=0)
     digits = jnp.pad(digits.reshape(12, 128), ((0, 4), (0, 0)))
     packed = jnp.concatenate([boxed[:, :BACK], digits], axis=1).astype(BF16)
-    packed = total(packed, "yh", 4).astype(BF16)
-    summed = total(packed, "zh", 4)
-    summed, mine_book = lax.optimization_barrier((summed, mine_book))
+    packed = total(packed, 0).astype(BF16)
+    packed, box = lax.optimization_barrier((packed, lax.axis_index(BOX)))
+    summed = total(packed, 1)
+    summed, mine_book, box = lax.optimization_barrier((summed, mine_book, box))
 
     counted = summed[:12, BACK:].reshape(3, 2, K)
     counted = counted[0] + LOW * counted[1] + (LOW * LOW) * counted[2]
-    box = lax.axis_index(BOX)
     fresh = []
     for half in range(2):
         old = lax.dynamic_slice_in_dim(mine_book, box * DS + MINE * half, DS, 0).astype(F32)

time: 137 us -> 134 us (0.978)
  blocking collectives: 59 us -> 55.3 us
    all_to_all x2, blocking collectives: 36.1 us -> 32.4 us  [gather(): lax.all_to_all(spreadout, axes, 0, 0, axis_index_groups=groups, tiled=True)]
where the time goes in v7:
time: 134 us
  blocking collectives  55.3 us (41%)
  starting transfers between devices  33.1 us (25%)
  Pallas kernels  26.3 us (20%)
  waiting for transfers between devices  14 us (10%)
  local copies, waits for them, and re-layouts  3.29 us (2%)
    all_to_all x2, blocking collectives, gather(): lax.all_to_all(spreadout, axes, 0, 0, axis_index_groups=groups, tiled=True)  32.4 us
    all_to_all x1, blocking collectives, spread(): lax.all_to_all(parts, axes, 0, 0, tiled=True).astype(F32)  22.9 us
    all_to_all x2, starting transfers between devices, gather(): lax.all_to_all(spreadout, axes, 0, 0, axis_index_groups=groups, tiled=True)  17.3 us
    ppermute x3, starting transfers between devices, swap(): return lax.ppermute(value, 'core', [(0, 1), (1, 0)])  15.8 us
    pallas_call x1, Pallas kernels, finish(): pl.pallas_call(polar_kernel, out_shape=(jax.ShapeDtypeStruct((TOK, D), BF...  14.9 us
    all_to_all x2, waiting for transfers between devices, gather(): lax.all_to_all(spreadout, axes, 0, 0, axis_index_groups=groups, tiled=True)  10.3 us
    pallas_call x1, Pallas kernels, tables(): pl.pallas_call(tables_kernel, out_shape=jax.ShapeDtypeStruct((2, MINE, 2...  7.76 us
    ppermute x3, waiting for transfers between devices, swap(): return lax.ppermute(value, 'core', [(0, 1), (1, 0)])  3.74 us
  transfers between devices with their start and end apart: 5, of which 4 were waited for; matrix products, arithmetic and copies ran while one was open for 0% of the time, Pallas kernels for 9%

profile of v7, /device:TPU:1, one launch (start us, length us, event | category | flops | bytes accessed | tf_op | source)
XLA Modules:
  0.0 133.6 jit_solution(13818858266190567649)
XLA Ops:
  0.6 0.0 copy-start
  0.7 0.7 copy-done
  1.4 0.7 broadcast_in_dim.52
  2.1 13.7 %all-to-all-start = ((bf16[32,16,256]{2,1,0:T(8,128)(2,1)}), bf16[32,16,256]{2,1,0:T(8,128)(2,1)S(1)}, u32[]{:S(2)}, u32[]{:S(2)}) async-start(bf16[32,16,256]{2,1,0:T(8,128)(2,1)} %broadcast_in_dim.52), calls=%async_computation | async-start | bytes 524288 | tf_op jit(solution)/shard_map/all_to_all | solution.py:56
  15.8 0.0 copy-start.2
  15.8 0.9 copy-done.2
  16.7 0.0 copy-start.1
  16.7 0.0 copy-start.3
  16.7 7.8 %tables.1.table_ref = bf16[2,256,640]{2,1,0:T(8,128)(2,1)S(1)} custom-call(bf16[512,1024]{1,0:T(8,128)(2,1)} %emb_ref.5, bf16[1024,1024]{1,0:T(8,128)(2,1)} %rot_hbm.1, s32[64,512]{1,0:T(8,128)S(1)} %bitcast.23), custom_call_target="tpu_custom_call" | custom-call | flops 8000000000 | bytes 4000000 | tf_op jit(solution)/shard_map/tables/pallas_call | solution.py:120
  24.5 1.0 all-to-all-done
  25.5 5.6 %collective-permute-start = (bf16[512,256]{1,0:T(8,128)(2,1)S(1)}, bf16[512,256]{1,0:T(8,128)(2,1)S(1)}, u32[]{:S(2)}, u32[]{:S(2)}) collective-permute-start(bf16[512,256]{1,0:T(8,128)(2,1)S(1)} %bitcast.21), channel_id=1, source_target_pairs={{0,32},{32,0},{1,33},{33,1},{2,34},{34,2},{3,35},{35,3},{4,36},{36... | collective-permute-start | bytes 786440 | tf_op jit(solution)/shard_map/ppermute | solution.py:68
  31.1 0.0 copy-done.1
  31.1 0.0 copy-done.3
  31.1 1.8 %crosses.2 = bf16[256,2688]{1,0:T(8,128)(2,1)S(1)} custom-call(s32[1]{0:T(128)} %bitcast.1.side_ref, bf16[512,1024]{1,0:T(8,128)(2,1)S(1)} %copy-done.1, s32[64,512]{1,0:T(8,128)S(1)} %bitcast.24, bf16[512,256]{1,0:T(8,128)(2,1)S(1)} %bitcast.22, bf16[2,256,640]{2,1,0:T(8,128)(2,1)S(1)} %tables.1.table_ref), custom_call_target="tpu_custom_call" | custom-call | flops 4000000000 | bytes 4000000 | tf_op jit(solution)/shard_map/crosses/pallas_call | solution.py:153
  33.0 0.0 collective-permute-done.book_ref
  33.0 1.9 %collective-permute-start.1 = (bf16[256,2688]{1,0:T(8,128)(2,1)S(1)}, bf16[256,2688]{1,0:T(8,128)(2,1)S(1)}, u32[]{:S(2)}, u32[]{:S(2)}) collective-permute-start(bf16[256,2688]{1,0:T(8,128)(2,1)S(1)} %crosses.2), channel_id=1, source_target_pairs={{0,32},{32,0},{1,33},{33,1},{2,34},{34,2},{3,35},{35,3},{4,36},{36... | collective-permute-start | bytes 4128776 | tf_op jit(solution)/shard_map/ppermute | solution.py:68
  34.9 1.8 %crosses.3 = bf16[256,2688]{1,0:T(8,128)(2,1)S(1)} custom-call(s32[1]{0:T(128)} %bitcast.side_ref, bf16[512,1024]{1,0:T(8,128)(2,1)S(1)} %copy-done.1, s32[64,512]{1,0:T(8,128)S(1)} %bitcast.25, bf16[512,256]{1,0:T(8,128)(2,1)S(1)} %collective-permute-done.book_ref, bf16[2,256,640]{2,1,0:T(8,128)(2,1)S(1)} %tables.1.table_ref), custom_call_target="tpu_custom_call" | custom-call | flops 4000000000 | bytes 4000000 | tf_op jit(solution)/shard_map/crosses/pallas_call | solution.py:153
  36.7 1.3 collective-permute-done.1
  38.0 0.3 add_convert_fusion
  38.3 22.9 %all_to_all.25 = bf16[16,16,2688]{2,1,0:T(8,128)(2,1)S(1)} all-to-all(bf16[16,16,2688]{2,1,0:T(8,128)(2,1)S(1)} %bitcast.26), channel_id=1, replica_groups=mesh['yh'=4,'yl'=2,'core'=2,'x'=4,'zh'=4,'zl'=2] {'x','yl','zl'}, dimensions={0} | all-to-all | bytes 2752512 | tf_op jit(solution)/shard_map/all_to_all | solution.py:60
  61.2 0.2 convert_reduce_fusion
  61.5 0.8 broadcast_in_dim.53
  62.3 3.6 %all-to-all-start.2 = ((bf16[4,16,2688]{2,1,0:T(8,128)(2,1)}), bf16[4,16,2688]{2,1,0:T(8,128)(2,1)S(1)}, u32[]{:S(2)}, u32[]{:S(2)}) async-start(bf16[4,16,2688]{2,1,0:T(8,128)(2,1)} %broadcast_in_dim.53), calls=%async_computation.2 | async-start | bytes 688128 | tf_op jit(solution)/shard_map/all_to_all | solution.py:56
  65.8 9.3 %all-to-all-done.2 = bf16[4,16,2688]{2,1,0:T(8,128)(2,1)S(1)} async-done(((bf16[4,16,2688]{2,1,0:T(8,128)(2,1)}), bf16[4,16,2688]{2,1,0:T(8,128)(2,1)S(1)}, u32[]{:S(2)}, u32[]{:S(2)}) %all-to-all-start.2) | async-done | bytes 344096 | tf_op jit(solution)/shard_map/all_to_all | solution.py:56
  75.1 0.1 reduce_sum.31
  75.2 15.1 %all_to_all.26 = bf16[4,16,2688]{2,1,0:T(8,128)(2,1)S(1)} all-to-all(bf16[4,16,2688]{2,1,0:T(8,128)(2,1)S(1)} %broadcast_in_dim.54), channel_id=1, replica_groups={{0,2,4,6},{1,3,5,7},{128,130,132,134},{129,131,133,135},{256,258,260,26..., dimensions={0} | all-to-all | bytes 688128 | tf_op jit(solution)/shard_map/all_to_all | solution.py:56
  90.4 0.1 broadcast_in_dim.59
  90.6 17.4 %all_to_all.27 = bf16[16,16,2560]{2,1,0:T(8,128)(2,1)S(1)} all-to-all(bf16[16,16,2560]{2,1,0:T(8,128)(2,1)S(1)} %broadcast_in_dim.59), channel_id=1, replica_groups=mesh['yh'=4,'yl'=2,'core'=2,'x'=4,'zh'=4,'zl'=2] {'x','yl','zl'}, dimensions={0} | all-to-all | bytes 2621440 | tf_op jit(solution)/shard_map/all_to_all | solution.py:56
  107.9 8.3 %collective-permute-start.2 = (bf16[256,2560]{1,0:T(8,128)(2,1)S(1)}, bf16[256,2560]{1,0:T(8,128)(2,1)S(1)}, u32[]{:S(2)}, u32[]{:S(2)}) collective-permute-start(bf16[256,2560]{1,0:T(8,128)(2,1)S(1)} %bitcast.19), channel_id=1, source_target_pairs={{0,32},{32,0},{1,33},{33,1},{2,34},{34,2},{3,35},{35,3},{4,36},{36... | collective-permute-start | bytes 3932168 | tf_op jit(solution)/shard_map/ppermute | solution.py:68
  116.2 2.5 %collective-permute-done.2.other_ref = bf16[256,2560]{1,0:T(8,128)(2,1)S(1)} collective-permute-done((bf16[256,2560]{1,0:T(8,128)(2,1)S(1)}, bf16[256,2560]{1,0:T(8,128)(2,1)S(1)}, u32[]{:S(2)}, u32[]{:S(2)}) %collective-permute-start.2) | collective-permute-done | bytes 1310752 | tf_op jit(solution)/shard_map/ppermute | solution.py:68
  118.7 14.9 %polar.1 = (bf16[512,1024]{1,0:T(8,128)(2,1)}, bf16[64,16,256]{2,1,0:T(8,128)(2,1)}) custom-call(s32[1]{0:T(128)} %bitcast.side_ref, bf16[256,2560]{1,0:T(8,128)(2,1)S(1)} %bitcast.20, bf16[256,2560]{1,0:T(8,128)(2,1)S(1)} %collective-permute-done.2.other_ref, bf16[512,1024]{1,0:T(8,128)(2,1)S(1)} %copy-done.1), custom_call_target="tpu_custom_call" | custom-call | flops 20000000000 | bytes 8000000 | tf_op jit(solution)/shard_map/polar/pallas_call | solution.py:234
  (18 shorter events, 0.2 us)
Async XLA Ops:
  0.6 0.7 copy-start
  2.1 23.4 %all-to-all-start = ((bf16[32,16,256]{2,1,0:T(8,128)(2,1)}), bf16[32,16,256]{2,1,0:T(8,128)(2,1)S(1)}, u32[]{:S(2)}, u32[]{:S(2)}) async-start(bf16[32,16,256]{2,1,0:T(8,128)(2,1)} %broadcast_in_dim.52), calls=%async_computation | async-start | bytes 524288 | tf_op jit(solution)/shard_map/all_to_all | solution.py:56
  15.8 0.9 copy-start.2
  16.7 14.4 %copy-start.1 = (bf16[512,1024]{1,0:T(8,128)(2,1)S(1)}, bf16[512,1024]{1,0:T(8,128)(2,1)}, u32[]{:S(2)}) copy-start(bf16[512,1024]{1,0:T(8,128)(2,1)} %emb_ref.5) | copy-start | bytes 3145732
  16.7 14.4 %copy-start.3 = (s32[512,64]{0,1:T(8,128)S(1)}, s32[512,64]{0,1:T(8,128)}, u32[]{:S(2)}) copy-start(s32[512,64]{0,1:T(8,128)} %param.6) | copy-start | bytes 393220
  25.5 7.5 %collective-permute-start = (bf16[512,256]{1,0:T(8,128)(2,1)S(1)}, bf16[512,256]{1,0:T(8,128)(2,1)S(1)}, u32[]{:S(2)}, u32[]{:S(2)}) collective-permute-start(bf16[512,256]{1,0:T(8,128)(2,1)S(1)} %bitcast.21), channel_id=1, source_target_pairs={{0,32},{32,0},{1,33},{33,1},{2,34},{34,2},{3,35},{35,3},{4,36},{36... | collective-permute-start | bytes 786440 | tf_op jit(solution)/shard_map/ppermute | solution.py:68
  33.0 5.0 %collective-permute-start.1 = (bf16[256,2688]{1,0:T(8,128)(2,1)S(1)}, bf16[256,2688]{1,0:T(8,128)(2,1)S(1)}, u32[]{:S(2)}, u32[]{:S(2)}) collective-permute-start(bf16[256,2688]{1,0:T(8,128)(2,1)S(1)} %crosses.2), channel_id=1, source_target_pairs={{0,32},{32,0},{1,33},{33,1},{2,34},{34,2},{3,35},{35,3},{4,36},{36... | collective-permute-start | bytes 4128776 | tf_op jit(solution)/shard_map/ppermute | solution.py:68
  62.3 12.8 %all-to-all-start.2 = ((bf16[4,16,2688]{2,1,0:T(8,128)(2,1)}), bf16[4,16,2688]{2,1,0:T(8,128)(2,1)S(1)}, u32[]{:S(2)}, u32[]{:S(2)}) async-start(bf16[4,16,2688]{2,1,0:T(8,128)(2,1)} %broadcast_in_dim.53), calls=%async_computation.2 | async-start | bytes 688128 | tf_op jit(solution)/shard_map/all_to_all | solution.py:56
  107.9 10.7 %collective-permute-start.2 = (bf16[256,2560]{1,0:T(8,128)(2,1)S(1)}, bf16[256,2560]{1,0:T(8,128)(2,1)S(1)}, u32[]{:S(2)}, u32[]{:S(2)}) collective-permute-start(bf16[256,2560]{1,0:T(8,128)(2,1)S(1)} %bitcast.19), channel_id=1, source_target_pairs={{0,32},{32,0},{1,33},{33,1},{2,34},{34,2},{3,35},{35,3},{4,36},{36... | collective-permute-start | bytes 3932168 | tf_op jit(solution)/shard_map/ppermute | solution.py:68

commit v8 on v7

--- a/solution.py
+++ b/solution.py
@@ -189,7 +189,10 @@
     symmetric(lambda at, right: dot(g2_ref[at, :], k_ref[:, right]), rest)
 
 
-def polar_kernel(side_ref, mine_ref, other_ref, emb_ref, out_ref, book_ref, y_ref, z_ref, g_ref, g2_ref, k_ref, w_ref, full_ref):
+def polar_kernel(
+    side_ref, mine_ref, other_ref, emb_ref, out_hbm, book_hbm,
+    out_ref, book_ref, y_ref, z_ref, g_ref, g2_ref, k_ref, w_ref, full_ref, sems,
+):
     side = side_ref[0]
     for rows_ref, at in ((mine_ref, side), (other_ref, 1 - side)):
         for q in range(HALF):
@@ -198,6 +201,9 @@
             y_ref[pl.ds(pl.multiple_of((2 * q + at) * DS, DS), DS), :] = rows_ref[here, left : left + D]
             left = 2 * D + (q // QUARTER) * K
             book_ref[2 * q + at] = rows_ref[here, left : left + K]
+
+    copies = [pltpu.make_async_copy(book_ref, book_hbm, sems.at[0])]
+    copies[0].start()
 
     squares = 0.0
     for i in range(PARTS):
@@ -227,7 +233,15 @@
     )
     turned = dot(emb_ref[...], z_ref[...], NT)
     two_steps(g_ref, g2_ref, k_ref, w_ref)
-    out_ref[...] = (2.25 * turned + dot(turned.astype(BF16), w_ref[...])).astype(BF16)
+    for i in range(2):
+        at = slice(i * MINE, (i + 1) * MINE)
+        part = 2.25 * turned[at] + dot(turned[at].astype(BF16), w_ref[...])
+        out_ref[at, :] = part.astype(BF16)
+        rows = pl.ds(i * MINE, MINE)
+        copies.append(pltpu.make_async_copy(out_ref.at[rows], out_hbm.at[rows], sems.at[1 + i]))
+        copies[-1].start()
+    for copy in copies:
+        copy.wait()
 
 
 def finish(side, mine, other, embeddings):
@@ -238,8 +252,10 @@
             jax.ShapeDtypeStruct((SUBS, DS, K), BF16),
         ),
         in_specs=[SMEM] + [VMEM] * 3,
-        out_specs=(VMEM,) * 2,
+        out_specs=(pl.BlockSpec(memory_space=pl.ANY),) * 2,
         scratch_shapes=[
+            pltpu.VMEM((TOK, D), BF16),
+            pltpu.VMEM((SUBS, DS, K), BF16),
             pltpu.VMEM((D, D), BF16),
             pltpu.VMEM((D, D), BF16),
             pltpu.VMEM((D, D), BF16),
@@ -247,8 +263,9 @@
             pltpu.VMEM((D, D), BF16),
             pltpu.VMEM((D, D), BF16),
             pltpu.VMEM((D, D), F32),
+            pltpu.SemaphoreType.DMA((3,)),
         ],
-        compiler_params=pltpu.CompilerParams(vmem_limit_bytes=32 * MIB),
+        compiler_params=pltpu.CompilerParams(vmem_limit_bytes=36 * MIB),
         cost_estimate=pl.CostEstimate(flops=20 * 10**9, bytes_accessed=8 * 10**6, transcendentals=0),
         name="polar",
     )(side, mine, other, embeddings)
@@ -261,6 +278,7 @@
 
     theirs = lax.dynamic_index_in_dim(codebook, 1 - core, 0, keepdims=False)
     other_book = gather(theirs, ROW, HALF).reshape(HALF * DS, K)
+    other_book, box = lax.optimization_barrier((other_book, lax.axis_index(BOX)))
     table = tables(embeddings, rotation, codes)
     mine_book = swap(other_book)
     sent = crosses(other, embeddings, codes, other_book, table)
@@ -278,7 +296,6 @@
     digits = jnp.pad(digits.reshape(12, 128), ((0, 4), (0, 0)))
     packed = jnp.concatenate([boxed[:, :BACK], digits], axis=1).astype(BF16)
     packed = total(packed, 0).astype(BF16)
-    packed, box = lax.optimization_barrier((packed, lax.axis_index(BOX)))
     summed = total(packed, 1)
     summed, mine_book, box = lax.optimization_barrier((summed, mine_book, box))
 

time: 134 us -> 134 us (level)
  blocking collectives: 55.3 us -> 67.9 us
  waiting for transfers between devices: 14 us -> 4.74 us
  starting transfers between devices: 33.1 us -> 30.2 us
    all_to_all x2 -> x3, blocking collectives: 32.4 us -> 45 us  [gather(): lax.all_to_all(spreadout, axes, 0, 0, axis_index_groups=groups, tiled=True)]
    all_to_all x2 -> x1, waiting for transfers between devices: 10.3 us -> 1 us  [gather(): lax.all_to_all(spreadout, axes, 0, 0, axis_index_groups=groups, tiled=True)]
    all_to_all x2 -> x1, starting transfers between devices: 17.3 us -> 13.7 us  [gather(): lax.all_to_all(spreadout, axes, 0, 0, axis_index_groups=groups, tiled=True)]
  transfers between devices with their start and end apart: 5 -> 4, of which waited for: 4 -> 3; matrix products, arithmetic and copies ran while one was open for 0% -> 0% of each run, Pallas kernels for 9% -> 9%
where the time goes in v8:
time: 134 us; the launch traced here: 133 us
  blocking collectives  67.9 us (51%)
  starting transfers between devices  30.2 us (23%)
  Pallas kernels  26 us (19%)
  waiting for transfers between devices  4.74 us (4%)
  local copies, waits for them, and re-layouts  2.56 us (2%)
    all_to_all x3, blocking collectives, gather(): lax.all_to_all(spreadout, axes, 0, 0, axis_index_groups=groups, tiled=True)  45 us
    all_to_all x1, blocking collectives, spread(): lax.all_to_all(parts, axes, 0, 0, tiled=True).astype(F32)  22.9 us
    ppermute x3, starting transfers between devices, swap(): return lax.ppermute(value, 'core', [(0, 1), (1, 0)])  16.5 us
    pallas_call x1, Pallas kernels, finish(): pl.pallas_call(polar_kernel, out_shape=(jax.ShapeDtypeStruct((TOK, D), BF...  14.6 us
    all_to_all x1, starting transfers between devices, gather(): lax.all_to_all(spreadout, axes, 0, 0, axis_index_groups=groups, tiled=True)  13.7 us
    pallas_call x1, Pallas kernels, tables(): pl.pallas_call(tables_kernel, out_shape=jax.ShapeDtypeStruct((2, MINE, 2...  7.76 us
    ppermute x3, waiting for transfers between devices, swap(): return lax.ppermute(value, 'core', [(0, 1), (1, 0)])  3.74 us
    pallas_call x2, Pallas kernels, crosses(): pl.pallas_call(cross_kernel, out_shape=jax.ShapeDtypeStruct((MINE, WIDE),...  3.61 us
  transfers between devices with their start and end apart: 4, of which 3 were waited for; matrix products, arithmetic and copies ran while one was open for 0% of the time, Pallas kernels for 9%

profile of v8, /device:TPU:1, one launch (start us, length us, event | category | flops | bytes accessed | tf_op | source)
XLA Modules:
  0.0 133.1 jit_solution(12104222459009819105)
XLA Ops:
  0.6 0.0 copy-start
  0.7 0.7 copy-done
  1.4 0.7 broadcast_in_dim.52
  2.1 13.7 %all-to-all-start = ((bf16[32,16,256]{2,1,0:T(8,128)(2,1)}), bf16[32,16,256]{2,1,0:T(8,128)(2,1)S(1)}, u32[]{:S(2)}, u32[]{:S(2)}) async-start(bf16[32,16,256]{2,1,0:T(8,128)(2,1)} %broadcast_in_dim.52), calls=%async_computation | async-start | bytes 524288 | tf_op jit(solution)/shard_map/all_to_all | solution.py:56
  15.8 0.0 copy-start.2
  15.8 0.9 copy-done.2
  16.7 0.0 copy-start.1
  16.7 0.0 copy-start.3
  16.7 7.8 %tables.1.table_ref = bf16[2,256,640]{2,1,0:T(8,128)(2,1)S(1)} custom-call(bf16[512,1024]{1,0:T(8,128)(2,1)} %emb_ref.5, bf16[1024,1024]{1,0:T(8,128)(2,1)} %rot_hbm.1, s32[64,512]{1,0:T(8,128)S(1)} %bitcast.23), custom_call_target="tpu_custom_call" | custom-call | flops 8000000000 | bytes 4000000 | tf_op jit(solution)/shard_map/tables/pallas_call | solution.py:120
  24.5 1.0 all-to-all-done
  25.5 5.6 %collective-permute-start = (bf16[512,256]{1,0:T(8,128)(2,1)S(1)}, bf16[512,256]{1,0:T(8,128)(2,1)S(1)}, u32[]{:S(2)}, u32[]{:S(2)}) collective-permute-start(bf16[512,256]{1,0:T(8,128)(2,1)S(1)} %bitcast.21), channel_id=1, source_target_pairs={{0,32},{32,0},{1,33},{33,1},{2,34},{34,2},{3,35},{35,3},{4,36},{36... | collective-permute-start | bytes 786440 | tf_op jit(solution)/shard_map/ppermute | solution.py:68
  31.1 0.0 copy-done.1
  31.1 0.0 copy-done.3
  31.1 1.8 %crosses.2 = bf16[256,2688]{1,0:T(8,128)(2,1)S(1)} custom-call(s32[1]{0:T(128)} %bitcast.1.side_ref, bf16[512,1024]{1,0:T(8,128)(2,1)S(1)} %copy-done.1, s32[64,512]{1,0:T(8,128)S(1)} %bitcast.24, bf16[512,256]{1,0:T(8,128)(2,1)S(1)} %bitcast.22, bf16[2,256,640]{2,1,0:T(8,128)(2,1)S(1)} %tables.1.table_ref), custom_call_target="tpu_custom_call" | custom-call | flops 4000000000 | bytes 4000000 | tf_op jit(solution)/shard_map/crosses/pallas_call | solution.py:153
  33.0 0.0 collective-permute-done.book_ref
  33.0 1.9 %collective-permute-start.1 = (bf16[256,2688]{1,0:T(8,128)(2,1)S(1)}, bf16[256,2688]{1,0:T(8,128)(2,1)S(1)}, u32[]{:S(2)}, u32[]{:S(2)}) collective-permute-start(bf16[256,2688]{1,0:T(8,128)(2,1)S(1)} %crosses.2), channel_id=1, source_target_pairs={{0,32},{32,0},{1,33},{33,1},{2,34},{34,2},{3,35},{35,3},{4,36},{36... | collective-permute-start | bytes 4128776 | tf_op jit(solution)/shard_map/ppermute | solution.py:68
  34.9 1.8 %crosses.3 = bf16[256,2688]{1,0:T(8,128)(2,1)S(1)} custom-call(s32[1]{0:T(128)} %bitcast.side_ref, bf16[512,1024]{1,0:T(8,128)(2,1)S(1)} %copy-done.1, s32[64,512]{1,0:T(8,128)S(1)} %bitcast.25, bf16[512,256]{1,0:T(8,128)(2,1)S(1)} %collective-permute-done.book_ref, bf16[2,256,640]{2,1,0:T(8,128)(2,1)S(1)} %tables.1.table_ref), custom_call_target="tpu_custom_call" | custom-call | flops 4000000000 | bytes 4000000 | tf_op jit(solution)/shard_map/crosses/pallas_call | solution.py:153
  36.7 1.3 collective-permute-done.1
  38.0 0.3 add_convert_fusion
  38.3 22.9 %all_to_all.25 = bf16[16,16,2688]{2,1,0:T(8,128)(2,1)S(1)} all-to-all(bf16[16,16,2688]{2,1,0:T(8,128)(2,1)S(1)} %bitcast.26), channel_id=1, replica_groups=mesh['yh'=4,'yl'=2,'core'=2,'x'=4,'zh'=4,'zl'=2] {'x','yl','zl'}, dimensions={0} | all-to-all | bytes 2752512 | tf_op jit(solution)/shard_map/all_to_all | solution.py:60
  61.2 0.2 convert_reduce_fusion
  61.6 13.4 %all_to_all.26 = bf16[4,16,2688]{2,1,0:T(8,128)(2,1)S(1)} all-to-all(bf16[4,16,2688]{2,1,0:T(8,128)(2,1)S(1)} %broadcast_in_dim.53), channel_id=1, replica_groups={{0,128,256,384},{1,129,257,385},{2,130,258,386},{3,131,259,387},{4,132,..., dimensions={0} | all-to-all | bytes 688128 | tf_op jit(solution)/shard_map/all_to_all | solution.py:56
  74.9 0.1 reduce_sum.31
  75.0 15.1 %all_to_all.27 = bf16[4,16,2688]{2,1,0:T(8,128)(2,1)S(1)} all-to-all(bf16[4,16,2688]{2,1,0:T(8,128)(2,1)S(1)} %broadcast_in_dim.54), channel_id=1, replica_groups={{0,2,4,6},{1,3,5,7},{128,130,132,134},{129,131,133,135},{256,258,260,26..., dimensions={0} | all-to-all | bytes 688128 | tf_op jit(solution)/shard_map/all_to_all | solution.py:56
  90.2 0.1 broadcast_in_dim.59
  90.3 16.6 %all_to_all.28 = bf16[16,16,2560]{2,1,0:T(8,128)(2,1)S(1)} all-to-all(bf16[16,16,2560]{2,1,0:T(8,128)(2,1)S(1)} %broadcast_in_dim.59), channel_id=1, replica_groups=mesh['yh'=4,'yl'=2,'core'=2,'x'=4,'zh'=4,'zl'=2] {'x','yl','zl'}, dimensions={0} | all-to-all | bytes 2621440 | tf_op jit(solution)/shard_map/all_to_all | solution.py:56
  106.9 8.9 %collective-permute-start.2 = (bf16[256,2560]{1,0:T(8,128)(2,1)S(1)}, bf16[256,2560]{1,0:T(8,128)(2,1)S(1)}, u32[]{:S(2)}, u32[]{:S(2)}) collective-permute-start(bf16[256,2560]{1,0:T(8,128)(2,1)S(1)} %bitcast.19), channel_id=1, source_target_pairs={{0,32},{32,0},{1,33},{33,1},{2,34},{34,2},{3,35},{35,3},{4,36},{36... | collective-permute-start | bytes 3932168 | tf_op jit(solution)/shard_map/ppermute | solution.py:68
  115.9 2.5 %collective-permute-done.2.other_ref = bf16[256,2560]{1,0:T(8,128)(2,1)S(1)} collective-permute-done((bf16[256,2560]{1,0:T(8,128)(2,1)S(1)}, bf16[256,2560]{1,0:T(8,128)(2,1)S(1)}, u32[]{:S(2)}, u32[]{:S(2)}) %collective-permute-start.2) | collective-permute-done | bytes 1310752 | tf_op jit(solution)/shard_map/ppermute | solution.py:68
  118.3 14.6 %polar.1 = (bf16[512,1024]{1,0:T(8,128)(2,1)}, bf16[64,16,256]{2,1,0:T(8,128)(2,1)}) custom-call(s32[1]{0:T(128)} %bitcast.side_ref, bf16[256,2560]{1,0:T(8,128)(2,1)S(1)} %bitcast.20, bf16[256,2560]{1,0:T(8,128)(2,1)S(1)} %collective-permute-done.2.other_ref, bf16[512,1024]{1,0:T(8,128)(2,1)S(1)} %copy-done.1), custom_call_target="tpu_custom_call" | custom-call | flops 20000000000 | bytes 8000000 | tf_op jit(solution)/shard_map/polar/pallas_call | solution.py:248
  (19 shorter events, 0.2 us)
Async XLA Ops:
  0.6 0.7 copy-start
  2.1 23.4 %all-to-all-start = ((bf16[32,16,256]{2,1,0:T(8,128)(2,1)}), bf16[32,16,256]{2,1,0:T(8,128)(2,1)S(1)}, u32[]{:S(2)}, u32[]{:S(2)}) async-start(bf16[32,16,256]{2,1,0:T(8,128)(2,1)} %broadcast_in_dim.52), calls=%async_computation | async-start | bytes 524288 | tf_op jit(solution)/shard_map/all_to_all | solution.py:56
  15.8 0.9 copy-start.2
  16.7 14.4 %copy-start.1 = (bf16[512,1024]{1,0:T(8,128)(2,1)S(1)}, bf16[512,1024]{1,0:T(8,128)(2,1)}, u32[]{:S(2)}) copy-start(bf16[512,1024]{1,0:T(8,128)(2,1)} %emb_ref.5) | copy-start | bytes 3145732
  16.7 14.4 %copy-start.3 = (s32[512,64]{0,1:T(8,128)S(1)}, s32[512,64]{0,1:T(8,128)}, u32[]{:S(2)}) copy-start(s32[512,64]{0,1:T(8,128)} %param.6) | copy-start | bytes 393220
  25.5 7.5 %collective-permute-start = (bf16[512,256]{1,0:T(8,128)(2,1)S(1)}, bf16[512,256]{1,0:T(8,128)(2,1)S(1)}, u32[]{:S(2)}, u32[]{:S(2)}) collective-permute-start(bf16[512,256]{1,0:T(8,128)(2,1)S(1)} %bitcast.21), channel_id=1, source_target_pairs={{0,32},{32,0},{1,33},{33,1},{2,34},{34,2},{3,35},{35,3},{4,36},{36... | collective-permute-start | bytes 786440 | tf_op jit(solution)/shard_map/ppermute | solution.py:68
  33.0 5.0 %collective-permute-start.1 = (bf16[256,2688]{1,0:T(8,128)(2,1)S(1)}, bf16[256,2688]{1,0:T(8,128)(2,1)S(1)}, u32[]{:S(2)}, u32[]{:S(2)}) collective-permute-start(bf16[256,2688]{1,0:T(8,128)(2,1)S(1)} %crosses.2), channel_id=1, source_target_pairs={{0,32},{32,0},{1,33},{33,1},{2,34},{34,2},{3,35},{35,3},{4,36},{36... | collective-permute-start | bytes 4128776 | tf_op jit(solution)/shard_map/ppermute | solution.py:68
  106.9 11.4 %collective-permute-start.2 = (bf16[256,2560]{1,0:T(8,128)(2,1)S(1)}, bf16[256,2560]{1,0:T(8,128)(2,1)S(1)}, u32[]{:S(2)}, u32[]{:S(2)}) collective-permute-start(bf16[256,2560]{1,0:T(8,128)(2,1)S(1)} %bitcast.19), channel_id=1, source_target_pairs={{0,32},{32,0},{1,33},{33,1},{2,34},{34,2},{3,35},{35,3},{4,36},{36... | collective-permute-start | bytes 3932168 | tf_op jit(solution)/shard_map/ppermute | solution.py:68

commit v9 on v8

--- a/solution.py
+++ b/solution.py
@@ -43,7 +43,7 @@
             for x in range(4):
                 for other in range(4):
                     for zl in range(2):
-                        along_y = core == turn
+                        along_y = core != turn
                         places = [(i, other) if along_y else (other, i) for i in range(4)]
                         groups.append(
                             [((((yh * 2 + yl) * 2 + core) * 4 + x) * 4 + zh) * 2 + zl for yh, zh in places]
@@ -51,13 +51,30 @@
     return groups
 
 
+def box_groups():
+    groups = []
+    for core in range(2):
+        for y in range(core, 8, 2):
+            for z in range(core, 8, 2):
+                groups.append(
+                    [
+                        (((y + yl) % 8 * 2 + core) * 4 + x) * 8 + (z + zl) % 8
+                        for x in range(4)
+                        for yl in range(2)
+                        for zl in range(2)
+                    ]
+                )
+    return groups
+
+
 def gather(value, axes, peers, groups=None):
     spreadout = jnp.broadcast_to(value[None], (peers,) + value.shape)
     return lax.all_to_all(spreadout, axes, 0, 0, axis_index_groups=groups, tiled=True)
 
 
-def spread(parts, axes):
-    return jnp.sum(lax.all_to_all(parts, axes, 0, 0, tiled=True).astype(F32), axis=0)
+def spread(parts, axes, groups=None):
+    got = lax.all_to_all(parts, axes, 0, 0, axis_index_groups=groups, tiled=True)
+    return jnp.sum(got.astype(F32), axis=0)
 
 
 def total(value, turn):
@@ -278,7 +295,8 @@
 
     theirs = lax.dynamic_index_in_dim(codebook, 1 - core, 0, keepdims=False)
     other_book = gather(theirs, ROW, HALF).reshape(HALF * DS, K)
-    other_book, box = lax.optimization_barrier((other_book, lax.axis_index(BOX)))
+    box = lax.axis_index(BOX) ^ (3 * core)
+    other_book, box = lax.optimization_barrier((other_book, box))
     table = tables(embeddings, rotation, codes)
     mine_book = swap(other_book)
     sent = crosses(other, embeddings, codes, other_book, table)
@@ -287,7 +305,7 @@
     kept = crosses(mine, embeddings, codes, mine_book, table)
 
     pair = (got.astype(F32) + kept.astype(F32)).astype(BF16)
-    boxed = spread(pair.reshape(16, 16, WIDE), BOX)
+    boxed = spread(pair.reshape(16, 16, WIDE), AXES, box_groups())
     counted = boxed[:8, BACK:].reshape(2, 2, K)
     counted = counted[:, 0] + LOW * counted[:, 1]
     rest = jnp.floor(counted * (1.0 / LOW))
@@ -309,7 +327,7 @@
         fresh.append(jnp.where(count > 0, sums / jnp.maximum(count, 1.0), old))
     own = jnp.concatenate([summed[:, : 2 * D]] + fresh, axis=1).astype(BF16)
 
-    rows = gather(own, BOX, 16).reshape(MINE, BACK)
+    rows = gather(own, AXES, 16, box_groups()).reshape(MINE, BACK)
     rerotated, new_codebook = finish(mine, rows, swap(rows), embeddings)
     return (new_codebook, rerotated)
 

time: 134 us -> 137 us (1.022)
  blocking collectives: 67.9 us -> 77.4 us
  starting transfers between devices: 30.2 us -> 23.7 us
    all_to_all x3, blocking collectives: 45 us -> 53.5 us  [gather(): lax.all_to_all(spreadout, axes, 0, 0, axis_index_groups=groups, tiled=True)]
    ppermute x3, starting transfers between devices: 16.5 us -> 10 us  [swap(): return lax.ppermute(value, 'core', [(0, 1), (1, 0)])]
  transfers between devices with their start and end apart: 4 -> 4, of which waited for: 3 -> 3; matrix products, arithmetic and copies ran while one was open for 0% -> 0% of each run, Pallas kernels for 9% -> 8%
where the time goes in v9:
time: 137 us; the launch traced here: 136 us
  blocking collectives  77.4 us (56%)
  Pallas kernels  26 us (19%)
  starting transfers between devices  23.7 us (17%)
  waiting for transfers between devices  4.74 us (3%)
  local copies, waits for them, and re-layouts  2.56 us (2%)
    all_to_all x3, blocking collectives, gather(): lax.all_to_all(spreadout, axes, 0, 0, axis_index_groups=groups, tiled=True)  53.5 us
    all_to_all x1, blocking collectives, spread(): lax.all_to_all(parts, axes, 0, 0, axis_index_groups=groups, tiled=True)  23.9 us
    pallas_call x1, Pallas kernels, finish(): pl.pallas_call(polar_kernel, out_shape=(jax.ShapeDtypeStruct((TOK, D), BF...  14.6 us
    all_to_all x1, starting transfers between devices, gather(): lax.all_to_all(spreadout, axes, 0, 0, axis_index_groups=groups, tiled=True)  13.7 us
    ppermute x3, starting transfers between devices, swap(): return lax.ppermute(value, 'core', [(0, 1), (1, 0)])  10 us
    pallas_call x1, Pallas kernels, tables(): pl.pallas_call(tables_kernel, out_shape=jax.ShapeDtypeStruct((2, MINE, 2...  7.76 us
    ppermute x3, waiting for transfers between devices, swap(): return lax.ppermute(value, 'core', [(0, 1), (1, 0)])  3.74 us
    pallas_call x2, Pallas kernels, crosses(): pl.pallas_call(cross_kernel, out_shape=jax.ShapeDtypeStruct((MINE, WIDE),...  3.61 us
  transfers between devices with their start and end apart: 4, of which 3 were waited for; matrix products, arithmetic and copies ran while one was open for 0% of the time, Pallas kernels for 8%

profile of v9, /device:TPU:1, one launch (start us, length us, event | category | flops | bytes accessed | tf_op | source)
XLA Modules:
  0.0 136.2 jit_solution(6268527091853294769)
XLA Ops:
  0.6 0.0 copy-start
  0.7 0.7 copy-done
  1.4 0.7 broadcast_in_dim.52
  2.1 13.7 %all-to-all-start = ((bf16[32,16,256]{2,1,0:T(8,128)(2,1)}), bf16[32,16,256]{2,1,0:T(8,128)(2,1)S(1)}, u32[]{:S(2)}, u32[]{:S(2)}) async-start(bf16[32,16,256]{2,1,0:T(8,128)(2,1)} %broadcast_in_dim.52), calls=%async_computation | async-start | bytes 524288 | tf_op jit(solution)/shard_map/all_to_all | solution.py:72
  15.8 0.0 copy-start.2
  15.8 0.9 copy-done.2
  16.7 0.0 copy-start.1
  16.7 0.0 copy-start.3
  16.7 7.8 %tables.1.table_ref = bf16[2,256,640]{2,1,0:T(8,128)(2,1)S(1)} custom-call(bf16[512,1024]{1,0:T(8,128)(2,1)} %emb_ref.5, bf16[1024,1024]{1,0:T(8,128)(2,1)} %rot_hbm.1, s32[64,512]{1,0:T(8,128)S(1)} %bitcast.23), custom_call_target="tpu_custom_call" | custom-call | flops 8000000000 | bytes 4000000 | tf_op jit(solution)/shard_map/tables/pallas_call | solution.py:137
  24.5 1.0 all-to-all-done
  25.5 5.6 %collective-permute-start = (bf16[512,256]{1,0:T(8,128)(2,1)S(1)}, bf16[512,256]{1,0:T(8,128)(2,1)S(1)}, u32[]{:S(2)}, u32[]{:S(2)}) collective-permute-start(bf16[512,256]{1,0:T(8,128)(2,1)S(1)} %bitcast.21), channel_id=1, source_target_pairs={{0,32},{32,0},{1,33},{33,1},{2,34},{34,2},{3,35},{35,3},{4,36},{36... | collective-permute-start | bytes 786440 | tf_op jit(solution)/shard_map/ppermute | solution.py:85
  31.1 0.0 copy-done.1
  31.1 0.0 copy-done.3
  31.1 1.8 %crosses.2 = bf16[256,2688]{1,0:T(8,128)(2,1)S(1)} custom-call(s32[1]{0:T(128)} %bitcast.1.side_ref, bf16[512,1024]{1,0:T(8,128)(2,1)S(1)} %copy-done.1, s32[64,512]{1,0:T(8,128)S(1)} %bitcast.24, bf16[512,256]{1,0:T(8,128)(2,1)S(1)} %bitcast.22, bf16[2,256,640]{2,1,0:T(8,128)(2,1)S(1)} %tables.1.table_ref), custom_call_target="tpu_custom_call" | custom-call | flops 4000000000 | bytes 4000000 | tf_op jit(solution)/shard_map/crosses/pallas_call | solution.py:170
  33.0 0.0 collective-permute-done.book_ref
  33.0 1.9 %collective-permute-start.1 = (bf16[256,2688]{1,0:T(8,128)(2,1)S(1)}, bf16[256,2688]{1,0:T(8,128)(2,1)S(1)}, u32[]{:S(2)}, u32[]{:S(2)}) collective-permute-start(bf16[256,2688]{1,0:T(8,128)(2,1)S(1)} %crosses.2), channel_id=1, source_target_pairs={{0,32},{32,0},{1,33},{33,1},{2,34},{34,2},{3,35},{35,3},{4,36},{36... | collective-permute-start | bytes 4128776 | tf_op jit(solution)/shard_map/ppermute | solution.py:85
  34.9 1.8 %crosses.3 = bf16[256,2688]{1,0:T(8,128)(2,1)S(1)} custom-call(s32[1]{0:T(128)} %bitcast.side_ref, bf16[512,1024]{1,0:T(8,128)(2,1)S(1)} %copy-done.1, s32[64,512]{1,0:T(8,128)S(1)} %bitcast.25, bf16[512,256]{1,0:T(8,128)(2,1)S(1)} %collective-permute-done.book_ref, bf16[2,256,640]{2,1,0:T(8,128)(2,1)S(1)} %tables.1.table_ref), custom_call_target="tpu_custom_call" | custom-call | flops 4000000000 | bytes 4000000 | tf_op jit(solution)/shard_map/crosses/pallas_call | solution.py:170
  36.7 1.3 collective-permute-done.1
  38.0 0.3 add_convert_fusion
  38.3 23.9 %all_to_all.25 = bf16[16,16,2688]{2,1,0:T(8,128)(2,1)S(1)} all-to-all(bf16[16,16,2688]{2,1,0:T(8,128)(2,1)S(1)} %bitcast.26), channel_id=1, replica_groups={{0,1,64,65,8,9,72,73,16,17,80,81,24,25,88,89},{2,3,66,67,10,11,74,75,18..., dimensions={0} | all-to-all | bytes 2752512 | tf_op jit(solution)/shard_map/all_to_all | solution.py:76
  62.3 0.2 convert_reduce_fusion
  62.6 15.0 %all_to_all.26 = bf16[4,16,2688]{2,1,0:T(8,128)(2,1)S(1)} all-to-all(bf16[4,16,2688]{2,1,0:T(8,128)(2,1)S(1)} %broadcast_in_dim.53), channel_id=1, replica_groups={{0,2,4,6},{1,3,5,7},{128,130,132,134},{129,131,133,135},{256,258,260,26..., dimensions={0} | all-to-all | bytes 688128 | tf_op jit(solution)/shard_map/all_to_all | solution.py:72
  77.6 0.1 reduce_sum.31
  77.7 13.5 %all_to_all.27 = bf16[4,16,2688]{2,1,0:T(8,128)(2,1)S(1)} all-to-all(bf16[4,16,2688]{2,1,0:T(8,128)(2,1)S(1)} %broadcast_in_dim.54), channel_id=1, replica_groups={{0,128,256,384},{1,129,257,385},{2,130,258,386},{3,131,259,387},{4,132,..., dimensions={0} | all-to-all | bytes 688128 | tf_op jit(solution)/shard_map/all_to_all | solution.py:72
  91.3 0.1 broadcast_in_dim.59
  91.4 25.0 %all_to_all.28 = bf16[16,16,2560]{2,1,0:T(8,128)(2,1)S(1)} all-to-all(bf16[16,16,2560]{2,1,0:T(8,128)(2,1)S(1)} %broadcast_in_dim.59), channel_id=1, replica_groups={{0,1,64,65,8,9,72,73,16,17,80,81,24,25,88,89},{2,3,66,67,10,11,74,75,18..., dimensions={0} | all-to-all | bytes 2621440 | tf_op jit(solution)/shard_map/all_to_all | solution.py:72
  116.4 2.5 %collective-permute-start.2 = (bf16[256,2560]{1,0:T(8,128)(2,1)S(1)}, bf16[256,2560]{1,0:T(8,128)(2,1)S(1)}, u32[]{:S(2)}, u32[]{:S(2)}) collective-permute-start(bf16[256,2560]{1,0:T(8,128)(2,1)S(1)} %bitcast.19), channel_id=1, source_target_pairs={{0,32},{32,0},{1,33},{33,1},{2,34},{34,2},{3,35},{35,3},{4,36},{36... | collective-permute-start | bytes 3932168 | tf_op jit(solution)/shard_map/ppermute | solution.py:85
  118.9 2.5 %collective-permute-done.2.other_ref = bf16[256,2560]{1,0:T(8,128)(2,1)S(1)} collective-permute-done((bf16[256,2560]{1,0:T(8,128)(2,1)S(1)}, bf16[256,2560]{1,0:T(8,128)(2,1)S(1)}, u32[]{:S(2)}, u32[]{:S(2)}) %collective-permute-start.2) | collective-permute-done | bytes 1310752 | tf_op jit(solution)/shard_map/ppermute | solution.py:85
  121.4 14.6 %polar.1 = (bf16[512,1024]{1,0:T(8,128)(2,1)}, bf16[64,16,256]{2,1,0:T(8,128)(2,1)}) custom-call(s32[1]{0:T(128)} %bitcast.side_ref, bf16[256,2560]{1,0:T(8,128)(2,1)S(1)} %bitcast.20, bf16[256,2560]{1,0:T(8,128)(2,1)S(1)} %collective-permute-done.2.other_ref, bf16[512,1024]{1,0:T(8,128)(2,1)S(1)} %copy-done.1), custom_call_target="tpu_custom_call" | custom-call | flops 20000000000 | bytes 8000000 | tf_op jit(solution)/shard_map/polar/pallas_call | solution.py:265
  (19 shorter events, 0.2 us)
Async XLA Ops:
  0.6 0.7 copy-start
  2.1 23.4 %all-to-all-start = ((bf16[32,16,256]{2,1,0:T(8,128)(2,1)}), bf16[32,16,256]{2,1,0:T(8,128)(2,1)S(1)}, u32[]{:S(2)}, u32[]{:S(2)}) async-start(bf16[32,16,256]{2,1,0:T(8,128)(2,1)} %broadcast_in_dim.52), calls=%async_computation | async-start | bytes 524288 | tf_op jit(solution)/shard_map/all_to_all | solution.py:72
  15.8 0.9 copy-start.2
  16.7 14.4 %copy-start.1 = (bf16[512,1024]{1,0:T(8,128)(2,1)S(1)}, bf16[512,1024]{1,0:T(8,128)(2,1)}, u32[]{:S(2)}) copy-start(bf16[512,1024]{1,0:T(8,128)(2,1)} %emb_ref.5) | copy-start | bytes 3145732
  16.7 14.4 %copy-start.3 = (s32[512,64]{0,1:T(8,128)S(1)}, s32[512,64]{0,1:T(8,128)}, u32[]{:S(2)}) copy-start(s32[512,64]{0,1:T(8,128)} %param.6) | copy-start | bytes 393220
  25.5 7.5 %collective-permute-start = (bf16[512,256]{1,0:T(8,128)(2,1)S(1)}, bf16[512,256]{1,0:T(8,128)(2,1)S(1)}, u32[]{:S(2)}, u32[]{:S(2)}) collective-permute-start(bf16[512,256]{1,0:T(8,128)(2,1)S(1)} %bitcast.21), channel_id=1, source_target_pairs={{0,32},{32,0},{1,33},{33,1},{2,34},{34,2},{3,35},{35,3},{4,36},{36... | collective-permute-start | bytes 786440 | tf_op jit(solution)/shard_map/ppermute | solution.py:85
  33.0 5.0 %collective-permute-start.1 = (bf16[256,2688]{1,0:T(8,128)(2,1)S(1)}, bf16[256,2688]{1,0:T(8,128)(2,1)S(1)}, u32[]{:S(2)}, u32[]{:S(2)}) collective-permute-start(bf16[256,2688]{1,0:T(8,128)(2,1)S(1)} %crosses.2), channel_id=1, source_target_pairs={{0,32},{32,0},{1,33},{33,1},{2,34},{34,2},{3,35},{35,3},{4,36},{36... | collective-permute-start | bytes 4128776 | tf_op jit(solution)/shard_map/ppermute | solution.py:85
  116.4 4.9 %collective-permute-start.2 = (bf16[256,2560]{1,0:T(8,128)(2,1)S(1)}, bf16[256,2560]{1,0:T(8,128)(2,1)S(1)}, u32[]{:S(2)}, u32[]{:S(2)}) collective-permute-start(bf16[256,2560]{1,0:T(8,128)(2,1)S(1)} %bitcast.19), channel_id=1, source_target_pairs={{0,32},{32,0},{1,33},{33,1},{2,34},{34,2},{3,35},{35,3},{4,36},{36... | collective-permute-start | bytes 3932168 | tf_op jit(solution)/shard_map/ppermute | solution.py:85

commit v10 on v9

--- a/solution.py
+++ b/solution.py
@@ -43,7 +43,7 @@
             for x in range(4):
                 for other in range(4):
                     for zl in range(2):
-                        along_y = core != turn
+                        along_y = core == turn
                         places = [(i, other) if along_y else (other, i) for i in range(4)]
                         groups.append(
                             [((((yh * 2 + yl) * 2 + core) * 4 + x) * 4 + zh) * 2 + zl for yh, zh in places]
@@ -213,7 +213,7 @@
     side = side_ref[0]
     for rows_ref, at in ((mine_ref, side), (other_ref, 1 - side)):
         for q in range(HALF):
-            here = pl.ds((q % QUARTER) * DS, DS)
+            here = pl.ds(pl.multiple_of(((q % QUARTER) ^ (3 * at)) * DS, DS), DS)
             left = (q // QUARTER) * D
             y_ref[pl.ds(pl.multiple_of((2 * q + at) * DS, DS), DS), :] = rows_ref[here, left : left + D]
             left = 2 * D + (q // QUARTER) * K
@@ -327,7 +327,7 @@
         fresh.append(jnp.where(count > 0, sums / jnp.maximum(count, 1.0), old))
     own = jnp.concatenate([summed[:, : 2 * D]] + fresh, axis=1).astype(BF16)
 
-    rows = gather(own, AXES, 16, box_groups()).reshape(MINE, BACK)
+    rows = gather(own, BOX, 16).reshape(MINE, BACK)
     rerotated, new_codebook = finish(mine, rows, swap(rows), embeddings)
     return (new_codebook, rerotated)
 

time: 137 us -> 134 us (0.978)
  blocking collectives: 77.4 us -> 70.5 us
  starting transfers between devices: 23.7 us -> 28.4 us
    all_to_all x3, blocking collectives: 53.5 us -> 46.5 us  [gather(): lax.all_to_all(spreadout, axes, 0, 0, axis_index_groups=groups, tiled=True)]
    ppermute x3, starting transfers between devices: 10 us -> 14.7 us  [swap(): return lax.ppermute(value, 'core', [(0, 1), (1, 0)])]
where the time goes in v10:
time: 134 us
  blocking collectives  70.5 us (53%)
  starting transfers between devices  28.4 us (21%)
  Pallas kernels  26 us (19%)
  waiting for transfers between devices  4.74 us (4%)
  local copies, waits for them, and re-layouts  2.56 us (2%)
    all_to_all x3, blocking collectives, gather(): lax.all_to_all(spreadout, axes, 0, 0, axis_index_groups=groups, tiled=True)  46.5 us
    all_to_all x1, blocking collectives, spread(): lax.all_to_all(parts, axes, 0, 0, axis_index_groups=groups, tiled=True)  23.9 us
    ppermute x3, starting transfers between devices, swap(): return lax.ppermute(value, 'core', [(0, 1), (1, 0)])  14.7 us
    pallas_call x1, Pallas kernels, finish(): pl.pallas_call(polar_kernel, out_shape=(jax.ShapeDtypeStruct((TOK, D), BF...  14.6 us
    all_to_all x1, starting transfers between devices, gather(): lax.all_to_all(spreadout, axes, 0, 0, axis_index_groups=groups, tiled=True)  13.7 us
    pallas_call x1, Pallas kernels, tables(): pl.pallas_call(tables_kernel, out_shape=jax.ShapeDtypeStruct((2, MINE, 2...  7.76 us
    ppermute x3, waiting for transfers between devices, swap(): return lax.ppermute(value, 'core', [(0, 1), (1, 0)])  3.74 us
    pallas_call x2, Pallas kernels, crosses(): pl.pallas_call(cross_kernel, out_shape=jax.ShapeDtypeStruct((MINE, WIDE),...  3.61 us
  transfers between devices with their start and end apart: 4, of which 3 were waited for; matrix products, arithmetic and copies ran while one was open for 0% of the time, Pallas kernels for 8%

profile of v10, /device:TPU:1, one launch (start us, length us, event | category | flops | bytes accessed | tf_op | source)
XLA Modules:
  0.0 133.9 jit_solution(2384421208448558111)
XLA Ops:
  0.6 0.0 copy-start
  0.7 0.7 copy-done
  1.4 0.7 broadcast_in_dim.52
  2.1 13.7 %all-to-all-start = ((bf16[32,16,256]{2,1,0:T(8,128)(2,1)}), bf16[32,16,256]{2,1,0:T(8,128)(2,1)S(1)}, u32[]{:S(2)}, u32[]{:S(2)}) async-start(bf16[32,16,256]{2,1,0:T(8,128)(2,1)} %broadcast_in_dim.52), calls=%async_computation | async-start | bytes 524288 | tf_op jit(solution)/shard_map/all_to_all | solution.py:72
  15.8 0.0 copy-start.2
  15.8 0.9 copy-done.2
  16.7 0.0 copy-start.1
  16.7 0.0 copy-start.3
  16.7 7.8 %tables.1.table_ref = bf16[2,256,640]{2,1,0:T(8,128)(2,1)S(1)} custom-call(bf16[512,1024]{1,0:T(8,128)(2,1)} %emb_ref.5, bf16[1024,1024]{1,0:T(8,128)(2,1)} %rot_hbm.1, s32[64,512]{1,0:T(8,128)S(1)} %bitcast.23), custom_call_target="tpu_custom_call" | custom-call | flops 8000000000 | bytes 4000000 | tf_op jit(solution)/shard_map/tables/pallas_call | solution.py:137
  24.5 1.0 all-to-all-done
  25.5 5.6 %collective-permute-start = (bf16[512,256]{1,0:T(8,128)(2,1)S(1)}, bf16[512,256]{1,0:T(8,128)(2,1)S(1)}, u32[]{:S(2)}, u32[]{:S(2)}) collective-permute-start(bf16[512,256]{1,0:T(8,128)(2,1)S(1)} %bitcast.21), channel_id=1, source_target_pairs={{0,32},{32,0},{1,33},{33,1},{2,34},{34,2},{3,35},{35,3},{4,36},{36... | collective-permute-start | bytes 786440 | tf_op jit(solution)/shard_map/ppermute | solution.py:85
  31.1 0.0 copy-done.1
  31.1 0.0 copy-done.3
  31.1 1.8 %crosses.2 = bf16[256,2688]{1,0:T(8,128)(2,1)S(1)} custom-call(s32[1]{0:T(128)} %bitcast.1.side_ref, bf16[512,1024]{1,0:T(8,128)(2,1)S(1)} %copy-done.1, s32[64,512]{1,0:T(8,128)S(1)} %bitcast.24, bf16[512,256]{1,0:T(8,128)(2,1)S(1)} %bitcast.22, bf16[2,256,640]{2,1,0:T(8,128)(2,1)S(1)} %tables.1.table_ref), custom_call_target="tpu_custom_call" | custom-call | flops 4000000000 | bytes 4000000 | tf_op jit(solution)/shard_map/crosses/pallas_call | solution.py:170
  33.0 0.0 collective-permute-done.book_ref
  33.0 1.9 %collective-permute-start.1 = (bf16[256,2688]{1,0:T(8,128)(2,1)S(1)}, bf16[256,2688]{1,0:T(8,128)(2,1)S(1)}, u32[]{:S(2)}, u32[]{:S(2)}) collective-permute-start(bf16[256,2688]{1,0:T(8,128)(2,1)S(1)} %crosses.2), channel_id=1, source_target_pairs={{0,32},{32,0},{1,33},{33,1},{2,34},{34,2},{3,35},{35,3},{4,36},{36... | collective-permute-start | bytes 4128776 | tf_op jit(solution)/shard_map/ppermute | solution.py:85
  34.9 1.8 %crosses.3 = bf16[256,2688]{1,0:T(8,128)(2,1)S(1)} custom-call(s32[1]{0:T(128)} %bitcast.side_ref, bf16[512,1024]{1,0:T(8,128)(2,1)S(1)} %copy-done.1, s32[64,512]{1,0:T(8,128)S(1)} %bitcast.25, bf16[512,256]{1,0:T(8,128)(2,1)S(1)} %collective-permute-done.book_ref, bf16[2,256,640]{2,1,0:T(8,128)(2,1)S(1)} %tables.1.table_ref), custom_call_target="tpu_custom_call" | custom-call | flops 4000000000 | bytes 4000000 | tf_op jit(solution)/shard_map/crosses/pallas_call | solution.py:170
  36.7 1.3 collective-permute-done.1
  38.0 0.3 add_convert_fusion
  38.3 23.9 %all_to_all.25 = bf16[16,16,2688]{2,1,0:T(8,128)(2,1)S(1)} all-to-all(bf16[16,16,2688]{2,1,0:T(8,128)(2,1)S(1)} %bitcast.26), channel_id=1, replica_groups={{0,1,64,65,8,9,72,73,16,17,80,81,24,25,88,89},{2,3,66,67,10,11,74,75,18..., dimensions={0} | all-to-all | bytes 2752512 | tf_op jit(solution)/shard_map/all_to_all | solution.py:76
  62.3 0.2 convert_reduce_fusion
  62.6 13.4 %all_to_all.26 = bf16[4,16,2688]{2,1,0:T(8,128)(2,1)S(1)} all-to-all(bf16[4,16,2688]{2,1,0:T(8,128)(2,1)S(1)} %broadcast_in_dim.53), channel_id=1, replica_groups={{0,128,256,384},{1,129,257,385},{2,130,258,386},{3,131,259,387},{4,132,..., dimensions={0} | all-to-all | bytes 688128 | tf_op jit(solution)/shard_map/all_to_all | solution.py:72
  76.0 0.1 reduce_sum.31
  76.1 15.1 %all_to_all.27 = bf16[4,16,2688]{2,1,0:T(8,128)(2,1)S(1)} all-to-all(bf16[4,16,2688]{2,1,0:T(8,128)(2,1)S(1)} %broadcast_in_dim.54), channel_id=1, replica_groups={{0,2,4,6},{1,3,5,7},{128,130,132,134},{129,131,133,135},{256,258,260,26..., dimensions={0} | all-to-all | bytes 688128 | tf_op jit(solution)/shard_map/all_to_all | solution.py:72
  91.4 0.1 broadcast_in_dim.59
  91.5 18.0 %all_to_all.28 = bf16[16,16,2560]{2,1,0:T(8,128)(2,1)S(1)} all-to-all(bf16[16,16,2560]{2,1,0:T(8,128)(2,1)S(1)} %broadcast_in_dim.59), channel_id=1, replica_groups=mesh['yh'=4,'yl'=2,'core'=2,'x'=4,'zh'=4,'zl'=2] {'x','yl','zl'}, dimensions={0} | all-to-all | bytes 2621440 | tf_op jit(solution)/shard_map/all_to_all | solution.py:72
  109.5 7.2 %collective-permute-start.2 = (bf16[256,2560]{1,0:T(8,128)(2,1)S(1)}, bf16[256,2560]{1,0:T(8,128)(2,1)S(1)}, u32[]{:S(2)}, u32[]{:S(2)}) collective-permute-start(bf16[256,2560]{1,0:T(8,128)(2,1)S(1)} %bitcast.19), channel_id=1, source_target_pairs={{0,32},{32,0},{1,33},{33,1},{2,34},{34,2},{3,35},{35,3},{4,36},{36... | collective-permute-start | bytes 3932168 | tf_op jit(solution)/shard_map/ppermute | solution.py:85
  116.7 2.5 %collective-permute-done.2.other_ref = bf16[256,2560]{1,0:T(8,128)(2,1)S(1)} collective-permute-done((bf16[256,2560]{1,0:T(8,128)(2,1)S(1)}, bf16[256,2560]{1,0:T(8,128)(2,1)S(1)}, u32[]{:S(2)}, u32[]{:S(2)}) %collective-permute-start.2) | collective-permute-done | bytes 1310752 | tf_op jit(solution)/shard_map/ppermute | solution.py:85
  119.2 14.6 %polar.1 = (bf16[512,1024]{1,0:T(8,128)(2,1)}, bf16[64,16,256]{2,1,0:T(8,128)(2,1)}) custom-call(s32[1]{0:T(128)} %bitcast.side_ref, bf16[256,2560]{1,0:T(8,128)(2,1)S(1)} %bitcast.20, bf16[256,2560]{1,0:T(8,128)(2,1)S(1)} %collective-permute-done.2.other_ref, bf16[512,1024]{1,0:T(8,128)(2,1)S(1)} %copy-done.1), custom_call_target="tpu_custom_call" | custom-call | flops 20000000000 | bytes 8000000 | tf_op jit(solution)/shard_map/polar/pallas_call | solution.py:265
  (19 shorter events, 0.2 us)
Async XLA Ops:
  0.6 0.7 copy-start
  2.1 23.4 %all-to-all-start = ((bf16[32,16,256]{2,1,0:T(8,128)(2,1)}), bf16[32,16,256]{2,1,0:T(8,128)(2,1)S(1)}, u32[]{:S(2)}, u32[]{:S(2)}) async-start(bf16[32,16,256]{2,1,0:T(8,128)(2,1)} %broadcast_in_dim.52), calls=%async_computation | async-start | bytes 524288 | tf_op jit(solution)/shard_map/all_to_all | solution.py:72
  15.8 0.9 copy-start.2
  16.7 14.4 %copy-start.1 = (bf16[512,1024]{1,0:T(8,128)(2,1)S(1)}, bf16[512,1024]{1,0:T(8,128)(2,1)}, u32[]{:S(2)}) copy-start(bf16[512,1024]{1,0:T(8,128)(2,1)} %emb_ref.5) | copy-start | bytes 3145732
  16.7 14.4 %copy-start.3 = (s32[512,64]{0,1:T(8,128)S(1)}, s32[512,64]{0,1:T(8,128)}, u32[]{:S(2)}) copy-start(s32[512,64]{0,1:T(8,128)} %param.6) | copy-start | bytes 393220
  25.5 7.5 %collective-permute-start = (bf16[512,256]{1,0:T(8,128)(2,1)S(1)}, bf16[512,256]{1,0:T(8,128)(2,1)S(1)}, u32[]{:S(2)}, u32[]{:S(2)}) collective-permute-start(bf16[512,256]{1,0:T(8,128)(2,1)S(1)} %bitcast.21), channel_id=1, source_target_pairs={{0,32},{32,0},{1,33},{33,1},{2,34},{34,2},{3,35},{35,3},{4,36},{36... | collective-permute-start | bytes 786440 | tf_op jit(solution)/shard_map/ppermute | solution.py:85
  33.0 5.0 %collective-permute-start.1 = (bf16[256,2688]{1,0:T(8,128)(2,1)S(1)}, bf16[256,2688]{1,0:T(8,128)(2,1)S(1)}, u32[]{:S(2)}, u32[]{:S(2)}) collective-permute-start(bf16[256,2688]{1,0:T(8,128)(2,1)S(1)} %crosses.2), channel_id=1, source_target_pairs={{0,32},{32,0},{1,33},{33,1},{2,34},{34,2},{3,35},{35,3},{4,36},{36... | collective-permute-start | bytes 4128776 | tf_op jit(solution)/shard_map/ppermute | solution.py:85
  109.5 9.6 %collective-permute-start.2 = (bf16[256,2560]{1,0:T(8,128)(2,1)S(1)}, bf16[256,2560]{1,0:T(8,128)(2,1)S(1)}, u32[]{:S(2)}, u32[]{:S(2)}) collective-permute-start(bf16[256,2560]{1,0:T(8,128)(2,1)S(1)} %bitcast.19), channel_id=1, source_target_pairs={{0,32},{32,0},{1,33},{33,1},{2,34},{34,2},{3,35},{35,3},{4,36},{36... | collective-permute-start | bytes 3932168 | tf_op jit(solution)/shard_map/ppermute | solution.py:85
